TPU v7x, 128 devices: a whole 4x4x4 slice. The times are simulated.
128 devices in a mesh: section: 2 (over core), fsdp: 2 (over x_lo), expert: 32 (over y, x_hi, z).
Axes of the slice: x: 4 (x_hi: 2, x_lo: 2; x = x_hi * 2 + x_lo), y: 4, z: 4, core: 2. Of those that a mesh axis runs over, the one named last changes fastest.
Arguments:
- inputs: bfloat16 [2, 6144, 1536], P(None, ('fsdp', 'expert')), may hold values from -6 to 6
- cotangent: bfloat16 [2, 6144, 1536], P(None, ('fsdp', 'expert')), may hold values from -6 to 6
- segments: int32 [2, 6144], P(None, ('fsdp', 'expert')), may hold values from 0 to 95, never falling along the last dimension, each value on 1 to 96 neighbouring positions
- expert_ids: int32 [2, 2, 6144, 4], P('section', None, ('fsdp', 'expert')), may hold values from 0 to 31, all different within a row; in each aligned block of 96 rows (0 to 95, 96 to 191, ..., all dimensions but the last counted through in order) at most 15 rows name the same one
- gate_logits: float32 [2, 2, 6144, 4], P('section', None, ('fsdp', 'expert')), may hold values from -3 to 3
- w_query: bfloat16 [2, 1536, 1536], P('section', 'fsdp'), may hold values from -0.15625 to 0.15625
- key_projection: bfloat16 [2, 1536, 256], P('section', 'fsdp'), may hold values from -0.15625 to 0.15625
- value_projection: bfloat16 [2, 1536, 256], P('section', 'fsdp'), may hold values from -0.15625 to 0.15625
- w_out: bfloat16 [2, 1536, 1536], P('section', 'fsdp'), may hold values from -0.875 to 0.875
- gain_attn: bfloat16 [2, 1536], P('section', 'fsdp'), may hold values from 0.5 to 1.5
- gain_moe: bfloat16 [2, 1536], P('section', 'fsdp'), may hold values from 0.5 to 1.5
- w_gate: bfloat16 [2, 32, 1536, 768], P('section', 'expert', 'fsdp'), may hold values from -0.15625 to 0.15625
- w_up: bfloat16 [2, 32, 1536, 768], P('section', 'expert', 'fsdp'), may hold values from -0.15625 to 0.15625
- w_down: bfloat16 [2, 32, 768, 1536], P('section', 'expert', 'fsdp'), may hold values from -0.625 to 0.625
Outputs:
- acts: bfloat16 [2, 2, 6144, 1536], P('section', None, ('fsdp', 'expert'))
- in_grads: bfloat16 [2, 2, 6144, 1536], P('section', None, ('fsdp', 'expert'))
- grad_query: float32 [2, 1536, 1536], P('section', 'fsdp')
- grad_key: float32 [2, 1536, 256], P('section', 'fsdp')
- grad_value: float32 [2, 1536, 256], P('section', 'fsdp')
- grad_out: float32 [2, 1536, 1536], P('section', 'fsdp')
- grad_gain_attn: float32 [2, 1536], P('section', 'fsdp')
- grad_gain_moe: float32 [2, 1536], P('section', 'fsdp')
- grad_gate: float32 [2, 32, 1536, 768], P('section', 'expert', 'fsdp')
- grad_up: float32 [2, 32, 1536, 768], P('section', 'expert', 'fsdp')
- grad_down: float32 [2, 32, 768, 1536], P('section', 'expert', 'fsdp')
Inputs may be any that keep to these rules, and one draw needn't show every extreme that they name: `segments`: segment ids never fall along a row; a document has 1 to 96 tokens, and one has exactly 96. `expert_ids`: each token names 4 different experts; among the 96 tokens of one device in one micro-batch and section no expert is named more than 15 times, a bound that some block reaches.
All inputs are finite; a program needn't handle non-finite values.
Results may differ from a plain program's by a relative error of at most 0.034.
Values may be sent and summed in bfloat16 or wider, within the bound.
A program may use at most 256 MiB of HBM per device.

v0:
```python
import jax
import jax.numpy as jnp
from jax import lax
from jax.sharding import PartitionSpec as P

HEAD_SIZE = 128


epsilon = 1e-06
rope_base = 1000000.0


def shifted(block, axis, distance):
    devices = range(lax.axis_size(axis))
    route = [(i - distance, i) for i in devices if i - distance in devices]
    return lax.ppermute(block, axis, route)


def rms_scale(operand, gain_row):
    inverse = lax.rsqrt(jnp.mean(operand * operand, axis=-1, keepdims=True) + epsilon)
    return operand * inverse * gain_row


def rotary_rotation(operand, rotary_angles):
    half_dim = operand.shape[-1] // 2
    cosine = jnp.cos(rotary_angles)[..., None, :]
    sine_part = jnp.sin(rotary_angles)[..., None, :]
    front_half = operand[..., :half_dim]
    second = operand[..., half_dim:]
    return jnp.concatenate(
        [front_half * cosine - second * sine_part, second * cosine + front_half * sine_part],
        axis=-1,
    )


def seq_layout(segment_row):
    sequence_length = segment_row.shape[0]
    same_doc = segment_row[:, None] == segment_row[None, :]
    row_index = lax.broadcasted_iota(jnp.int32, (sequence_length, sequence_length), 0)
    col_index = lax.broadcasted_iota(jnp.int32, (sequence_length, sequence_length), 1)
    places = jnp.sum((same_doc & (col_index < row_index)).astype(jnp.int32), axis=-1)
    frequency = rope_base ** (-(jnp.arange(HEAD_SIZE // 2, dtype=jnp.float32) * 2.0 / HEAD_SIZE))
    rotary_angles = places.astype(jnp.float32)[:, None] * frequency[None, :]
    return (rotary_angles, same_doc & (col_index <= row_index))


def score_block(query_rows, key_head_rows, allowed):
    raw_scores = jnp.einsum(
        "qhgd,khd->hgqk", query_rows, key_head_rows, preferred_element_type=jnp.float32
    )
    return jnp.where(allowed[None, None], raw_scores * HEAD_SIZE ** (-0.5), -1e30)


def slot_plan(chosen, experts_all):
    entry_expert = chosen.reshape(-1)
    one_hot = (entry_expert[:, None] == jnp.arange(experts_all, dtype=jnp.int32)[None, :]).astype(
        jnp.int32
    )
    entry_slot = jnp.sum((jnp.cumsum(one_hot, axis=0) - one_hot) * one_hot, axis=1)
    return (entry_expert, entry_slot)


def layer_forward(section_input, segment_row, chosen, logits, weights, capacity, experts_all):
    w_query, key_projection, value_projection, w_out, gain_attn, gain_moe, w_gate, w_up, w_down = (
        weights
    )
    sequence_length, width_model = section_input.shape
    top_count = chosen.shape[1]
    kv_heads = key_projection.shape[1] // HEAD_SIZE
    q_heads = w_query.shape[1] // HEAD_SIZE
    group_portion = q_heads // kv_heads
    rotary_angles, allowed = seq_layout(segment_row)
    start_rows = section_input.astype(jnp.float32)
    norm_one = rms_scale(start_rows, gain_attn.astype(jnp.float32)).astype(jnp.bfloat16)
    query_rows = jnp.dot(norm_one, w_query, preferred_element_type=jnp.float32).reshape(
        sequence_length, q_heads, HEAD_SIZE
    )
    query_rows = (
        rotary_rotation(query_rows, rotary_angles)
        .astype(jnp.bfloat16)
        .reshape(sequence_length, kv_heads, group_portion, HEAD_SIZE)
    )
    key_head_rows = jnp.dot(norm_one, key_projection, preferred_element_type=jnp.float32).reshape(
        sequence_length, kv_heads, HEAD_SIZE
    )
    key_head_rows = rotary_rotation(key_head_rows, rotary_angles).astype(jnp.bfloat16)
    value_head_rows = jnp.dot(
        norm_one, value_projection, preferred_element_type=jnp.float32
    ).astype(jnp.bfloat16)
    value_head_rows = value_head_rows.reshape(sequence_length, kv_heads, HEAD_SIZE)
    scores = score_block(query_rows, key_head_rows, allowed)
    top_score = jnp.max(scores, axis=-1, keepdims=True)
    exp_scores = jnp.exp(scores - top_score)
    exp_total = jnp.sum(exp_scores, axis=-1, keepdims=True)
    attn_probs = (exp_scores / exp_total).astype(jnp.bfloat16)
    log_total = top_score + jnp.log(exp_total)
    attn_mixed = jnp.einsum(
        "hgqk,khd->qhgd", attn_probs, value_head_rows, preferred_element_type=jnp.float32
    )
    attn_mixed = attn_mixed.reshape(sequence_length, q_heads * HEAD_SIZE).astype(jnp.bfloat16)
    hidden_one = start_rows + jnp.dot(attn_mixed, w_out, preferred_element_type=jnp.float32)
    norm_two = rms_scale(hidden_one, gain_moe.astype(jnp.float32)).astype(jnp.bfloat16)
    entry_expert, entry_slot = slot_plan(chosen, experts_all)
    copies = jnp.repeat(norm_two, top_count, axis=0)
    dispatch = (
        jnp.zeros((experts_all, capacity, width_model), jnp.bfloat16)
        .at[entry_expert, entry_slot]
        .set(copies)
    )
    expert_local = w_gate.shape[0]
    owners = experts_all // expert_local
    received = lax.all_to_all(dispatch, "expert", split_axis=0, concat_axis=0, tiled=True)
    items = received.shape[1]
    slot_rows = received.reshape(owners, expert_local, items, width_model)
    gate_pre = jnp.einsum("sxcd,xdh->sxch", slot_rows, w_gate, preferred_element_type=jnp.float32)
    up_pre = jnp.einsum("sxcd,xdh->sxch", slot_rows, w_up, preferred_element_type=jnp.float32)
    hidden = (jax.nn.gelu(gate_pre) * up_pre).astype(jnp.bfloat16)
    result_rows = jnp.einsum("sxch,xhd->sxcd", hidden, w_down, preferred_element_type=jnp.float32)
    result_rows = result_rows.astype(jnp.bfloat16).reshape(experts_all, items, width_model)
    returned_rows = lax.all_to_all(result_rows, "expert", split_axis=0, concat_axis=0, tiled=True)
    returned_rows, received = (returned_rows, received)
    picked = returned_rows[entry_expert, entry_slot].reshape(
        sequence_length, top_count, width_model
    )
    gate_weights = jax.nn.softmax(logits, axis=-1)
    result = (
        hidden_one + jnp.sum(gate_weights[:, :, None] * picked.astype(jnp.float32), axis=1)
    ).astype(jnp.bfloat16)
    kept_values = (
        section_input,
        segment_row,
        norm_one,
        query_rows,
        key_head_rows,
        value_head_rows,
        log_total,
        attn_mixed,
        hidden_one,
        norm_two,
        entry_expert,
        entry_slot,
        gate_weights,
        received,
    )
    return (result, kept_values)


def layer_backward(incoming, kept_values, weights):
    w_query, key_projection, value_projection, w_out, gain_attn, gain_moe, w_gate, w_up, w_down = (
        weights
    )
    (
        section_input,
        segment_row,
        norm_one,
        query_rows,
        key_head_rows,
        value_head_rows,
        log_total,
        attn_mixed,
        hidden_one,
        norm_two,
        entry_expert,
        entry_slot,
        gate_weights,
        received,
    ) = kept_values
    sequence_length, width_model = section_input.shape
    top_count = gate_weights.shape[1]
    experts_all, capacity = (received.shape[0], received.shape[1])
    expert_local = w_gate.shape[0]
    owners = experts_all // expert_local
    kv_heads = key_head_rows.shape[1]
    group_portion = query_rows.shape[2]
    q_heads = kv_heads * group_portion
    d_pick = (
        (gate_weights[:, :, None] * incoming[:, None, :])
        .reshape(sequence_length * top_count, width_model)
        .astype(jnp.bfloat16)
    )
    d_dispatch = (
        jnp.zeros((experts_all, capacity, width_model), jnp.bfloat16)
        .at[entry_expert, entry_slot]
        .set(d_pick)
    )
    d_received = lax.all_to_all(d_dispatch, "expert", split_axis=0, concat_axis=0, tiled=True)
    slot_rows = received.reshape(owners, expert_local, capacity, width_model)
    d_rows = d_received.reshape(owners, expert_local, capacity, width_model)
    gate_pre = jnp.einsum("sxcd,xdh->sxch", slot_rows, w_gate, preferred_element_type=jnp.float32)
    up_pre = jnp.einsum("sxcd,xdh->sxch", slot_rows, w_up, preferred_element_type=jnp.float32)
    d_hidden = jnp.einsum("sxcd,xhd->sxch", d_rows, w_down, preferred_element_type=jnp.float32)
    activation, gelu_back = jax.vjp(jax.nn.gelu, gate_pre)
    hidden = (activation * up_pre).astype(jnp.bfloat16)
    grad_down = jnp.einsum("sxch,sxcd->xhd", hidden, d_rows, preferred_element_type=jnp.float32)
    d_gate = gelu_back(d_hidden * up_pre)[0].astype(jnp.bfloat16)
    d_up = (d_hidden * activation).astype(jnp.bfloat16)
    grad_gate = jnp.einsum("sxcd,sxch->xdh", slot_rows, d_gate, preferred_element_type=jnp.float32)
    grad_up = jnp.einsum("sxcd,sxch->xdh", slot_rows, d_up, preferred_element_type=jnp.float32)
    d_inner = jnp.einsum("sxch,xdh->sxcd", d_gate, w_gate, preferred_element_type=jnp.float32)
    d_inner = d_inner + jnp.einsum("sxch,xdh->sxcd", d_up, w_up, preferred_element_type=jnp.float32)
    d_inner = d_inner.astype(jnp.bfloat16).reshape(experts_all, capacity, width_model)
    d_back = lax.all_to_all(d_inner, "expert", split_axis=0, concat_axis=0, tiled=True)
    d_norm_two = jnp.sum(
        d_back[entry_expert, entry_slot]
        .reshape(sequence_length, top_count, width_model)
        .astype(jnp.float32),
        axis=1,
    )
    norm_out, norm_back = jax.vjp(rms_scale, hidden_one, gain_moe.astype(jnp.float32))
    d_from_norm, grad_gain_moe = norm_back(d_norm_two)
    d_hidden_one = incoming + d_from_norm
    d_attn = d_hidden_one.astype(jnp.bfloat16)
    grad_out = jnp.einsum("sa,sd->ad", attn_mixed, d_attn, preferred_element_type=jnp.float32)
    d_mixed = jnp.einsum("sd,ad->sa", d_attn, w_out, preferred_element_type=jnp.float32).astype(
        jnp.bfloat16
    )
    d_mixed = d_mixed.reshape(sequence_length, kv_heads, group_portion, HEAD_SIZE)
    rotary_angles, allowed = seq_layout(segment_row)
    scores = score_block(query_rows, key_head_rows, allowed)
    attn_probs = jnp.exp(scores - log_total)
    d_probs = jnp.einsum(
        "qhgd,khd->hgqk", d_mixed, value_head_rows, preferred_element_type=jnp.float32
    )
    d_values = jnp.einsum(
        "hgqk,qhgd->khd",
        attn_probs.astype(jnp.bfloat16),
        d_mixed,
        preferred_element_type=jnp.float32,
    )
    d_scores = (
        attn_probs
        * (d_probs - jnp.sum(d_probs * attn_probs, axis=-1, keepdims=True))
        * HEAD_SIZE ** (-0.5)
    )
    d_scores = d_scores.astype(jnp.bfloat16)
    d_queries = jnp.einsum(
        "hgqk,khd->qhgd", d_scores, key_head_rows, preferred_element_type=jnp.float32
    )
    d_keys = jnp.einsum("hgqk,qhgd->khd", d_scores, query_rows, preferred_element_type=jnp.float32)
    d_queries = (
        rotary_rotation(d_queries.reshape(sequence_length, q_heads, HEAD_SIZE), -rotary_angles)
        .reshape(sequence_length, q_heads * HEAD_SIZE)
        .astype(jnp.bfloat16)
    )
    d_keys = (
        rotary_rotation(d_keys, -rotary_angles)
        .reshape(sequence_length, kv_heads * HEAD_SIZE)
        .astype(jnp.bfloat16)
    )
    d_values = d_values.reshape(sequence_length, kv_heads * HEAD_SIZE).astype(jnp.bfloat16)
    grad_query = jnp.einsum("sd,se->de", norm_one, d_queries, preferred_element_type=jnp.float32)
    grad_key = jnp.einsum("sd,se->de", norm_one, d_keys, preferred_element_type=jnp.float32)
    grad_value = jnp.einsum("sd,se->de", norm_one, d_values, preferred_element_type=jnp.float32)
    d_norm_one = jnp.einsum("se,de->sd", d_queries, w_query, preferred_element_type=jnp.float32)
    d_norm_one = d_norm_one + jnp.einsum(
        "se,de->sd", d_keys, key_projection, preferred_element_type=jnp.float32
    )
    d_norm_one = d_norm_one + jnp.einsum(
        "se,de->sd", d_values, value_projection, preferred_element_type=jnp.float32
    )
    first_norm, norm_back_one = jax.vjp(
        rms_scale, section_input.astype(jnp.float32), gain_attn.astype(jnp.float32)
    )
    d_start, grad_gain_attn = norm_back_one(d_norm_one)
    d_section_input = d_hidden_one + d_start
    grads = (
        grad_query,
        grad_key,
        grad_value,
        grad_out,
        grad_gain_attn,
        grad_gain_moe,
        grad_gate,
        grad_up,
        grad_down,
    )
    return (d_section_input, grads)


def shard_grads(
    grad_query,
    grad_key,
    grad_value,
    grad_out,
    grad_gain_attn,
    grad_gain_moe,
    grad_gate,
    grad_up,
    grad_down,
):
    return (
        lax.psum_scatter(
            grad_query.astype(jnp.bfloat16), "fsdp", scatter_dimension=0, tiled=True
        ).astype(jnp.float32),
        lax.psum_scatter(
            grad_key.astype(jnp.bfloat16), "fsdp", scatter_dimension=0, tiled=True
        ).astype(jnp.float32),
        lax.psum_scatter(
            grad_value.astype(jnp.bfloat16), "fsdp", scatter_dimension=0, tiled=True
        ).astype(jnp.float32),
        lax.psum_scatter(
            grad_out.astype(jnp.bfloat16), "fsdp", scatter_dimension=0, tiled=True
        ).astype(jnp.float32),
        lax.psum_scatter(
            grad_gain_attn.astype(jnp.bfloat16), "fsdp", scatter_dimension=0, tiled=True
        ).astype(jnp.float32),
        lax.psum_scatter(
            grad_gain_moe.astype(jnp.bfloat16), "fsdp", scatter_dimension=0, tiled=True
        ).astype(jnp.float32),
        lax.psum_scatter(
            grad_gate.astype(jnp.bfloat16), "fsdp", scatter_dimension=1, tiled=True
        ).astype(jnp.float32),
        lax.psum_scatter(
            grad_up.astype(jnp.bfloat16), "fsdp", scatter_dimension=1, tiled=True
        ).astype(jnp.float32),
        lax.psum_scatter(
            grad_down.astype(jnp.bfloat16), "fsdp", scatter_dimension=1, tiled=True
        ).astype(jnp.float32),
    )


def local(
    inputs,
    cotangent,
    segments,
    expert_ids,
    gate_logits,
    w_query,
    key_projection,
    value_projection,
    w_out,
    gain_attn,
    gain_moe,
    w_gate,
    w_up,
    w_down,
):
    is_first = lax.axis_index("section") == 0
    weights = (
        lax.all_gather(w_query[0], "fsdp", axis=0, tiled=True),
        lax.all_gather(key_projection[0], "fsdp", axis=0, tiled=True),
        lax.all_gather(value_projection[0], "fsdp", axis=0, tiled=True),
        lax.all_gather(w_out[0], "fsdp", axis=0, tiled=True),
        lax.all_gather(gain_attn[0], "fsdp", axis=0, tiled=True),
        lax.all_gather(gain_moe[0], "fsdp", axis=0, tiled=True),
        lax.all_gather(w_gate[0], "fsdp", axis=1, tiled=True),
        lax.all_gather(w_up[0], "fsdp", axis=1, tiled=True),
        lax.all_gather(w_down[0], "fsdp", axis=1, tiled=True),
    )
    micro_count = inputs.shape[0]
    sequence_length = inputs.shape[1]
    width_model = inputs.shape[2]
    top_count = expert_ids.shape[-1]
    experts_all = lax.axis_size("expert") * w_gate.shape[1]
    capacity = 5 * sequence_length * top_count // (4 * experts_all)
    received_rows = jnp.zeros((sequence_length, width_model), jnp.bfloat16)
    stashed = []
    outputs = []
    for moment in range(micro_count + 1):
        early_index = min(moment, micro_count - 1)
        late_index = max(moment - 1, 0)
        section_input = jnp.where(is_first, inputs[early_index], received_rows)
        segment_row = jnp.where(is_first, segments[early_index], segments[late_index])
        chosen = jnp.where(is_first, expert_ids[0, early_index], expert_ids[0, late_index])
        logits = jnp.where(is_first, gate_logits[0, early_index], gate_logits[0, late_index])
        result, kept_values = layer_forward(
            section_input, segment_row, chosen, logits, weights, capacity, experts_all
        )
        stashed.append(kept_values)
        outputs.append(result)
        if moment < micro_count:
            received_rows = shifted(result, "section", 1)
    acts = jnp.where(is_first, jnp.stack(outputs[:micro_count]), jnp.stack(outputs[1:]))[None]
    totals = tuple((jnp.zeros(weight.shape, jnp.float32) for weight in weights))
    returned_grad = jnp.zeros((sequence_length, width_model), jnp.bfloat16)
    grad_list = []
    for moment in range(micro_count + 1):
        early_index = min(moment, micro_count - 1)
        incoming = jnp.where(
            is_first, returned_grad.astype(jnp.float32), cotangent[early_index].astype(jnp.float32)
        )
        kept_values = jax.tree.map(
            lambda early_pick, late_pick: jnp.where(is_first, early_pick, late_pick),
            stashed[max(moment - 1, 0)],
            stashed[min(moment + 1, micro_count)],
        )
        d_section_input, grads = layer_backward(incoming, kept_values, weights)
        valid_step = jnp.where(is_first, moment >= 1, moment < micro_count)
        totals = tuple(
            (
                jnp.where(valid_step, total_sum + grad_part, total_sum)
                for total_sum, grad_part in zip(totals, grads)
            )
        )
        d_rounded = d_section_input.astype(jnp.bfloat16)
        grad_list.append(d_rounded)
        if moment < micro_count:
            returned_grad = shifted(d_rounded, "section", -1)
    in_grads = jnp.where(is_first, jnp.stack(grad_list[1:]), jnp.stack(grad_list[:micro_count]))[
        None
    ]
    (
        grad_query,
        grad_key,
        grad_value,
        grad_out,
        grad_gain_attn,
        grad_gain_moe,
        grad_gate,
        grad_up,
        grad_down,
    ) = totals
    grad_query, grad_key, grad_value, grad_out, grad_gain_attn, grad_gain_moe = (
        lax.psum(grad_query.astype(jnp.bfloat16), "expert").astype(jnp.float32),
        lax.psum(grad_key.astype(jnp.bfloat16), "expert").astype(jnp.float32),
        lax.psum(grad_value.astype(jnp.bfloat16), "expert").astype(jnp.float32),
        lax.psum(grad_out.astype(jnp.bfloat16), "expert").astype(jnp.float32),
        lax.psum(grad_gain_attn.astype(jnp.bfloat16), "expert").astype(jnp.float32),
        lax.psum(grad_gain_moe.astype(jnp.bfloat16), "expert").astype(jnp.float32),
    )
    shards = tuple(
        shard_grads(
            grad_query,
            grad_key,
            grad_value,
            grad_out,
            grad_gain_attn,
            grad_gain_moe,
            grad_gate,
            grad_up,
            grad_down,
        )
    )
    return (
        acts,
        in_grads,
        shards[0][None],
        shards[1][None],
        shards[2][None],
        shards[3][None],
        shards[4][None],
        shards[5][None],
        shards[6][None],
        shards[7][None],
        shards[8][None],
    )


def solution(mesh):
    return jax.shard_map(
        local,
        mesh=mesh,
        in_specs=(
            P(None, ("fsdp", "expert"), None),
            P(None, ("fsdp", "expert"), None),
            P(None, ("fsdp", "expert")),
            P("section", None, ("fsdp", "expert"), None),
            P("section", None, ("fsdp", "expert"), None),
            P("section", "fsdp", None),
            P("section", "fsdp", None),
            P("section", "fsdp", None),
            P("section", "fsdp", None),
            P("section", "fsdp"),
            P("section", "fsdp"),
            P("section", "expert", "fsdp", None),
            P("section", "expert", "fsdp", None),
            P("section", "expert", "fsdp", None),
        ),
        out_specs=(
            P("section", None, ("fsdp", "expert"), None),
            P("section", None, ("fsdp", "expert"), None),
            P("section", "fsdp", None),
            P("section", "fsdp", None),
            P("section", "fsdp", None),
            P("section", "fsdp", None),
            P("section", "fsdp"),
            P("section", "fsdp"),
            P("section", "expert", "fsdp", None),
            P("section", "expert", "fsdp", None),
            P("section", "expert", "fsdp", None),
        ),
        check_vma=False,
    )
```

profile of v0, /device:TPU:0, one launch (start us, length us, event | category | flops | bytes accessed | tf_op | source)
XLA Modules:
  0.0 1809.6 jit_solution(15485379787369400175)
XLA Ops:
  16.8 13.7 all-gather.2
  30.8 19.1 %all-gather.1 = bf16[1,1536,256]{2,1,0:T(8,128)(2,1)S(1)} all-gather(bf16[1,768,256]{2,1,0:T(8,128)(2,1)S(1)} %copy-done.127), channel_id=3, replica_groups=mesh['section'=2,'fsdp'=2,'expert'=32] {'fsdp'}, dimensions={1}, use_global_device_ids=true | all-gather | bytes 1179648 | tf_op jit(solution)/shard_map/all_gather | solution.py:342
  62.0 24.2 %all-gather.15.cloned.1.call-done = bf16[1,1536,1536]{2,1,0:T(8,128)(2,1)} async-done(((bf16[1,768,1536]{2,1,0:T(8,128)(2,1)}), bf16[1,1536,1536]{2,1,0:T(8,128)(2,1)}) %all-gather.15.cloned.1.call-update) | async-done | bytes 4718608 | tf_op jit(solution)/shard_map/all_gather | solution.py:340
  86.3 6.6 copy.118
  98.7 57.0 %all-gather.17.cloned.1.call-done = bf16[1,1536,1536]{2,1,0:T(8,128)(2,1)} async-done(((bf16[1,768,1536]{2,1,0:T(8,128)(2,1)}), bf16[1,1536,1536]{2,1,0:T(8,128)(2,1)}) %all-gather.17.cloned.1.call-update) | async-done | bytes 4718608 | tf_op jit(solution)/shard_map/all_gather | solution.py:343
  161.7 46.7 %scatter_fusion = bf16[32,15,1536]{2,0,1:T(8,128)(2,1)S(1)} fusion(bf16[32,15,1536]{2,0,1:T(8,128)(2,1)S(1)} %broadcast.1175.clone, s32[384]{0:T(512)S(1)} %get-tuple-element.33, bf16[384,1536]{1,0:T(8,128)(2,1)} %reshape.1951), kind=kCustom, calls=%fused_computation.6 | custom fusion | bytes 3542016 | tf_op jit(solution)/shard_map/scatter | solution.py:108
  210.3 9.7 all-to-all-start
  220.1 39.4 %all-to-all-done = bf16[32,15,1536]{2,1,0:T(8,128)(2,1)} async-done(((bf16[32,15,1536]{2,1,0:T(8,128)(2,1)}), bf16[32,15,1536]{2,1,0:T(8,128)(2,1)}, u32[]{:S(2)}, u32[]{:S(2)}) %all-to-all-start) | async-done | bytes 1474592 | tf_op jit(solution)/shard_map/all_to_all | solution.py:112
  264.7 30.7 %all-gather.23.cloned.1.call-done = bf16[1,1,768,1536]{3,2,1,0:T(8,128)(2,1)} async-done(((bf16[1,1,384,1536]{3,2,1,0:T(8,128)(2,1)}), bf16[1,1,768,1536]{3,2,1,0:T(8,128)(2,1)}) %all-gather.23.cloned.1.call-update) | async-done | bytes 2359312 | tf_op jit(solution)/shard_map/all_gather | solution.py:348
  295.3 6.7 convolution_convert_fusion.2
  304.0 10.2 all-to-all-start.1
  315.5 22.1 %all-to-all-done.1 = bf16[32,15,1536]{2,1,0:T(8,128)(2,1)} async-done(((bf16[32,15,1536]{2,1,0:T(8,128)(2,1)}), bf16[32,15,1536]{2,1,0:T(8,128)(2,1)}, u32[]{:S(2)}, u32[]{:S(2)}) %all-to-all-start.1) | async-done | bytes 1474592 | tf_op jit(solution)/shard_map/all_to_all | solution.py:120
  339.9 8.3 gather_fusion
  373.9 46.6 %scatter_fusion.1 = bf16[32,15,1536]{2,0,1:T(8,128)(2,1)S(1)} fusion(bf16[32,15,1536]{2,0,1:T(8,128)(2,1)S(1)} %broadcast.1175.clone.1, s32[384]{0:T(512)S(1)} %get-tuple-element.35, bf16[384,1536]{1,0:T(8,128)(2,1)} %reshape.1957), kind=kCustom, calls=%fused_computation.7 | custom fusion | bytes 3542016 | tf_op jit(solution)/shard_map/scatter | solution.py:108
  421.4 30.1 %all_to_all.60 = bf16[32,15,1536]{2,1,0:T(8,128)(2,1)S(1)} all-to-all(bf16[32,15,1536]{2,1,0:T(8,128)(2,1)S(1)} %copy.144), channel_id=1, replica_groups=mesh['section'=2,'fsdp'=2,'expert'=32] {'expert'}, dimensions={0} | all-to-all | bytes 2949120 | tf_op jit(solution)/shard_map/all_to_all | solution.py:112
  455.7 6.7 convolution_convert_fusion.1
  469.5 22.3 %all-to-all-done.3 = bf16[32,15,1536]{2,1,0:T(8,128)(2,1)} async-done(((bf16[32,15,1536]{2,1,0:T(8,128)(2,1)}), bf16[32,15,1536]{2,1,0:T(8,128)(2,1)}, u32[]{:S(2)}, u32[]{:S(2)}) %all-to-all-start.3) | async-done | bytes 1474592 | tf_op jit(solution)/shard_map/all_to_all | solution.py:120
  494.1 8.3 gather_fusion.1
  532.9 46.6 %scatter_fusion.2 = bf16[32,15,1536]{2,0,1:T(8,128)(2,1)S(1)} fusion(bf16[32,15,1536]{2,0,1:T(8,128)(2,1)S(1)} %broadcast.1175.clone.2, s32[384]{0:T(512)S(1)} %get-tuple-element.34, bf16[384,1536]{1,0:T(8,128)(2,1)} %reshape.1963), kind=kCustom, calls=%fused_computation.8 | custom fusion | bytes 3542016 | tf_op jit(solution)/shard_map/scatter | solution.py:108
  596.0 46.7 %scatter_fusion.3 = bf16[32,15,1536]{2,0,1:T(8,128)(2,1)S(1)} fusion(bf16[32,15,1536]{2,0,1:T(8,128)(2,1)S(1)} %broadcast.1175.clone.3, s32[384]{0:T(512)S(1)} %get-tuple-element.38, bf16[384,1536]{1,0:T(8,128)(2,1)} %multiply_convert_fusion.2), kind=kCustom, calls=%fused_computation.9 | custom fusion | bytes 3542016 | tf_op jit(solution)/shard_map/scatter | solution.py:184
  644.7 10.1 all-to-all-start.6
  665.3 10.0 all-to-all-done.6
  675.3 5.9 fusion.310
  697.1 7.8 convolution_convert_fusion
  714.5 5.4 all-to-all-start.5
  727.9 8.3 gather_fusion.3
  744.8 8.3 gather_fusion.2
  801.5 46.7 %scatter_fusion.4 = bf16[32,15,1536]{2,0,1:T(8,128)(2,1)S(1)} fusion(bf16[32,15,1536]{2,0,1:T(8,128)(2,1)S(1)} %broadcast.1175.clone.4, s32[384]{0:T(512)S(1)} %get-tuple-element.24, bf16[384,1536]{1,0:T(8,128)(2,1)} %multiply_convert_fusion.1), kind=kCustom, calls=%fused_computation.10 | custom fusion | bytes 3542016 | tf_op jit(solution)/shard_map/scatter | solution.py:184
  850.1 6.9 all-to-all-start.8
  857.1 5.4 fusion.73
  865.6 15.2 all-to-all-done.8
  880.8 5.9 fusion.311
  892.4 6.2 all-to-all-start.9
  900.0 21.4 %all-to-all-done.9 = bf16[32,15,1536]{2,1,0:T(8,128)(2,1)} async-done(((bf16[32,15,1536]{2,1,0:T(8,128)(2,1)}), bf16[32,15,1536]{2,1,0:T(8,128)(2,1)}, u32[]{:S(2)}, u32[]{:S(2)}) %all-to-all-start.9) | async-done | bytes 1474592 | tf_op jit(solution)/shard_map/all_to_all | solution.py:202
  923.7 8.3 gather_fusion.4
  974.7 46.6 %scatter_fusion.5 = bf16[32,15,1536]{2,0,1:T(8,128)(2,1)S(1)} fusion(bf16[32,15,1536]{2,0,1:T(8,128)(2,1)S(1)} %broadcast.1175, s32[384]{0:T(512)S(1)} %copy-done.3, bf16[384,1536]{1,0:T(8,128)(2,1)} %multiply_convert_fusion), kind=kCustom, calls=%fused_computation.11 | custom fusion | bytes 3542016 | tf_op jit(solution)/shard_map/scatter | solution.py:184
  1023.3 5.5 all-to-all-start.10
  1037.3 15.3 all-to-all-done.10
  1052.6 5.9 fusion.312
  1064.1 6.2 all-to-all-start.11
  1073.8 19.3 %all-to-all-done.11 = bf16[32,15,1536]{2,1,0:T(8,128)(2,1)} async-done(((bf16[32,15,1536]{2,1,0:T(8,128)(2,1)}), bf16[32,15,1536]{2,1,0:T(8,128)(2,1)}, u32[]{:S(2)}, u32[]{:S(2)}) %all-to-all-start.11) | async-done | bytes 1474592 | tf_op jit(solution)/shard_map/all_to_all | solution.py:202
  1095.4 8.5 gather_fusion.5
  1146.6 7.7 fusion.3
  1184.2 6.0 fusion.30
  1190.3 37.1 %reduce-scatter.20.cloned.1.call-done = bf16[768,1536]{1,0:T(8,128)(2,1)} async-done(((bf16[1536,1536]{1,0:T(8,128)(2,1)}), bf16[768,1536]{1,0:T(8,128)(2,1)}) %reduce-scatter.20.cloned.1.call-update) | async-done | bytes 2359312 | tf_op jit(solution)/shard_map/reduce_scatter | solution.py:301
  1227.4 66.7 %reduce-scatter.14.cloned.1.call-done = bf16[768,1536]{1,0:T(8,128)(2,1)} async-done(((bf16[1536,1536]{1,0:T(8,128)(2,1)}), bf16[768,1536]{1,0:T(8,128)(2,1)}) %reduce-scatter.14.cloned.1.call-update) | async-done | bytes 2359312 | tf_op jit(solution)/shard_map/reduce_scatter | solution.py:292
  1307.3 96.8 %all-reduce.2 = (bf16[768]{0:T(1024)(128)(2,1)S(1)}, bf16[768]{0:T(1024)(128)(2,1)S(1)}) all-reduce(bf16[768]{0:T(1024)(128)(2,1)S(1)} %dynamic-slice.1, bf16[768]{0:T(1024)(128)(2,1)S(1)} %dynamic-slice.3), channel_id=1, replica_groups=mesh['section'=2,'fsdp'=2,'expert'=32] {'expert'}, use_global_device_ids=true, to_apply=%region_71.72 | all-reduce | flops 1536 | bytes 6144 | tf_op jit(solution)/shard_map/psum | solution.py:418
  1420.3 373.1 %all-reduce.7.cloned.1.call-done = (bf16[768,1536]{1,0:T(8,128)(2,1)}, bf16[768,256]{1,0:T(8,128)(2,1)}, bf16[768,256]{1,0:T(8,128)(2,1)}, bf16[768,1536]{1,0:T(8,128)(2,1)}) async-done(((bf16[768,1536]{1,0:T(8,128)(2,1)}, bf16[768,256]{1,0:T(8,128)(2,1)}, bf16[768,256]{1,0:T(8,128)(2,1)}, bf16[768,1536]{1,0:T(8,128)(2,1)}), (bf16[768,1536]{1,0:T(8,128)(2,1)}, bf16[768,256]{1,0:T(8,128)(2,1)}, ...) | async-done | bytes 5505040 | tf_op jit(solution)/shard_map/psum | solution.py:414
  (802 shorter events, 422.9 us)
Async XLA Ops:
  7.2 79.1 %all-gather.15.cloned.1.call-start = ((), (), s32[]{:S(2)}) async-start(), calls=%async_computation.22 | async-start | bytes 7077888 | tf_op jit(solution)/shard_map/all_gather | solution.py:340
  7.9 147.8 %all-gather.17.cloned.1.call-start = ((), (), s32[]{:S(2)}) async-start(), calls=%async_computation.23 | async-start | bytes 7077888 | tf_op jit(solution)/shard_map/all_gather | solution.py:343
  8.7 211.4 %all-gather.21.cloned.1.call-start = ((), (), s32[]{:S(2)}) async-start(), calls=%async_computation.25 | async-start | bytes 3538944 | tf_op jit(solution)/shard_map/all_gather | solution.py:347
  9.4 255.2 %all-gather.19.cloned.1.call-start = ((), (), s32[]{:S(2)}) async-start(), calls=%async_computation.24 | async-start | bytes 3538944 | tf_op jit(solution)/shard_map/all_gather | solution.py:346
  10.0 285.3 %all-gather.23.cloned.1.call-start = ((), (), s32[]{:S(2)}) async-start(), calls=%async_computation.26 | async-start | bytes 3538944 | tf_op jit(solution)/shard_map/all_gather | solution.py:348
  10.6 20.1 %copy-start.168 = (s32[96]{0:T(128)}, s32[96]{0:T(128)S(1)}, u32[]{:S(2)}) copy-start(s32[96]{0:T(128)S(1)} %get-tuple-element.140) | copy-start | bytes 1156
  10.7 20.1 %copy-start.170 = (s32[96]{0:T(128)}, s32[96]{0:T(128)S(1)}, u32[]{:S(2)}) copy-start(s32[96]{0:T(128)S(1)} %get-tuple-element.137) | copy-start | bytes 1156
  10.7 20.1 %copy-start.172 = (s32[96]{0:T(128)}, s32[96]{0:T(128)S(1)}, u32[]{:S(2)}) copy-start(s32[96]{0:T(128)S(1)} %get-tuple-element.141) | copy-start | bytes 1156
  12.4 80.5 %copy-start.142 = (f32[96]{0:T(128)}, f32[96]{0:T(128)S(1)}, u32[]{:S(2)}) copy-start(f32[96]{0:T(128)S(1)} %add_rsqrt_fusion.5) | copy-start | bytes 1156
  16.7 504.0 %copy-start.41 = (f32[1536]{0:T(1024)}, f32[1536]{0:T(1024)S(1)}, u32[]{:S(2)}) copy-start(f32[1536]{0:T(1024)S(1)} %convert_reduce_fusion.7) | copy-start | bytes 18436
  30.5 926.1 %copy-start = (bf16[1,1536,256]{2,1,0:T(8,128)(2,1)}, bf16[1,1536,256]{2,1,0:T(8,128)(2,1)S(1)}, u32[]{:S(2)}) copy-start(bf16[1,1536,256]{2,1,0:T(8,128)(2,1)S(1)} %all-gather.2) | copy-start | bytes 2359300
  51.2 41.7 %copy-start.98 = (bf16[96,256]{1,0:T(8,128)(2,1)}, bf16[96,256]{1,0:T(8,128)(2,1)S(1)}, u32[]{:S(2)}) copy-start(bf16[96,256]{1,0:T(8,128)(2,1)S(1)} %convolution_convert_fusion.8) | copy-start | bytes 147460
  55.8 474.6 %copy-start.81 = (f32[1536]{0:T(1024)}, f32[1536]{0:T(1024)S(1)}, u32[]{:S(2)}) copy-start(f32[1536]{0:T(1024)S(1)} %convert_reduce_fusion.6) | copy-start | bytes 18436
  61.2 36.0 %copy-start.85 = (bf16[96,2,128]{2,0,1:T(8,128)(2,1)}, bf16[96,2,128]{2,0,1:T(8,128)(2,1)S(1)}, u32[]{:S(2)}) copy-start(bf16[96,2,128]{2,0,1:T(8,128)(2,1)S(1)} %pad_maximum_fusion.6) | copy-start | bytes 147460
  98.7 60.4 %copy-start.25 = (bf16[96,1536]{1,0:T(8,128)(2,1)}, bf16[96,1536]{1,0:T(8,128)(2,1)S(1)}, u32[]{:S(2)}) copy-start(bf16[96,1536]{1,0:T(8,128)(2,1)S(1)} %convert_element_type.511) | copy-start | bytes 884740
  210.3 49.2 %all-to-all-start = ((bf16[32,15,1536]{2,1,0:T(8,128)(2,1)}), bf16[32,15,1536]{2,1,0:T(8,128)(2,1)}, u32[]{:S(2)}, u32[]{:S(2)}) async-start(bf16[32,15,1536]{2,1,0:T(8,128)(2,1)} %copy.127), calls=%async_computation | async-start | bytes 3145728 | tf_op jit(solution)/shard_map/all_to_all | solution.py:112
  304.0 33.6 %all-to-all-start.1 = ((bf16[32,15,1536]{2,1,0:T(8,128)(2,1)}), bf16[32,15,1536]{2,1,0:T(8,128)(2,1)}, u32[]{:S(2)}, u32[]{:S(2)}) async-start(bf16[32,15,1536]{2,1,0:T(8,128)(2,1)} %copy.130), calls=%async_computation.1 | async-start | bytes 3145728 | tf_op jit(solution)/shard_map/all_to_all | solution.py:120
  314.8 25.1 %copy-start.164 = (f32[96]{0:T(128)}, f32[96]{0:T(128)S(1)}, u32[]{:S(2)}) copy-start(f32[96]{0:T(128)S(1)} %get-tuple-element.29) | copy-start | bytes 1156
  314.8 25.1 %copy-start.166 = (f32[96]{0:T(128)}, f32[96]{0:T(128)S(1)}, u32[]{:S(2)}) copy-start(f32[96]{0:T(128)S(1)} %get-tuple-element.30) | copy-start | bytes 1156
  355.0 2.6 collective-permute-start
  421.4 31.3 %copy-start.193 = (bf16[1,1,1536,768]{3,2,1,0:T(8,128)(2,1)S(1)}, bf16[1,1,1536,768]{3,2,1,0:T(8,128)(2,1)}, u32[]{:S(2)}) copy-start(bf16[1,1,1536,768]{3,2,1,0:T(8,128)(2,1)} %all-gather.21.cloned.1.call-done) | copy-start | bytes 7077892
  464.4 27.4 %all-to-all-start.3 = ((bf16[32,15,1536]{2,1,0:T(8,128)(2,1)}), bf16[32,15,1536]{2,1,0:T(8,128)(2,1)}, u32[]{:S(2)}, u32[]{:S(2)}) async-start(bf16[32,15,1536]{2,1,0:T(8,128)(2,1)} %copy.147), calls=%async_computation.3 | async-start | bytes 3145728 | tf_op jit(solution)/shard_map/all_to_all | solution.py:120
  469.4 24.7 %copy-start.162 = (f32[96]{0:T(128)}, f32[96]{0:T(128)S(1)}, u32[]{:S(2)}) copy-start(f32[96]{0:T(128)S(1)} %fusion.495) | copy-start | bytes 1156
  509.2 6.3 collective-permute-start.1
  581.5 63.1 %all-to-all-start.4 = ((bf16[32,15,1536]{2,1,0:T(8,128)(2,1)}), bf16[32,15,1536]{2,1,0:T(8,128)(2,1)}, u32[]{:S(2)}, u32[]{:S(2)}) async-start(bf16[32,15,1536]{2,1,0:T(8,128)(2,1)} %copy.158), calls=%async_computation.4 | async-start | bytes 3145728 | tf_op jit(solution)/shard_map/all_to_all | solution.py:112
  644.7 30.6 %all-to-all-start.6 = ((bf16[32,15,1536]{2,1,0:T(8,128)(2,1)}), bf16[32,15,1536]{2,1,0:T(8,128)(2,1)}, u32[]{:S(2)}, u32[]{:S(2)}) async-start(bf16[32,15,1536]{2,1,0:T(8,128)(2,1)} %copy.169), calls=%async_computation.6 | async-start | bytes 3145728 | tf_op jit(solution)/shard_map/all_to_all | solution.py:186
  686.8 26.6 %all-to-all-start.7 = ((bf16[32,15,1536]{2,1,0:T(8,128)(2,1)}), bf16[32,15,1536]{2,1,0:T(8,128)(2,1)S(1)}, u32[]{:S(2)}, u32[]{:S(2)}) async-start(bf16[32,15,1536]{2,1,0:T(8,128)(2,1)} %copy.173), calls=%async_computation.7 | async-start | bytes 3145728 | tf_op jit(solution)/shard_map/all_to_all | solution.py:202
  714.5 27.9 %all-to-all-start.5 = ((bf16[32,15,1536]{2,1,0:T(8,128)(2,1)}), bf16[32,15,1536]{2,1,0:T(8,128)(2,1)}, u32[]{:S(2)}, u32[]{:S(2)}) async-start(bf16[32,15,1536]{2,1,0:T(8,128)(2,1)} %copy.161), calls=%async_computation.5 | async-start | bytes 3145728 | tf_op jit(solution)/shard_map/all_to_all | solution.py:120
  767.5 20.9 %copy-start.12 = (f32[96,1536]{1,0:T(8,128)}, f32[96,1536]{1,0:T(8,128)S(1)}, u32[]{:S(2)}) copy-start(f32[96,1536]{1,0:T(8,128)S(1)} %fusion.346) | copy-start | bytes 1769476
  788.6 3.5 collective-permute-start.2
  850.1 30.7 %all-to-all-start.8 = ((bf16[32,15,1536]{2,1,0:T(8,128)(2,1)}), bf16[32,15,1536]{2,1,0:T(8,128)(2,1)}, u32[]{:S(2)}, u32[]{:S(2)}) async-start(bf16[32,15,1536]{2,1,0:T(8,128)(2,1)} %copy.186), calls=%async_computation.8 | async-start | bytes 3145728 | tf_op jit(solution)/shard_map/all_to_all | solution.py:186
  892.4 29.0 %all-to-all-start.9 = ((bf16[32,15,1536]{2,1,0:T(8,128)(2,1)}), bf16[32,15,1536]{2,1,0:T(8,128)(2,1)}, u32[]{:S(2)}, u32[]{:S(2)}) async-start(bf16[32,15,1536]{2,1,0:T(8,128)(2,1)} %copy.190), calls=%async_computation.9 | async-start | bytes 3145728 | tf_op jit(solution)/shard_map/all_to_all | solution.py:202
  900.0 23.7 %copy-start.5 = (s32[384]{0:T(512)S(1)}, s32[384]{0:T(512)}, u32[]{:S(2)}) copy-start(s32[384]{0:T(512)} %get-tuple-element.23) | copy-start | bytes 4612
  941.3 20.8 %copy-start.14 = (f32[96,1536]{1,0:T(8,128)}, f32[96,1536]{1,0:T(8,128)S(1)}, u32[]{:S(2)}) copy-start(f32[96,1536]{1,0:T(8,128)S(1)} %fusion.349) | copy-start | bytes 1769476
  962.3 3.5 collective-permute-start.3
  1023.3 29.2 %all-to-all-start.10 = ((bf16[32,15,1536]{2,1,0:T(8,128)(2,1)}), bf16[32,15,1536]{2,1,0:T(8,128)(2,1)}, u32[]{:S(2)}, u32[]{:S(2)}) async-start(bf16[32,15,1536]{2,1,0:T(8,128)(2,1)} %copy.201), calls=%async_computation.10 | async-start | bytes 3145728 | tf_op jit(solution)/shard_map/all_to_all | solution.py:186
  1064.1 29.0 %all-to-all-start.11 = ((bf16[32,15,1536]{2,1,0:T(8,128)(2,1)}), bf16[32,15,1536]{2,1,0:T(8,128)(2,1)}, u32[]{:S(2)}, u32[]{:S(2)}) async-start(bf16[32,15,1536]{2,1,0:T(8,128)(2,1)} %copy.205), calls=%async_computation.11 | async-start | bytes 3145728 | tf_op jit(solution)/shard_map/all_to_all | solution.py:202
  1070.3 120.0 %reduce-scatter.18.cloned.1.call-start = ((), (), s32[]{:S(2)}) async-start(), calls=%async_computation.29 | async-start | bytes 1179648 | tf_op jit(solution)/shard_map/reduce_scatter | solution.py:298
  1073.8 21.5 %copy-start.4 = (s32[384]{0:T(512)S(1)}, s32[384]{0:T(512)}, u32[]{:S(2)}) copy-start(s32[384]{0:T(512)} %get-tuple-element.37) | copy-start | bytes 4612
  1119.8 70.5 %reduce-scatter.16.cloned.1.call-start = ((), (), s32[]{:S(2)}) async-start(), calls=%async_computation.28 | async-start | bytes 1179648 | tf_op jit(solution)/shard_map/reduce_scatter | solution.py:295
  1128.5 98.9 %reduce-scatter.20.cloned.1.call-start = ((), (), s32[]{:S(2)}) async-start(), calls=%async_computation.30 | async-start | bytes 7077888 | tf_op jit(solution)/shard_map/reduce_scatter | solution.py:301
  1135.6 158.5 %reduce-scatter.14.cloned.1.call-start = ((), (), s32[]{:S(2)}) async-start(), calls=%async_computation.27 | async-start | bytes 7077888 | tf_op jit(solution)/shard_map/reduce_scatter | solution.py:292
  1154.3 252.1 %reduce-scatter.10.cloned.1.call-start = ((), (), s32[]{:S(2)}) async-start(), calls=%async_computation.20 | async-start | bytes 3538944 | tf_op jit(solution)/shard_map/reduce_scatter | solution.py:313
  1164.8 244.5 %reduce-scatter.8.cloned.1.call-start = ((), (), s32[]{:S(2)}) async-start(), calls=%async_computation.19 | async-start | bytes 3538944 | tf_op jit(solution)/shard_map/reduce_scatter | solution.py:310
  1175.1 242.2 %reduce-scatter.12.cloned.1.call-start = ((), (), s32[]{:S(2)}) async-start(), calls=%async_computation.21 | async-start | bytes 3538944 | tf_op jit(solution)/shard_map/reduce_scatter | solution.py:316
  1190.2 603.3 %all-reduce.7.cloned.1.call-start = ((), (), s32[]{:S(2)}) async-start(), calls=%async_computation.31 | async-start | bytes 11010048 | tf_op jit(solution)/shard_map/psum | solution.py:414
  1301.9 103.6 %copy-start.77 = (bf16[96,1536]{1,0:T(8,128)(2,1)S(1)}, bf16[96,1536]{1,0:T(8,128)(2,1)}, u32[]{:S(2)}) copy-start(bf16[96,1536]{1,0:T(8,128)(2,1)} %copy-done.76) | copy-start | bytes 884740
  1301.9 103.6 %copy-start.79 = (bf16[96,1536]{1,0:T(8,128)(2,1)S(1)}, bf16[96,1536]{1,0:T(8,128)(2,1)}, u32[]{:S(2)}) copy-start(bf16[96,1536]{1,0:T(8,128)(2,1)} %copy-done.78) | copy-start | bytes 884740
  (201 other events, 722.4 us)
Sparse Core Ops, SparseCore 0:
  9.7 76.5 all-gather.14
  87.9 67.7 all-gather.16
  157.4 39.5 all-gather.20
  198.5 56.3 all-gather.18
  256.4 38.9 all-gather.22
  1119.9 17.5 reduce-scatter.17
  1140.0 20.9 reduce-scatter.15
  1163.9 63.4 reduce-scatter.19
  1230.6 63.4 reduce-scatter.13
  1296.9 38.5 reduce-scatter.9
  1338.5 38.5 reduce-scatter.7
  1379.4 37.9 reduce-scatter.11
  1420.3 373.1 all-reduce.6
where the time goes:
time: 1830 us; the launch traced here: 1810 us
  waiting for transfers between devices  776 us (42%)
  local copies, waits for them, and re-layouts  447 us (24%)
  matrix products  227 us (12%)
  blocking collectives  174 us (10%)
  other arithmetic  84.2 us (5%)
  starting transfers between devices  83 us (5%)
  between operations  18.4 us (1%)
    psum x1, waiting for transfers between devices, local(): lax.psum(grad_query.astype(jnp.bfloat16), 'expert').astype(jnp.float32)  373 us
    scatter x6, local copies, waits for them, and re-layouts, layer_backward(): d_dispatch = jnp.zeros((experts_all, capacity, width_model), jnp.bfloat16...  146 us
    scatter x6, local copies, waits for them, and re-layouts, layer_forward(): dispatch = jnp.zeros((experts_all, capacity, width_model), jnp.bfloat16)....  145 us
    psum x1, blocking collectives, local(): lax.psum(grad_gain_attn.astype(jnp.bfloat16), 'expert').astype(jnp.float32)  96.8 us
    reduce_scatter x1, waiting for transfers between devices, shard_grads(): lax.psum_scatter(grad_query.astype(jnp.bfloat16), 'fsdp', scatter_dimensi...  66.7 us
    all_gather x1, waiting for transfers between devices, local(): lax.all_gather(w_out[0], 'fsdp', axis=0, tiled=True)  57 us
    all_to_all x3, waiting for transfers between devices, layer_forward(): lax.all_to_all(result_rows, 'expert', split_axis=0, concat_axis=0, tiled=...  47.5 us
    all_to_all x3, waiting for transfers between devices, layer_backward(): lax.all_to_all(d_inner, 'expert', split_axis=0, concat_axis=0, tiled=True)  45.8 us
  transfers between devices with their start and end apart: 28, of which 20 were waited for; matrix products, arithmetic and copies ran while one was open for 16% of the time, Pallas kernels for 0%

commit v1 on v0

v1 whole, which is shorter than its diff:
```python
import functools

import jax
import jax.numpy as jnp
from jax import lax
from jax.experimental import pallas as pl
from jax.experimental.pallas import tpu as pltpu
from jax.sharding import PartitionSpec as P

MESH = pl.DeviceIdType.MESH
BF = jnp.bfloat16
F32 = jnp.float32

HEAD = 128
EPS = 1e-06
ROPE_BASE = 1000000.0
GELU_C = 0.7978845608
GELU_A = 0.044715

MB = 2
SEQ = 96
WIDTH = 1536
HALF = 768
EXPERTS = 32
SLOTS = 16
ROWS = EXPERTS * SLOTS
HIDDEN = 768
HEADS = 6
QKV = 1024


def dot(a, b):
    return jnp.dot(a, b, preferred_element_type=F32)


def dot_nt(a, b):
    return lax.dot_general(a, b, (((1,), (1,)), ((), ())), preferred_element_type=F32)


def dot_tn(a, b):
    return lax.dot_general(a, b, (((0,), (0,)), ((), ())), preferred_element_type=F32)


def aligned(start, size, unit):
    return pl.ds(pl.multiple_of(start, unit), size)


def inverse_rms(rows):
    return lax.rsqrt(jnp.mean(rows * rows, axis=-1, keepdims=True) + EPS)


def rms_back(rows, inverse, gain, grad):
    scaled = gain * grad
    return inverse * scaled - rows * (inverse * inverse * inverse) * jnp.mean(
        scaled * rows, axis=-1, keepdims=True
    )


def rotate(head, cos, sin):
    return head * cos + pltpu.roll(head, HEAD // 2, 1) * sin


def section_kernel(
    x_in,
    ct_in,
    wq_in,
    wk_in,
    wv_in,
    wo_in,
    wg_in,
    wu_in,
    wd_in,
    gain_one,
    gain_two,
    ids_t,
    logits_t,
    cos_t,
    sin_t,
    mask_t,
    acts_out,
    ingrad_out,
    gains_out,
    n2rows_out,
    dyrows_out,
    hid_out,
    dgate_out,
    dup_out,
    n1_out,
    dqkv_out,
    att_out,
    da_out,
    wqkv,
    wo,
    wg,
    wu,
    wd,
    xpair,
    n1s,
    qkvs,
    att,
    hid_one,
    part_own,
    part_send,
    part_recv,
    sel,
    cg_hi,
    cg_lo,
    dsend,
    bsend,
    n2recv,
    yrecv,
    dyrecv,
    dn2recv,
    gs,
    us,
    hid,
    acts_s,
    g_buf,
    dh_s,
    da_pair,
    dqkv_all,
    dn1_send,
    dn1_recv,
    ingrad_s,
    gains_acc,
    lw_sem,
    ws_sem,
    wr_sem,
    as_sem,
    ar_sem,
    ps_sem,
    pr_sem,
    xs_sem,
    xr_sem,
    gs_sem,
    gr_sem,
    out_sem,
    go_sem,
):
    sec = lax.axis_index("section")
    f = lax.axis_index("fsdp")
    e = lax.axis_index("expert")
    other = 1 - f
    own_rows = aligned(f * SEQ, SEQ, 16)
    other_rows = aligned(other * SEQ, SEQ, 16)
    own_half = aligned(f * HALF, HALF, 128)
    other_half = aligned(other * HALF, HALF, 128)
    my_slots = aligned(e * SLOTS, SLOTS, 16)
    partner = {"fsdp": other}
    first, second = sec == 0, sec == 1

    barrier = pltpu.get_barrier_semaphore()

    @pl.loop(1, EXPERTS)
    def _(d):
        pl.semaphore_signal(
            barrier, inc=1, device_id={"expert": lax.rem(e + d, EXPERTS)}, device_id_type=MESH
        )

    for place in ({"fsdp": other}, {"section": 1 - sec}, {"section": 1 - sec, "fsdp": other}):
        pl.semaphore_signal(barrier, inc=1, device_id=place, device_id_type=MESH)

    local = [
        (wq_in.at[:, own_half], wqkv.at[own_half, pl.ds(0, HALF)]),
        (wk_in.at[:, aligned(f * HEAD, HEAD, 128)], wqkv.at[own_half, pl.ds(HALF, HEAD)]),
        (wv_in.at[:, aligned(f * HEAD, HEAD, 128)], wqkv.at[own_half, pl.ds(HALF + HEAD, HEAD)]),
        (wo_in, wo),
        (wg_in, wg.at[own_half]),
        (wu_in, wu.at[own_half]),
        (wd_in, wd.at[aligned(f * (HIDDEN // 2), HIDDEN // 2, 16)]),
    ]
    local = [pltpu.make_async_copy(a, b, lw_sem.at[i]) for i, (a, b) in enumerate(local)]
    for copy in local:
        copy.start()
    x_local = pltpu.make_async_copy(x_in, xpair.at[:, own_rows], lw_sem.at[7])
    ct_local = pltpu.make_async_copy(ct_in, g_buf, lw_sem.at[8])
    pl.when(first)(x_local.start)
    pl.when(second)(ct_local.start)

    def remote(src, dst, i):
        return pltpu.make_async_remote_copy(
            src_ref=src,
            dst_ref=dst,
            send_sem=ws_sem.at[i],
            recv_sem=wr_sem.at[i],
            device_id=partner,
            device_id_type=MESH,
        )

    w_attn = [
        remote(wq_in.at[:, other_half], wqkv.at[own_half, pl.ds(0, HALF)], 0),
        remote(
            wk_in.at[:, aligned(other * HEAD, HEAD, 128)],
            wqkv.at[own_half, pl.ds(HALF, HEAD)],
            1,
        ),
        remote(
            wv_in.at[:, aligned(other * HEAD, HEAD, 128)],
            wqkv.at[own_half, pl.ds(HALF + HEAD, HEAD)],
            2,
        ),
    ]
    w_moe = [
        remote(wg_in, wg.at[own_half], 3),
        remote(wu_in, wu.at[own_half], 4),
        remote(wd_in, wd.at[aligned(f * (HIDDEN // 2), HIDDEN // 2, 16)], 5),
    ]
    x_remote = remote(x_in, xpair.at[:, own_rows], 6)

    pl.semaphore_wait(barrier, EXPERTS - 1 + 3)

    @pl.when(first)
    def _():
        x_remote.start()
        for copy in w_attn + w_moe:
            copy.start()

    gains_acc[...] = jnp.zeros_like(gains_acc)

    @pl.loop(0, MB)
    def _(m):
        ids = ids_t[m]
        logits = logits_t[m]
        raised = jnp.exp(logits - jnp.max(logits, axis=0, keepdims=True))
        gates = raised / jnp.sum(raised, axis=0, keepdims=True)
        expert = lax.broadcasted_iota(jnp.int32, (EXPERTS, SEQ), 0)
        named = jnp.zeros((EXPERTS, SEQ), F32)
        weight = jnp.zeros((EXPERTS, SEQ), F32)
        for k in range(4):
            hit = expert == ids[k : k + 1, :]
            named = jnp.where(hit, 1.0, named)
            weight = jnp.where(hit, gates[k : k + 1, :], weight)
        earlier = lax.broadcasted_iota(jnp.int32, (SEQ, SEQ), 0) < lax.broadcasted_iota(
            jnp.int32, (SEQ, SEQ), 1
        )
        slot = dot(named.astype(BF), jnp.where(earlier, 1.0, 0.0).astype(BF))
        slot = jnp.where(named > 0.0, slot, -1.0)
        place = lax.broadcasted_iota(jnp.int32, (EXPERTS, SLOTS, SEQ), 1).astype(F32)
        chosen = jnp.where(
            jnp.broadcast_to(slot[:, None, :], (EXPERTS, SLOTS, SEQ)) == place, 1.0, 0.0
        )
        scaled = chosen * jnp.broadcast_to(weight[:, None, :], (EXPERTS, SLOTS, SEQ))
        scaled = scaled.reshape(ROWS, SEQ)
        high = scaled.astype(BF)
        sel[m] = chosen.reshape(ROWS, SEQ).astype(BF)
        cg_hi[m] = high
        cg_lo[m] = (scaled - high.astype(F32)).astype(BF)

    def exchange(kind, m, src, dst):
        @pl.loop(1, EXPERTS)
        def _(d):
            p = lax.rem(e + d, EXPERTS)
            pltpu.make_async_remote_copy(
                src_ref=src.at[m, aligned(p * SLOTS, SLOTS, 16)],
                dst_ref=dst.at[m, my_slots],
                send_sem=as_sem.at[kind, m],
                recv_sem=ar_sem.at[kind, m],
                device_id={"expert": p},
                device_id_type=MESH,
            ).start()

        dst[m, my_slots] = src[m, my_slots]

    def received(kind, m, dst):
        whole = dst.at[m, pl.ds(0, ROWS - SLOTS)]
        pltpu.make_async_copy(whole, whole, ar_sem.at[kind, m]).wait()

    def sent(kind, m, src):
        whole = src.at[m, pl.ds(0, ROWS - SLOTS)]
        pltpu.make_async_copy(whole, whole, as_sem.at[kind, m]).wait()

    def to_partner(kind, m, src, dst):
        return pltpu.make_async_remote_copy(
            src_ref=src,
            dst_ref=dst,
            send_sem=ps_sem.at[kind, m],
            recv_sem=pr_sem.at[kind, m],
            device_id=partner,
            device_id_type=MESH,
        )

    def acts_copy(m, cross):
        return pltpu.make_async_remote_copy(
            src_ref=acts_s.at[m],
            dst_ref=xpair.at[m, own_rows],
            send_sem=xs_sem.at[cross, m],
            recv_sem=xr_sem.at[f, m],
            device_id={"section": 1, "fsdp": other} if cross else {"section": 1},
            device_id_type=MESH,
        )

    def acts_arrived(m):
        for at, rows in ((f, own_rows), (other, other_rows)):
            place = xpair.at[m, rows]
            pltpu.make_async_copy(place, place, xr_sem.at[at, m]).wait()

    def grad_copy(m):
        return pltpu.make_async_remote_copy(
            src_ref=ingrad_s.at[m],
            dst_ref=g_buf.at[m],
            send_sem=gs_sem.at[m],
            recv_sem=gr_sem.at[m],
            device_id={"section": 0},
            device_id_type=MESH,
        )

    def out_copy(i, src, dst, m):
        return pltpu.make_async_copy(src, dst, out_sem.at[i, m])

    def send_dy(m):
        gate = jnp.sum(cg_hi[m].astype(F32) + cg_lo[m].astype(F32), axis=1, keepdims=True)

        @pl.loop(0, WIDTH // 512)
        def _(j):
            cols = aligned(j * 512, 512, 128)
            bsend[m, :, cols] = (dot(sel[m], g_buf[m, :, cols]) * gate).astype(BF)

        exchange(2, m, bsend, dyrecv)

    @pl.when(second)
    def _():
        ct_local.wait()
        pl.semaphore_wait(go_sem, 1)
        for copy in w_attn:
            copy.start()
        pl.loop(0, MB)(send_dy)
        for copy in w_moe:
            copy.start()

    @pl.when(first)
    def _():
        x_local.wait()
        x_remote.wait_recv()

    for copy in local[:4]:
        copy.wait()
    for copy in w_attn:
        copy.wait_recv()

    def heads_of(ref, m, rows):
        return jnp.concatenate(
            [ref[m, rows, pl.ds(h * HEAD, HEAD)] for h in range(HEADS)], axis=0
        )

    def softmax_of(m, s, queries, keys):
        scores = dot_nt(queries, keys) * HEAD ** (-0.5)
        allowed = jnp.concatenate([mask_t[m, s]] * HEADS, axis=0)
        scores = jnp.where(allowed > 0.0, scores, -1e30)
        raised = jnp.exp(scores - jnp.max(scores, axis=-1, keepdims=True))
        return raised / jnp.sum(raised, axis=-1, keepdims=True)

    def attend(m):
        rows = xpair[m].astype(F32)
        n1s[m] = (rows * inverse_rms(rows) * gain_one[...]).astype(BF)
        cos, sin = cos_t[m], sin_t[m]
        for j in range(4):
            block = dot(n1s[m], wqkv[:, pl.ds(j * 256, 256)])
            qkvs[m, :, pl.ds(j * 256, HEAD)] = rotate(block[:, :HEAD], cos, sin).astype(BF)
            late = block[:, HEAD:]
            if j < 3:
                late = rotate(late, cos, sin)
            qkvs[m, :, pl.ds(j * 256 + HEAD, HEAD)] = late.astype(BF)

        @pl.loop(0, 2)
        def _(s):
            at = aligned(s * SEQ, SEQ, 16)
            queries = heads_of(qkvs, m, at)
            keys = qkvs[m, at, pl.ds(HALF, HEAD)]
            values = qkvs[m, at, pl.ds(HALF + HEAD, HEAD)]
            probs = softmax_of(m, s, queries, keys).astype(BF)
            mixed = dot(probs, values).astype(BF)
            for h in range(HEADS):
                att[m, at, pl.ds(h * HEAD, HEAD)] = mixed[h * SEQ : (h + 1) * SEQ]

        @pl.loop(0, WIDTH // 512)
        def _(j):
            cols = aligned(j * 512, 512, 128)
            block = dot(att[m], wo[:, cols])
            top, low = block[:SEQ], block[SEQ:]
            mine = f == 0
            hid_one[m, :, cols] = jnp.where(mine, top, low)
            part_send[m, :, cols] = jnp.where(mine, low, top).astype(BF)

        to_partner(0, m, part_send.at[m], part_recv.at[m]).start()

    def dispatch(m):
        to_partner(0, m, part_send.at[m], part_recv.at[m]).wait_recv()
        rows = xpair[m, own_rows].astype(F32) + (hid_one[m] + part_recv[m].astype(F32))
        hid_one[m] = rows
        n2 = (rows * inverse_rms(rows) * gain_two[...]).astype(BF)
        dsend[m] = dot(sel[m], n2).astype(BF)
        exchange(0, m, dsend, n2recv)

    def forward(m):
        pl.when(second)(lambda: acts_arrived(m))
        attend(m)
        dispatch(m)

    pl.loop(0, MB)(forward)

    for copy in local[4:]:
        copy.wait()
    for copy in w_moe:
        copy.wait_recv()

    @pl.when(first)
    def _():
        for copy in w_attn + w_moe:
            copy.wait_send()
        pl.semaphore_signal(go_sem, inc=1, device_id={"section": 1}, device_id_type=MESH)

    def experts(m):
        received(0, m, n2recv)
        out_copy(0, n2recv.at[m], n2rows_out.at[m], m).start()

        @pl.loop(0, HIDDEN // 256)
        def _(j):
            cols = aligned(j * 256, 256, 128)
            gate = dot(n2recv[m], wg[:, cols])
            up = dot(n2recv[m], wu[:, cols])
            bend = jnp.tanh(GELU_C * (gate + GELU_A * gate * gate * gate))
            gs[m, :, cols] = gate.astype(BF)
            us[m, :, cols] = up.astype(BF)
            hid[m, :, cols] = (0.5 * gate * (1.0 + bend) * up).astype(BF)

        out_copy(1, hid.at[m], hid_out.at[m], m).start()
        pl.when(second)(lambda: sent(2, m, bsend))

        @pl.loop(0, WIDTH // 512)
        def _(j):
            cols = aligned(j * 512, 512, 128)
            bsend[m, :, cols] = dot(hid[m], wd[:, cols]).astype(BF)

        exchange(1, m, bsend, yrecv)

    pl.loop(0, MB)(experts)

    def combine(m):
        received(1, m, yrecv)

        @pl.loop(0, WIDTH // 512)
        def _(j):
            cols = aligned(j * 512, 512, 128)
            block = yrecv[m, :, cols]
            mixed = dot_tn(cg_hi[m], block) + dot_tn(cg_lo[m], block)
            acts_s[m, :, cols] = (hid_one[m, :, cols] + mixed).astype(BF)

        out_copy(2, acts_s.at[m], acts_out.at[m], m).start()

    @pl.when(first)
    def _():
        @pl.loop(0, MB)
        def _(m):
            combine(m)
            for cross in (0, 1):
                acts_copy(m, cross).start()

        @pl.loop(0, MB)
        def _(m):
            sent(1, m, bsend)
            place = g_buf.at[m]
            pltpu.make_async_copy(place, place, gr_sem.at[m]).wait()
            send_dy(m)

    def experts_back(m):
        received(2, m, dyrecv)
        out_copy(3, dyrecv.at[m], dyrows_out.at[m], m).start()

        @pl.loop(0, HIDDEN // 256)
        def _(j):
            cols = aligned(j * 256, 256, 128)
            dhid = dot_nt(dyrecv[m], wd[cols, :])
            gate = gs[m, :, cols].astype(F32)
            up = us[m, :, cols].astype(F32)
            square = gate * gate
            bend = jnp.tanh(GELU_C * (gate + GELU_A * square * gate))
            half = 0.5 * (1.0 + bend)
            slope = half + 0.5 * gate * (1.0 - bend * bend) * (
                GELU_C * (1.0 + 3.0 * GELU_A * square)
            )
            gs[m, :, cols] = (dhid * up * slope).astype(BF)
            us[m, :, cols] = (dhid * (gate * half)).astype(BF)

        out_copy(4, gs.at[m], dgate_out.at[m], m).start()
        out_copy(5, us.at[m], dup_out.at[m], m).start()
        pl.when(first)(lambda: sent(2, m, bsend))
        pl.when(second)(lambda: sent(1, m, bsend))

        @pl.loop(0, WIDTH // 512)
        def _(j):
            cols = aligned(j * 512, 512, 128)
            block = dot_nt(gs[m], wg[cols, :]) + dot_nt(us[m], wu[cols, :])
            bsend[m, :, cols] = block.astype(BF)

        exchange(3, m, bsend, dn2recv)

    pl.loop(0, MB)(experts_back)

    def attend_back(m):
        received(3, m, dn2recv)
        rows = hid_one[m]
        inverse = inverse_rms(rows)

        @pl.loop(0, WIDTH // 512)
        def _(j):
            cols = aligned(j * 512, 512, 128)
            dh_s[m, :, cols] = dot_tn(sel[m], dn2recv[m, :, cols])

        grad = dh_s[m]
        gains_acc[1:2] += jnp.sum(grad * rows * inverse, axis=0, keepdims=True)
        total = g_buf[m].astype(F32) + rms_back(rows, inverse, gain_two[...], grad)
        dh_s[m] = total
        da_pair[m, own_rows] = total.astype(BF)
        da_copy = to_partner(1, m, da_pair.at[m, own_rows], da_pair.at[m, own_rows])
        da_copy.start()
        da_copy.wait_recv()
        out_copy(6, da_pair.at[m], da_out.at[m], m).start()

        @pl.loop(0, 2)
        def _(s):
            at = aligned(s * SEQ, SEQ, 16)
            dmix = dot_nt(da_pair[m, at], wo[...]).astype(BF)
            dmix = jnp.concatenate(
                [dmix[:, h * HEAD : (h + 1) * HEAD] for h in range(HEADS)], axis=0
            )
            queries = heads_of(qkvs, m, at)
            keys = qkvs[m, at, pl.ds(HALF, HEAD)]
            values = qkvs[m, at, pl.ds(HALF + HEAD, HEAD)]
            probs = softmax_of(m, s, queries, keys)
            dprobs = dot_nt(dmix, values)
            dvalues = dot_tn(probs.astype(BF), dmix)
            dscores = probs * (dprobs - jnp.sum(dprobs * probs, axis=-1, keepdims=True))
            dscores = (dscores * HEAD ** (-0.5)).astype(BF)
            cos = cos_t[m, at]
            sin = -sin_t[m, at]
            dkeys = rotate(dot_tn(dscores, queries), cos, sin)
            dqueries = dot(dscores, keys)
            for h in range(HEADS):
                part = rotate(dqueries[h * SEQ : (h + 1) * SEQ], cos, sin)
                dqkv_all[m, f, at, pl.ds(h * HEAD, HEAD)] = part.astype(BF)
            dqkv_all[m, f, at, pl.ds(HALF, HEAD)] = dkeys.astype(BF)
            dqkv_all[m, f, at, pl.ds(HALF + HEAD, HEAD)] = dvalues.astype(BF)

        dqkv_copy = to_partner(3, m, dqkv_all.at[m, f], dqkv_all.at[m, f])
        dqkv_copy.start()

        @pl.loop(0, WIDTH // 512)
        def _(j):
            cols = aligned(j * 512, 512, 128)
            block = dot_nt(dqkv_all[m, f], wqkv[cols, :])
            top, low = block[:SEQ], block[SEQ:]
            mine = f == 0
            part_own[:, cols] = jnp.where(mine, top, low)
            dn1_send[m, :, cols] = jnp.where(mine, low, top).astype(BF)

        dn1_copy = to_partner(2, m, dn1_send.at[m], dn1_recv.at[m])
        dn1_copy.start()
        dn1_copy.wait_recv()
        grad = part_own[...] + dn1_recv[m].astype(F32)
        rows = xpair[m, own_rows].astype(F32)
        inverse = inverse_rms(rows)
        gains_acc[0:1] += jnp.sum(grad * rows * inverse, axis=0, keepdims=True)
        ingrad_s[m] = (dh_s[m] + rms_back(rows, inverse, gain_one[...], grad)).astype(BF)
        out_copy(7, ingrad_s.at[m], ingrad_out.at[m], m).start()
        pl.when(second)(grad_copy(m).start)

    pl.loop(0, MB)(attend_back)

    pl.when(second)(lambda: pl.loop(0, MB)(combine))

    @pl.loop(0, MB)
    def _(m):
        to_partner(3, m, dqkv_all.at[m, f], dqkv_all.at[m, f]).wait_recv()
        out_copy(8, n1s.at[m, :, own_half], n1_out.at[m], m).start()
        out_copy(9, dqkv_all.at[m], dqkv_out.at[m], m).start()
        out_copy(10, att.at[m], att_out.at[m], m).start()
        sent(0, m, dsend)
        sent(3, m, bsend)
        to_partner(0, m, part_send.at[m], part_recv.at[m]).wait_send()
        to_partner(1, m, da_pair.at[m, own_rows], da_pair.at[m, own_rows]).wait_send()
        to_partner(2, m, dn1_send.at[m], dn1_recv.at[m]).wait_send()
        to_partner(3, m, dqkv_all.at[m, f], dqkv_all.at[m, f]).wait_send()

    gains_out[...] = gains_acc[...]

    @pl.when(first)
    def _():
        x_remote.wait_send()

        @pl.loop(0, MB)
        def _(m):
            for cross in (0, 1):
                acts_copy(m, cross).wait_send()

    @pl.when(second)
    def _():
        for copy in w_attn + w_moe:
            copy.wait_send()

        @pl.loop(0, MB)
        def _(m):
            grad_copy(m).wait_send()

    @pl.loop(0, MB)
    def _(m):
        pairs = (
            (n2recv, n2rows_out),
            (hid, hid_out),
            (acts_s, acts_out),
            (dyrecv, dyrows_out),
            (gs, dgate_out),
            (us, dup_out),
            (da_pair, da_out),
            (ingrad_s, ingrad_out),
            (None, n1_out),
            (dqkv_all, dqkv_out),
            (att, att_out),
        )
        for i, (src, dst) in enumerate(pairs):
            src = n1s.at[m, :, own_half] if src is None else src.at[m]
            out_copy(i, src, dst.at[m], m).wait()


def run_sections(*operands):
    def out(*shape, dtype=BF):
        return jax.ShapeDtypeStruct(shape, dtype)

    vmem = pl.BlockSpec(memory_space=pltpu.VMEM)
    anywhere = pl.BlockSpec(memory_space=pl.ANY)
    dma = pltpu.SemaphoreType.DMA
    return pl.pallas_call(
        section_kernel,
        name="sections",
        out_shape=(
            out(MB, SEQ, WIDTH),
            out(MB, SEQ, WIDTH),
            out(8, WIDTH, dtype=F32),
            out(MB, ROWS, WIDTH),
            out(MB, ROWS, WIDTH),
            out(MB, ROWS, HIDDEN),
            out(MB, ROWS, HIDDEN),
            out(MB, ROWS, HIDDEN),
            out(MB, 2 * SEQ, HALF),
            out(MB, 2, 2 * SEQ, QKV),
            out(MB, 2 * SEQ, HALF),
            out(MB, 2 * SEQ, WIDTH),
        ),
        in_specs=[anywhere] * 9 + [vmem] * 7,
        out_specs=[anywhere] * 2 + [vmem] + [anywhere] * 9,
        scratch_shapes=[
            pltpu.VMEM((WIDTH, QKV), BF),
            pltpu.VMEM((HALF, WIDTH), BF),
            pltpu.VMEM((WIDTH, HIDDEN), BF),
            pltpu.VMEM((WIDTH, HIDDEN), BF),
            pltpu.VMEM((HIDDEN, WIDTH), BF),
            pltpu.VMEM((MB, 2 * SEQ, WIDTH), BF),
            pltpu.VMEM((MB, 2 * SEQ, WIDTH), BF),
            pltpu.VMEM((MB, 2 * SEQ, QKV), BF),
            pltpu.VMEM((MB, 2 * SEQ, HALF), BF),
            pltpu.VMEM((MB, SEQ, WIDTH), F32),
            pltpu.VMEM((SEQ, WIDTH), F32),
            pltpu.VMEM((MB, SEQ, WIDTH), BF),
            pltpu.VMEM((MB, SEQ, WIDTH), BF),
            pltpu.VMEM((MB, ROWS, SEQ), BF),
            pltpu.VMEM((MB, ROWS, SEQ), BF),
            pltpu.VMEM((MB, ROWS, SEQ), BF),
            pltpu.VMEM((MB, ROWS, WIDTH), BF),
            pltpu.VMEM((MB, ROWS, WIDTH), BF),
            pltpu.VMEM((MB, ROWS, WIDTH), BF),
            pltpu.VMEM((MB, ROWS, WIDTH), BF),
            pltpu.VMEM((MB, ROWS, WIDTH), BF),
            pltpu.VMEM((MB, ROWS, WIDTH), BF),
            pltpu.VMEM((MB, ROWS, HIDDEN), BF),
            pltpu.VMEM((MB, ROWS, HIDDEN), BF),
            pltpu.VMEM((MB, ROWS, HIDDEN), BF),
            pltpu.VMEM((MB, SEQ, WIDTH), BF),
            pltpu.VMEM((MB, SEQ, WIDTH), BF),
            pltpu.VMEM((MB, SEQ, WIDTH), F32),
            pltpu.VMEM((MB, 2 * SEQ, WIDTH), BF),
            pltpu.VMEM((MB, 2, 2 * SEQ, QKV), BF),
            pltpu.VMEM((MB, SEQ, WIDTH), BF),
            pltpu.VMEM((MB, SEQ, WIDTH), BF),
            pltpu.VMEM((MB, SEQ, WIDTH), BF),
            pltpu.VMEM((8, WIDTH), F32),
            dma((9,)),
            dma((7,)),
            dma((7,)),
            dma((4, MB)),
            dma((4, MB)),
            dma((4, MB)),
            dma((4, MB)),
            dma((2, MB)),
            dma((2, MB)),
            dma((MB,)),
            dma((MB,)),
            dma((11, MB)),
            pltpu.SemaphoreType.REGULAR,
        ],
        compiler_params=pltpu.CompilerParams(
            collective_id=0, has_side_effects=True, vmem_limit_bytes=62 * 2**20
        ),
    )(*operands)


CHUNK_ROWS = 48
CHUNK_COLS = 1792


def reduce_kernel(v_in, small_in, sum_out, small_out, parts, small, reduced, rs_sem, rr_sem, gs_sem, gr_sem, ss_sem, sr_sem, l_sem):
    e = lax.axis_index("expert")
    barrier = pltpu.get_barrier_semaphore()

    @pl.loop(1, EXPERTS)
    def _(d):
        pl.semaphore_signal(
            barrier, inc=1, device_id={"expert": lax.rem(e + d, EXPERTS)}, device_id_type=MESH
        )

    pl.semaphore_wait(barrier, EXPERTS - 1)

    def remote(src, dst, send, recv, p):
        return pltpu.make_async_remote_copy(
            src_ref=src,
            dst_ref=dst,
            send_sem=send,
            recv_sem=recv,
            device_id={"expert": p},
            device_id_type=MESH,
        )

    def all_but_one(ref, sem):
        part = ref.at[pl.ds(0, EXPERTS - 1)]
        pltpu.make_async_copy(part, part, sem).wait()

    own = pltpu.make_async_copy(v_in.at[e], parts.at[e], l_sem.at[0])
    own.start()

    @pl.loop(1, EXPERTS)
    def _(d):
        p = lax.rem(e + d, EXPERTS)
        remote(v_in.at[p], parts.at[e], rs_sem, rr_sem, p).start()

    @pl.loop(1, EXPERTS)
    def _(d):
        p = lax.rem(e + d, EXPERTS)
        remote(small_in, small.at[e], ss_sem, sr_sem, p).start()

    small[e] = small_in[...]
    own.wait()
    all_but_one(parts, rr_sem)
    for i in range(CHUNK_ROWS // 16):
        rows = pl.ds(i * 16, 16)
        total = lax.fori_loop(
            1,
            EXPERTS,
            lambda k, acc: acc + parts[k, rows].astype(F32),
            parts[0, rows].astype(F32),
        )
        reduced[rows] = total.astype(BF)

    own = pltpu.make_async_copy(reduced, sum_out.at[e], l_sem.at[1])
    own.start()

    @pl.loop(1, EXPERTS)
    def _(d):
        p = lax.rem(e + d, EXPERTS)
        remote(reduced, sum_out.at[e], gs_sem, gr_sem, p).start()

    all_but_one(small, sr_sem)
    small_out[...] = lax.fori_loop(
        1, EXPERTS, lambda k, acc: acc + small[k], small[0]
    )
    own.wait()
    all_but_one(parts, rs_sem)
    all_but_one(small, ss_sem)
    all_but_one(sum_out, gr_sem)
    all_but_one(sum_out, gs_sem)


def reduce_attention(v, small):
    vmem = pl.BlockSpec(memory_space=pltpu.VMEM)
    anywhere = pl.BlockSpec(memory_space=pl.ANY)
    dma = pltpu.SemaphoreType.DMA
    return pl.pallas_call(
        reduce_kernel,
        name="reduce_attention",
        out_shape=(
            jax.ShapeDtypeStruct(v.shape, BF),
            jax.ShapeDtypeStruct(small.shape, F32),
        ),
        in_specs=[anywhere, vmem],
        out_specs=[anywhere, vmem],
        scratch_shapes=[
            pltpu.VMEM((EXPERTS, CHUNK_ROWS, CHUNK_COLS), BF),
            pltpu.VMEM((EXPERTS,) + small.shape, F32),
            pltpu.VMEM((CHUNK_ROWS, CHUNK_COLS), BF),
            dma,
            dma,
            dma,
            dma,
            dma,
            dma,
            dma((2,)),
        ],
        compiler_params=pltpu.CompilerParams(
            collective_id=1, has_side_effects=True, vmem_limit_bytes=40 * 2**20
        ),
    )(v, small)


def swap(block):
    return lax.ppermute(block, "fsdp", [(0, 1), (1, 0)])


def local(
    inputs,
    cotangent,
    segments,
    expert_ids,
    gate_logits,
    w_query,
    key_projection,
    value_projection,
    w_out,
    gain_attn,
    gain_moe,
    w_gate,
    w_up,
    w_down,
):
    f = lax.axis_index("fsdp")
    pair_segments = jnp.swapaxes(lax.all_gather(segments, "fsdp"), 0, 1)
    gains = lax.all_gather(jnp.stack([gain_attn[0], gain_moe[0]]), "fsdp", axis=1, tiled=True)
    gains = gains.astype(F32)
    same = pair_segments[..., :, None] == pair_segments[..., None, :]
    row = lax.broadcasted_iota(jnp.int32, (SEQ, SEQ), 0)
    col = lax.broadcasted_iota(jnp.int32, (SEQ, SEQ), 1)
    places = jnp.sum((same & (col < row)).astype(F32), axis=-1)
    frequency = ROPE_BASE ** (-(jnp.arange(HEAD // 2, dtype=F32) * 2.0 / HEAD))
    angles = places[..., None] * frequency
    cosine, sine = jnp.cos(angles), jnp.sin(angles)
    cos_t = jnp.concatenate([cosine, cosine], axis=-1).reshape(MB, 2 * SEQ, HEAD)
    sin_t = jnp.concatenate([-sine, sine], axis=-1).reshape(MB, 2 * SEQ, HEAD)
    mask_t = (same & (col <= row)).astype(F32)
    (
        acts,
        in_grads,
        gain_parts,
        n2rows,
        dyrows,
        hid,
        dgate,
        dup,
        n1,
        dqkv,
        att,
        da,
    ) = run_sections(
        inputs,
        cotangent,
        w_query[0],
        key_projection[0],
        value_projection[0],
        w_out[0],
        w_gate[0, 0],
        w_up[0, 0],
        w_down[0, 0],
        gains[0:1],
        gains[1:2],
        jnp.swapaxes(expert_ids[0], 1, 2),
        jnp.swapaxes(gate_logits[0], 1, 2),
        cos_t,
        sin_t,
        mask_t,
    )
    n2rows = n2rows.reshape(MB * ROWS, WIDTH)
    dyrows = dyrows.reshape(MB * ROWS, WIDTH)
    hid = hid.reshape(MB * ROWS, HIDDEN)
    dgate = dgate.reshape(MB * ROWS, HIDDEN)
    dup = dup.reshape(MB * ROWS, HIDDEN)

    def pair_sum(left, right, size):
        theirs = lax.dynamic_slice_in_dim(left, (1 - f) * size, size, 1)
        mine = lax.dynamic_slice_in_dim(left, f * size, size, 1)
        arrived = swap(dot_tn(theirs, right).astype(BF))
        return dot_tn(mine, right) + arrived.astype(F32)

    grad_gate = pair_sum(n2rows, dgate, HALF)
    grad_up = pair_sum(n2rows, dup, HALF)
    grad_down = pair_sum(hid, dyrows, HIDDEN // 2)

    n1 = n1.reshape(MB * 2 * SEQ, HALF)
    dqkv = jnp.swapaxes(dqkv, 1, 2).reshape(MB * 2 * SEQ, 2, QKV)
    dq = dqkv[:, :, :HALF].reshape(MB * 2 * SEQ, WIDTH)
    dk = dqkv[:, :, HALF : HALF + HEAD].reshape(MB * 2 * SEQ, 2 * HEAD)
    dv = dqkv[:, :, HALF + HEAD :].reshape(MB * 2 * SEQ, 2 * HEAD)
    v_first = dot_tn(n1, jnp.concatenate([dq, dk], axis=1)).astype(BF)
    gv = dot_tn(n1, dv).astype(BF)
    go = dot_tn(att.reshape(MB * 2 * SEQ, HALF), da.reshape(MB * 2 * SEQ, WIDTH)).astype(BF)
    v_all = jnp.concatenate([v_first, jnp.concatenate([gv, go], axis=1)], axis=0)
    theirs = lax.dynamic_slice_in_dim(gain_parts[:2], (1 - f) * HALF, HALF, 1)
    mine = lax.dynamic_slice_in_dim(gain_parts[:2], f * HALF, HALF, 1)
    small = (mine + swap(theirs)).reshape(12, HEAD)
    small = jnp.concatenate([small, jnp.zeros((4, HEAD), F32)], axis=0)
    total, small = reduce_attention(v_all.reshape(EXPERTS, CHUNK_ROWS, CHUNK_COLS), small)
    total = total.reshape(2 * HALF, CHUNK_COLS).astype(F32)
    small = small[:12].reshape(2, HALF)
    return (
        acts[None],
        in_grads[None],
        total[None, :HALF, :WIDTH],
        total[None, :HALF, WIDTH:],
        total[None, HALF:, : 2 * HEAD],
        total[None, HALF:, 2 * HEAD :],
        small[0][None],
        small[1][None],
        grad_gate[None, None],
        grad_up[None, None],
        grad_down[None, None],
    )


def solution(mesh):
    return jax.shard_map(
        local,
        mesh=mesh,
        in_specs=(
            P(None, ("fsdp", "expert"), None),
            P(None, ("fsdp", "expert"), None),
            P(None, ("fsdp", "expert")),
            P("section", None, ("fsdp", "expert"), None),
            P("section", None, ("fsdp", "expert"), None),
            P("section", "fsdp", None),
            P("section", "fsdp", None),
            P("section", "fsdp", None),
            P("section", "fsdp", None),
            P("section", "fsdp"),
            P("section", "fsdp"),
            P("section", "expert", "fsdp", None),
            P("section", "expert", "fsdp", None),
            P("section", "expert", "fsdp", None),
        ),
        out_specs=(
            P("section", None, ("fsdp", "expert"), None),
            P("section", None, ("fsdp", "expert"), None),
            P("section", "fsdp", None),
            P("section", "fsdp", None),
            P("section", "fsdp", None),
            P("section", "fsdp", None),
            P("section", "fsdp"),
            P("section", "fsdp"),
            P("section", "expert", "fsdp", None),
            P("section", "expert", "fsdp", None),
            P("section", "expert", "fsdp", None),
        ),
        check_vma=False,
    )
```

time: 1830 us -> 617 us (0.34)
  waiting for transfers between devices: 776 us -> 0.01 us
  Pallas kernels: 0 us -> 542 us
  local copies, waits for them, and re-layouts: 447 us -> 14.8 us
  matrix products: 227 us -> 26.9 us
  blocking collectives: 174 us -> 8.79 us
  starting transfers between devices: 83 us -> 4.05 us
  other arithmetic: 84.2 us -> 13.2 us
    pallas_call x0 -> x2, Pallas kernels: none -> 542 us  [the longest x1 411 us: run_sections(): pl.pallas_call(section_kernel, name='sections', out_shape=(out(MB, SEQ, W...]
    psum x1 -> x0, waiting for transfers between devices: 373 us -> none  [local(): lax.psum(grad_query.astype(jnp.bfloat16), 'expert').astype(jnp.float32)]
    scatter x12 -> x0, local copies, waits for them, and re-layouts: 291 us -> none  [the longest x6 146 us: layer_backward(): d_dispatch = jnp.zeros((experts_all, capacity, width_model), jnp.bfloat16...]
    dot_general x87 -> x9, matrix products: 227 us -> 26.9 us  [dot_tn(): lax.dot_general(a, b, (((0,), (0,)), ((), ())), preferred_element_type=F32)]
    all_to_all x11 -> x0, waiting for transfers between devices: 173 us -> none  [the longest x3 47.5 us: layer_forward(): lax.all_to_all(result_rows, 'expert', split_axis=0, concat_axis=0, tiled=...]
    all_gather x5 -> x0, waiting for transfers between devices: 112 us -> none  [the longest x1 57 us: local(): lax.all_gather(w_out[0], 'fsdp', axis=0, tiled=True)]
    reduce_scatter x7 -> x0, waiting for transfers between devices: 109 us -> none  [the longest x1 66.7 us: shard_grads(): lax.psum_scatter(grad_query.astype(jnp.bfloat16), 'fsdp', scatter_dimensi...]
    psum x1 -> x0, blocking collectives: 96.8 us -> none  [local(): lax.psum(grad_gain_attn.astype(jnp.bfloat16), 'expert').astype(jnp.float32)]
  transfers between devices with their start and end apart: 28 -> 4, of which waited for: 20 -> 0; matrix products, arithmetic and copies ran while one was open for 16% -> 7% of each run, Pallas kernels for 0% -> 22%
where the time goes in v1:
time: 617 us; the launch traced here: 611 us
  Pallas kernels  542 us (88%)
  matrix products  26.9 us (4%)
  local copies, waits for them, and re-layouts  14.8 us (2%)
  other arithmetic  13.2 us (2%)
  blocking collectives  8.79 us (1%)
    pallas_call x1, Pallas kernels, run_sections(): pl.pallas_call(section_kernel, name='sections', out_shape=(out(MB, SEQ, W...  411 us
    pallas_call x1, Pallas kernels, reduce_attention(): pl.pallas_call(reduce_kernel, name='reduce_attention', out_shape=(jax.Sha...  132 us
    dot_general x9, matrix products, dot_tn(): lax.dot_general(a, b, (((0,), (0,)), ((), ())), preferred_element_type=F32)  26.9 us
  transfers between devices with their start and end apart: 4, of which 0 were waited for; matrix products, arithmetic and copies ran while one was open for 7% of the time, Pallas kernels for 22%

profile of v1, /device:TPU:0, one launch (start us, length us, event | category | flops | bytes accessed | tf_op | source)
XLA Modules:
  0.0 610.9 jit_solution(15241537998935101375)
XLA Ops:
  0.7 4.5 all-gather.1
  5.2 0.7 pad_maximum_fusion.2
  5.9 4.3 all_gather.9
  10.2 0.6 fusion.28
  10.8 0.2 convert_reduce_fusion
  11.1 0.1 mul.38
  11.2 0.8 fusion.18.mask_t
  12.0 0.8 fusion.19
  12.7 0.9 pad_maximum_fusion
  13.6 410.6 %sections.1 = (bf16[2,96,1536]{2,1,0:T(8,128)(2,1)}, bf16[2,96,1536]{2,1,0:T(8,128)(2,1)}, f32[8,1536]{1,0:T(8,128)}, bf16[2,512,1536]{2,1,0:T(8,128)(2,1)}, bf1...) custom-call(bf16[2,96,1536]{2,1,0:T(8,128)(2,1)} %x_in.1, ...), custom_call_target="tpu_custom_call" | custom-call | tf_op jit(solution)/shard_map/sections/pallas_call | solution.py:631
  424.2 0.8 slice.51
  425.0 0.8 collective-permute-start
  425.9 4.5 convolution_convert_fusion.3
  430.4 1.2 collective-permute-start.1
  431.6 0.0 copy-done.7
  431.6 2.5 convolution_convert_fusion.2
  434.0 0.9 collective-permute-start.2
  434.9 0.0 copy-done.5
  434.9 3.7 convolution_convert_fusion.1
  438.6 1.2 collective-permute-start.3
  439.8 0.1 copy.41
  439.9 0.1 fusion.27
  440.0 0.1 slice.62
  440.1 0.7 copy.42
  440.8 0.2 copy.43
  441.0 0.2 copy.44
  441.2 0.4 convolution_convert_fusion.4
  441.6 1.6 convolution_convert_fusion
  443.3 1.4 bitcast_convert_fusion.1
  444.7 8.5 %maximum_maximum_fusion = bf16[1536,1792]{1,0:T(8,128)(2,1)} fusion(bf16[768,1536]{1,0:T(8,128)(2,1)S(1)} %bitcast_convert_fusion.1, bf16[768,256]{1,0:T(8,128)(2,1)S(1)} %convolution_convert_fusion.4, bf16[768,1792]{1,0:T(8,128)(2,1)S(1)} %convolution_convert_fusion), kind=kLoop, calls=%fused_computation | loop fusion | flops 16515072 | bytes 11010048 | tf_op jit(solution)/shard_map/concatenate | solution.py:900
  453.2 0.0 collective-permute-done
  453.3 2.6 copy-done
  455.8 131.8 %reduce_attention.1 = (bf16[32,48,1792]{2,1,0:T(8,128)(2,1)S(1)}, f32[16,128]{1,0:T(8,128)S(1)}) custom-call(bf16[32,48,1792]{2,1,0:T(8,128)(2,1)S(1)} %bitcast.71, f32[16,128]{1,0:T(8,128)S(1)} %concatenate.25.small_in), custom_call_target="tpu_custom_call" | custom-call | tf_op jit(solution)/shard_map/reduce_attention/pallas_call | solution.py:784
  587.6 1.2 bitcast_convert_fusion
  588.8 5.2 slice_bitcast_fusion
  594.0 0.6 copy.51
  594.6 0.6 copy.52
  595.2 1.2 slice_bitcast_fusion.2
  596.4 0.0 collective-permute-done.1
  596.4 0.0 copy-done.12
  596.5 4.3 add_bitcast_fusion.2
  600.7 0.0 collective-permute-done.2
  600.8 4.3 add_bitcast_fusion.1
  605.1 0.0 collective-permute-done.3
  605.1 4.2 add_bitcast_fusion
  609.3 0.8 copy.55
  610.1 0.0 copy-done.2
  610.1 0.8 copy.56
  (34 shorter events, 0.1 us)
Async XLA Ops:
  425.0 28.2 %collective-permute-start = (f32[2,768]{1,0:T(2,128)S(1)}, f32[2,768]{1,0:T(2,128)S(1)}, u32[]{:S(2)}, u32[]{:S(2)}) collective-permute-start(f32[2,768]{1,0:T(2,128)S(1)} %constant_dynamic-slice_fusion), channel_id=1, source_target_pairs={{0,32},{32,0},{1,33},{33,1},{2,34},{34,2},{3,35},{35,3},{4,36},{36... | collective-permute-start | bytes 18440 | tf_op jit(solution)/shard_map/ppermute | solution.py:812
  425.9 5.7 copy-start.7
  425.9 5.7 copy-start.10
  430.4 166.1 %collective-permute-start.1 = (bf16[768,768]{1,0:T(8,128)(2,1)}, bf16[768,768]{1,0:T(8,128)(2,1)}, u32[]{:S(2)}, u32[]{:S(2)}) collective-permute-start(bf16[768,768]{1,0:T(8,128)(2,1)} %convolution_convert_fusion.3), channel_id=1, source_target_pairs={{0,32},{32,0},{1,33},{33,1},{2,34},{34,2},{3,35},{35,3},{4,36},{36... | collective-permute-start | bytes 3538952 | tf_op jit(solution)/shard_map/ppermute | solution.py:812
  431.6 3.3 copy-start.5
  434.0 166.7 %collective-permute-start.2 = (bf16[768,768]{1,0:T(8,128)(2,1)}, bf16[768,768]{1,0:T(8,128)(2,1)}, u32[]{:S(2)}, u32[]{:S(2)}) collective-permute-start(bf16[768,768]{1,0:T(8,128)(2,1)} %convolution_convert_fusion.2), channel_id=1, source_target_pairs={{0,32},{32,0},{1,33},{33,1},{2,34},{34,2},{3,35},{35,3},{4,36},{36... | collective-permute-start | bytes 3538952 | tf_op jit(solution)/shard_map/ppermute | solution.py:812
  434.9 4.9 copy-start.1
  438.6 166.5 %collective-permute-start.3 = (bf16[384,1536]{1,0:T(8,128)(2,1)}, bf16[384,1536]{1,0:T(8,128)(2,1)}, u32[]{:S(2)}, u32[]{:S(2)}) collective-permute-start(bf16[384,1536]{1,0:T(8,128)(2,1)} %convolution_convert_fusion.1), channel_id=1, source_target_pairs={{0,32},{32,0},{1,33},{33,1},{2,34},{34,2},{3,35},{35,3},{4,36},{36... | collective-permute-start | bytes 3538952 | tf_op jit(solution)/shard_map/ppermute | solution.py:812
  440.0 1.2 copy-start.4
  441.6 1.7 copy-start.13
  441.6 1.7 copy-start.14
  453.2 2.6 copy-start
  588.8 7.6 %copy-start.12 = (bf16[2,512,768]{2,1,0:T(8,128)(2,1)S(1)}, bf16[2,512,768]{2,1,0:T(8,128)(2,1)}, u32[]{:S(2)}) copy-start(bf16[2,512,768]{2,1,0:T(8,128)(2,1)} %get-tuple-element.35) | copy-start | bytes 4718596
  594.0 2.4 copy-start.8
  596.4 4.3 copy-start.11
  600.7 4.3 copy-start.6
  600.7 4.3 copy-start.9
  605.1 4.2 copy-start.3
  605.1 5.0 copy-start.2

commit v2 on v1

--- a/solution.py
+++ b/solution.py
@@ -702,114 +702,400 @@
     )(*operands)
 
 
-CHUNK_ROWS = 48
-CHUNK_COLS = 1792
-
-
-def reduce_kernel(v_in, small_in, sum_out, small_out, parts, small, reduced, rs_sem, rr_sem, gs_sem, gr_sem, ss_sem, sr_sem, l_sem):
+BAND = 192
+SLICE = 48
+WIDE = 1792
+NARROW = 896
+
+
+def grads_kernel(
+    n2_in,
+    dy_in,
+    hid_in,
+    dgate_in,
+    dup_in,
+    n1_in,
+    dqkv_in,
+    att_in,
+    da_in,
+    gains_in,
+    q_out,
+    k_out,
+    v_out,
+    o_out,
+    gate_out,
+    up_out,
+    down_out,
+    gains_out,
+    n2,
+    dy,
+    hid,
+    dgate,
+    dup,
+    n1,
+    dqkv,
+    att,
+    da,
+    v_a,
+    v_b,
+    r1_a,
+    r1_b,
+    s1_a,
+    s1_b,
+    r2_a,
+    r2_b,
+    s2_a,
+    s2_b,
+    r3_a,
+    r3_b,
+    g_a,
+    g_b,
+    their_gate,
+    their_up,
+    their_down,
+    part_gate,
+    part_up,
+    part_down,
+    own_gate,
+    own_up,
+    own_down,
+    small,
+    small_recv,
+    load_sem,
+    send_sem,
+    recv_sem,
+    pair_send,
+    pair_recv,
+    small_send,
+    small_recv_sem,
+    out_sem,
+):
+    f = lax.axis_index("fsdp")
     e = lax.axis_index("expert")
+    y, x, z = e // 8, lax.rem(e // 4, 2), lax.rem(e, 4)
+    other = 1 - f
+    own_half = aligned(f * HALF, HALF, 128)
+    other_half = aligned(other * HALF, HALF, 128)
+    own_quarter = aligned(f * (HIDDEN // 2), HIDDEN // 2, 128)
+    other_quarter = aligned(other * (HIDDEN // 2), HIDDEN // 2, 128)
+
+    def along_y(d):
+        return {"expert": lax.rem(y + d, 4) * 8 + x * 4 + z}
+
+    def along_z(d):
+        return {"expert": y * 8 + x * 4 + lax.rem(z + d, 4)}
+
+    twin = {"expert": y * 8 + (1 - x) * 4 + z}
+    partner = {"fsdp": other}
+
     barrier = pltpu.get_barrier_semaphore()
-
-    @pl.loop(1, EXPERTS)
-    def _(d):
-        pl.semaphore_signal(
-            barrier, inc=1, device_id={"expert": lax.rem(e + d, EXPERTS)}, device_id_type=MESH
-        )
-
-    pl.semaphore_wait(barrier, EXPERTS - 1)
-
-    def remote(src, dst, send, recv, p):
+    neighbours = [along_y(d) for d in (1, 2, 3)] + [along_z(d) for d in (1, 2, 3)]
+    neighbours += [twin, partner]
+    for place in neighbours:
+        pl.semaphore_signal(barrier, inc=1, device_id=place, device_id_type=MESH)
+
+    loads = [
+        (att_in, att),
+        (da_in, da),
+        (n1_in, n1),
+        (dqkv_in, dqkv),
+        (n2_in, n2),
+        (dgate_in, dgate),
+        (dup_in, dup),
+        (hid_in, hid),
+        (dy_in, dy),
+    ]
+    loads = [pltpu.make_async_copy(a, b, load_sem.at[i]) for i, (a, b) in enumerate(loads)]
+    for copy in loads:
+        copy.start()
+
+    def remote(src, dst, send, recv, place):
         return pltpu.make_async_remote_copy(
             src_ref=src,
             dst_ref=dst,
             send_sem=send,
             recv_sem=recv,
-            device_id={"expert": p},
+            device_id=place,
             device_id_type=MESH,
         )
 
-    def all_but_one(ref, sem):
-        part = ref.at[pl.ds(0, EXPERTS - 1)]
-        pltpu.make_async_copy(part, part, sem).wait()
-
-    own = pltpu.make_async_copy(v_in.at[e], parts.at[e], l_sem.at[0])
-    own.start()
-
-    @pl.loop(1, EXPERTS)
-    def _(d):
-        p = lax.rem(e + d, EXPERTS)
-        remote(v_in.at[p], parts.at[e], rs_sem, rr_sem, p).start()
-
-    @pl.loop(1, EXPERTS)
-    def _(d):
-        p = lax.rem(e + d, EXPERTS)
-        remote(small_in, small.at[e], ss_sem, sr_sem, p).start()
-
-    small[e] = small_in[...]
-    own.wait()
-    all_but_one(parts, rr_sem)
-    for i in range(CHUNK_ROWS // 16):
-        rows = pl.ds(i * 16, 16)
-        total = lax.fori_loop(
-            1,
-            EXPERTS,
-            lambda k, acc: acc + parts[k, rows].astype(F32),
-            parts[0, rows].astype(F32),
+    def wait_for(ref, sem):
+        pltpu.make_async_copy(ref, ref, sem).wait()
+
+    for copy in loads[:2]:
+        copy.wait()
+
+    @pl.loop(0, WIDTH // 512)
+    def _(j):
+        cols = aligned(j * 512, 512, 128)
+        v_b[:, cols] = dot_tn(att[...], da[:, cols]).astype(BF)
+
+    for copy in loads[2:4]:
+        copy.wait()
+
+    def over_micro(cols):
+        block = jnp.concatenate([dqkv[m, :, :, cols] for m in range(MB)], axis=1)
+        return [dot_tn(n1[...], block[g]).astype(BF) for g in range(2)]
+
+    for g, block in enumerate(over_micro(pl.ds(HALF + HEAD, HEAD))):
+        v_b[:, pl.ds(WIDTH + g * HEAD, HEAD)] = block
+    pl.semaphore_wait(barrier, len(neighbours))
+
+    lanes = (
+        (0, v_a, r1_a, s1_a, r2_a, s2_a, r3_a, g_a, along_y, y, along_z, z),
+        (1, v_b, r1_b, s1_b, r2_b, s2_b, r3_b, g_b, along_z, z, along_y, y),
+    )
+
+    def spread_one(lane):
+        i, v, r1, _, _, _, _, _, axis, at, _, _ = lane
+        for d in (1, 2, 3):
+            rows = aligned(lax.rem(at + d, 4) * BAND, BAND, 16)
+            remote(v.at[rows], r1.at[at], send_sem.at[i, 0], recv_sem.at[i, 0], axis(d)).start()
+
+    spread_one(lanes[1])
+    for j in range(3):
+        for g, block in enumerate(over_micro(pl.ds(j * 256, 256))):
+            v_a[:, pl.ds(g * HALF + j * 256, 256)] = block
+    for g, block in enumerate(over_micro(pl.ds(HALF, HEAD))):
+        v_a[:, pl.ds(WIDTH + g * HEAD, HEAD)] = block
+    spread_one(lanes[0])
+
+    small[...] = gains_in[...]
+    small_pair = remote(
+        small.at[:, other_half],
+        small_recv.at[0],
+        small_send.at[0],
+        small_recv_sem.at[0],
+        partner,
+    )
+    small_pair.start()
+
+    for copy in loads[4:6]:
+        copy.wait()
+    their_gate[...] = dot_tn(n2[:, other_half], dgate[...]).astype(BF)
+    pair = [remote(their_gate, part_gate, pair_send.at[0], pair_recv.at[0], partner)]
+    pair[0].start()
+    loads[6].wait()
+    their_up[...] = dot_tn(n2[:, other_half], dup[...]).astype(BF)
+    pair.append(remote(their_up, part_up, pair_send.at[1], pair_recv.at[1], partner))
+    pair[1].start()
+    for copy in loads[7:]:
+        copy.wait()
+    their_down[...] = dot_tn(hid[:, other_quarter], dy[...]).astype(BF)
+    pair.append(remote(their_down, part_down, pair_send.at[2], pair_recv.at[2], partner))
+    pair[2].start()
+    own_gate[...] = dot_tn(n2[:, own_half], dgate[...])
+    own_up[...] = dot_tn(n2[:, own_half], dup[...])
+    own_down[...] = dot_tn(hid[:, own_quarter], dy[...])
+
+    def spread_small(i, axis):
+        for d in (1, 2, 3):
+            remote(
+                small.at[:, pl.ds(0, HALF)],
+                small_recv.at[1 + 3 * i + d - 1],
+                small_send.at[1 + 3 * i + d - 1],
+                small_recv_sem.at[1 + 3 * i + d - 1],
+                axis(d),
+            ).start()
+
+    def join_small(i, axis):
+        for d in (1, 2, 3):
+            remote(
+                small.at[:, pl.ds(0, HALF)],
+                small_recv.at[1 + 3 * i + d - 1],
+                small_send.at[1 + 3 * i + d - 1],
+                small_recv_sem.at[1 + 3 * i + d - 1],
+                axis(d),
+            ).wait()
+        total = small[:, pl.ds(0, HALF)]
+        for d in (1, 2, 3):
+            total = total + small_recv[1 + 3 * i + d - 1]
+        small[:, pl.ds(0, HALF)] = total
+
+    small_pair.wait()
+    small[:, pl.ds(0, HALF)] = small[:, own_half] + small_recv[0]
+    spread_small(0, along_y)
+
+    def join_one(lane):
+        i, v, r1, s1, r2, _, _, _, _, at, axis, to = lane
+        wait_for(r1.at[pl.ds(0, 3)], recv_sem.at[i, 0])
+        total = v[aligned(at * BAND, BAND, 16)].astype(F32)
+        for d in (1, 2, 3):
+            total = total + r1[lax.rem(at + d, 4)].astype(F32)
+        s1[...] = total.astype(BF)
+        for d in (1, 2, 3):
+            rows = aligned(lax.rem(to + d, 4) * SLICE, SLICE, 16)
+            remote(s1.at[rows], r2.at[to], send_sem.at[i, 1], recv_sem.at[i, 1], axis(d)).start()
+
+    join_one(lanes[1])
+    join_one(lanes[0])
+    join_small(0, along_y)
+    spread_small(1, along_z)
+
+    mine = aligned(x * NARROW, NARROW, 128)
+    theirs = aligned((1 - x) * NARROW, NARROW, 128)
+
+    def join_two(lane):
+        i, _, _, s1, r2, s2, r3, _, _, _, _, to = lane
+        wait_for(r2.at[pl.ds(0, 3)], recv_sem.at[i, 1])
+        total = s1[aligned(to * SLICE, SLICE, 16)].astype(F32)
+        for d in (1, 2, 3):
+            total = total + r2[lax.rem(to + d, 4)].astype(F32)
+        s2[...] = total.astype(BF)
+        remote(s2.at[:, theirs], r3, send_sem.at[i, 2], recv_sem.at[i, 2], twin).start()
+
+    join_two(lanes[1])
+    join_two(lanes[0])
+    join_small(1, along_z)
+    small_twin = remote(
+        small.at[:, pl.ds(0, HALF)],
+        small_recv.at[7],
+        small_send.at[7],
+        small_recv_sem.at[7],
+        twin,
+    )
+    small_twin.start()
+
+    def place_of(lane):
+        _, _, _, _, _, _, _, _, _, at, _, to = lane
+        return aligned(at * BAND + to * SLICE, SLICE, 16)
+
+    def join_three(lane):
+        i, _, _, _, _, s2, r3, g, _, _, _, _ = lane
+        wait_for(r3, recv_sem.at[i, 2])
+        total = s2[:, mine].astype(F32) + r3[...].astype(F32)
+        g[place_of(lane), mine] = total.astype(BF)
+        part = g.at[place_of(lane), mine]
+        remote(part, part, send_sem.at[i, 3], recv_sem.at[i, 3], twin).start()
+
+    def gather_two(lane):
+        i, _, _, _, _, _, _, g, _, _, axis, _ = lane
+        wait_for(g.at[place_of(lane), theirs], recv_sem.at[i, 3])
+        part = g.at[place_of(lane)]
+        for d in (1, 2, 3):
+            remote(part, part, send_sem.at[i, 4], recv_sem.at[i, 4], axis(d)).start()
+
+    def gather_one(lane):
+        i, _, _, _, _, _, _, g, axis, at, _, _ = lane
+        wait_for(g.at[pl.ds(0, 3 * SLICE)], recv_sem.at[i, 4])
+        part = g.at[aligned(at * BAND, BAND, 16)]
+        for d in (1, 2, 3):
+            remote(part, part, send_sem.at[i, 5], recv_sem.at[i, 5], axis(d)).start()
+
+    for step in (join_three, gather_two, gather_one):
+        step(lanes[1])
+        step(lanes[0])
+
+    small_twin.wait()
+    gains_out[...] = small[:, pl.ds(0, HALF)] + small_recv[7]
+
+    def out_copy(i, src, dst):
+        copy = pltpu.make_async_copy(src, dst, out_sem.at[i])
+        copy.start()
+        return copy
+
+    outs = []
+    for i, (arrived, part, own, dst) in enumerate(
+        (
+            (pair[0], part_gate, own_gate, gate_out),
+            (pair[1], part_up, own_up, up_out),
+            (pair[2], part_down, own_down, down_out),
         )
-        reduced[rows] = total.astype(BF)
-
-    own = pltpu.make_async_copy(reduced, sum_out.at[e], l_sem.at[1])
-    own.start()
-
-    @pl.loop(1, EXPERTS)
-    def _(d):
-        p = lax.rem(e + d, EXPERTS)
-        remote(reduced, sum_out.at[e], gs_sem, gr_sem, p).start()
-
-    all_but_one(small, sr_sem)
-    small_out[...] = lax.fori_loop(
-        1, EXPERTS, lambda k, acc: acc + small[k], small[0]
-    )
-    own.wait()
-    all_but_one(parts, rs_sem)
-    all_but_one(small, ss_sem)
-    all_but_one(sum_out, gr_sem)
-    all_but_one(sum_out, gs_sem)
-
-
-def reduce_attention(v, small):
+    ):
+        arrived.wait_recv()
+        part[...] = (own[...] + part[...].astype(F32)).astype(BF)
+        outs.append(out_copy(i, part, dst))
+
+    wait_for(g_b.at[pl.ds(0, 3 * BAND)], recv_sem.at[1, 5])
+    outs.append(out_copy(3, g_b.at[:, pl.ds(0, WIDTH)], o_out))
+    outs.append(out_copy(4, g_b.at[:, pl.ds(WIDTH, 256)], v_out))
+    wait_for(g_a.at[pl.ds(0, 3 * BAND)], recv_sem.at[0, 5])
+    outs.append(out_copy(5, g_a.at[:, pl.ds(0, WIDTH)], q_out))
+    outs.append(out_copy(6, g_a.at[:, pl.ds(WIDTH, 256)], k_out))
+
+    for lane in lanes:
+        i, v, _, s1, _, s2, _, g = lane[:8]
+        wait_for(v.at[pl.ds(0, 3 * BAND)], send_sem.at[i, 0])
+        wait_for(s1.at[pl.ds(0, 3 * SLICE)], send_sem.at[i, 1])
+        wait_for(s2.at[:, theirs], send_sem.at[i, 2])
+        wait_for(g.at[place_of(lane), mine], send_sem.at[i, 3])
+        wait_for(g.at[pl.ds(0, 3 * SLICE)], send_sem.at[i, 4])
+        wait_for(g.at[pl.ds(0, 3 * BAND)], send_sem.at[i, 5])
+    for copy in pair:
+        copy.wait_send()
+    for copy in outs:
+        copy.wait()
+
+
+def reduce_grads(*operands):
+    def out(*shape):
+        return jax.ShapeDtypeStruct(shape, BF)
+
     vmem = pl.BlockSpec(memory_space=pltpu.VMEM)
     anywhere = pl.BlockSpec(memory_space=pl.ANY)
     dma = pltpu.SemaphoreType.DMA
+    lane = [
+        pltpu.VMEM((HALF, WIDE), BF),
+        pltpu.VMEM((4, BAND, WIDE), BF),
+        pltpu.VMEM((BAND, WIDE), BF),
+        pltpu.VMEM((4, SLICE, WIDE), BF),
+        pltpu.VMEM((SLICE, WIDE), BF),
+        pltpu.VMEM((SLICE, NARROW), BF),
+        pltpu.VMEM((HALF, WIDE), BF),
+    ]
+    expert = [
+        pltpu.VMEM((HALF, HIDDEN), BF),
+        pltpu.VMEM((HALF, HIDDEN), BF),
+        pltpu.VMEM((HIDDEN // 2, WIDTH), BF),
+    ]
     return pl.pallas_call(
-        reduce_kernel,
-        name="reduce_attention",
+        grads_kernel,
+        name="grads",
         out_shape=(
-            jax.ShapeDtypeStruct(v.shape, BF),
-            jax.ShapeDtypeStruct(small.shape, F32),
+            out(HALF, WIDTH),
+            out(HALF, 256),
+            out(HALF, 256),
+            out(HALF, WIDTH),
+            out(HALF, HIDDEN),
+            out(HALF, HIDDEN),
+            out(HIDDEN // 2, WIDTH),
+            jax.ShapeDtypeStruct((8, HALF), F32),
         ),
-        in_specs=[anywhere, vmem],
-        out_specs=[anywhere, vmem],
+        in_specs=[anywhere] * 9 + [vmem],
+        out_specs=[anywhere] * 7 + [vmem],
         scratch_shapes=[
-            pltpu.VMEM((EXPERTS, CHUNK_ROWS, CHUNK_COLS), BF),
-            pltpu.VMEM((EXPERTS,) + small.shape, F32),
-            pltpu.VMEM((CHUNK_ROWS, CHUNK_COLS), BF),
-            dma,
-            dma,
-            dma,
-            dma,
-            dma,
-            dma,
-            dma((2,)),
+            pltpu.VMEM((MB * ROWS, WIDTH), BF),
+            pltpu.VMEM((MB * ROWS, WIDTH), BF),
+            pltpu.VMEM((MB * ROWS, HIDDEN), BF),
+            pltpu.VMEM((MB * ROWS, HIDDEN), BF),
+            pltpu.VMEM((MB * ROWS, HIDDEN), BF),
+            pltpu.VMEM((MB * 2 * SEQ, HALF), BF),
+            pltpu.VMEM((MB, 2, 2 * SEQ, QKV), BF),
+            pltpu.VMEM((MB * 2 * SEQ, HALF), BF),
+            pltpu.VMEM((MB * 2 * SEQ, WIDTH), BF),
+        ]
+        + [part for shape in lane for part in (shape, shape)]
+        + expert
+        + expert
+        + [
+            pltpu.VMEM((HALF, HIDDEN), F32),
+            pltpu.VMEM((HALF, HIDDEN), F32),
+            pltpu.VMEM((HIDDEN // 2, WIDTH), F32),
+            pltpu.VMEM((8, WIDTH), F32),
+            pltpu.VMEM((8, 8, HALF), F32),
+            dma((9,)),
+            dma((2, 6)),
+            dma((2, 6)),
+            dma((3,)),
+            dma((3,)),
+            dma((8,)),
+            dma((8,)),
+            dma((7,)),
         ],
         compiler_params=pltpu.CompilerParams(
-            collective_id=1, has_side_effects=True, vmem_limit_bytes=40 * 2**20
+            collective_id=1, has_side_effects=True, vmem_limit_bytes=62 * 2**20
         ),
-    )(v, small)
-
-
-def swap(block):
-    return lax.ppermute(block, "fsdp", [(0, 1), (1, 0)])
+    )(*operands)
 
 
 def local(
@@ -828,7 +1114,6 @@
     w_up,
     w_down,
 ):
-    f = lax.axis_index("fsdp")
     pair_segments = jnp.swapaxes(lax.all_gather(segments, "fsdp"), 0, 1)
     gains = lax.all_gather(jnp.stack([gain_attn[0], gain_moe[0]]), "fsdp", axis=1, tiled=True)
     gains = gains.astype(F32)
@@ -873,50 +1158,30 @@
         sin_t,
         mask_t,
     )
-    n2rows = n2rows.reshape(MB * ROWS, WIDTH)
-    dyrows = dyrows.reshape(MB * ROWS, WIDTH)
-    hid = hid.reshape(MB * ROWS, HIDDEN)
-    dgate = dgate.reshape(MB * ROWS, HIDDEN)
-    dup = dup.reshape(MB * ROWS, HIDDEN)
-
-    def pair_sum(left, right, size):
-        theirs = lax.dynamic_slice_in_dim(left, (1 - f) * size, size, 1)
-        mine = lax.dynamic_slice_in_dim(left, f * size, size, 1)
-        arrived = swap(dot_tn(theirs, right).astype(BF))
-        return dot_tn(mine, right) + arrived.astype(F32)
-
-    grad_gate = pair_sum(n2rows, dgate, HALF)
-    grad_up = pair_sum(n2rows, dup, HALF)
-    grad_down = pair_sum(hid, dyrows, HIDDEN // 2)
-
-    n1 = n1.reshape(MB * 2 * SEQ, HALF)
-    dqkv = jnp.swapaxes(dqkv, 1, 2).reshape(MB * 2 * SEQ, 2, QKV)
-    dq = dqkv[:, :, :HALF].reshape(MB * 2 * SEQ, WIDTH)
-    dk = dqkv[:, :, HALF : HALF + HEAD].reshape(MB * 2 * SEQ, 2 * HEAD)
-    dv = dqkv[:, :, HALF + HEAD :].reshape(MB * 2 * SEQ, 2 * HEAD)
-    v_first = dot_tn(n1, jnp.concatenate([dq, dk], axis=1)).astype(BF)
-    gv = dot_tn(n1, dv).astype(BF)
-    go = dot_tn(att.reshape(MB * 2 * SEQ, HALF), da.reshape(MB * 2 * SEQ, WIDTH)).astype(BF)
-    v_all = jnp.concatenate([v_first, jnp.concatenate([gv, go], axis=1)], axis=0)
-    theirs = lax.dynamic_slice_in_dim(gain_parts[:2], (1 - f) * HALF, HALF, 1)
-    mine = lax.dynamic_slice_in_dim(gain_parts[:2], f * HALF, HALF, 1)
-    small = (mine + swap(theirs)).reshape(12, HEAD)
-    small = jnp.concatenate([small, jnp.zeros((4, HEAD), F32)], axis=0)
-    total, small = reduce_attention(v_all.reshape(EXPERTS, CHUNK_ROWS, CHUNK_COLS), small)
-    total = total.reshape(2 * HALF, CHUNK_COLS).astype(F32)
-    small = small[:12].reshape(2, HALF)
+    gq, gk, gv, go, grad_gate, grad_up, grad_down, gains = reduce_grads(
+        n2rows.reshape(MB * ROWS, WIDTH),
+        dyrows.reshape(MB * ROWS, WIDTH),
+        hid.reshape(MB * ROWS, HIDDEN),
+        dgate.reshape(MB * ROWS, HIDDEN),
+        dup.reshape(MB * ROWS, HIDDEN),
+        n1.reshape(MB * 2 * SEQ, HALF),
+        dqkv,
+        att.reshape(MB * 2 * SEQ, HALF),
+        da.reshape(MB * 2 * SEQ, WIDTH),
+        gain_parts,
+    )
     return (
         acts[None],
         in_grads[None],
-        total[None, :HALF, :WIDTH],
-        total[None, :HALF, WIDTH:],
-        total[None, HALF:, : 2 * HEAD],
-        total[None, HALF:, 2 * HEAD :],
-        small[0][None],
-        small[1][None],
-        grad_gate[None, None],
-        grad_up[None, None],
-        grad_down[None, None],
+        gq[None].astype(F32),
+        gk[None].astype(F32),
+        gv[None].astype(F32),
+        go[None].astype(F32),
+        gains[0:1],
+        gains[1:2],
+        grad_gate[None, None].astype(F32),
+        grad_up[None, None].astype(F32),
+        grad_down[None, None].astype(F32),
     )
 
 

time: 617 us -> 524 us (0.85)
  Pallas kernels: 542 us -> 491 us
  matrix products: 26.9 us -> 0 us
  local copies, waits for them, and re-layouts: 14.8 us -> 4.85 us
    pallas_call x1, Pallas kernels: 132 us -> 89.5 us  [reduce_grads(): pl.pallas_call(grads_kernel, name='grads', out_shape=(out(HALF, WIDTH), o...]
    dot_general x9 -> x0, matrix products: 26.9 us -> none  [dot_tn(): lax.dot_general(a, b, (((0,), (0,)), ((), ())), preferred_element_type=F32)]
    convert_element_type x1 -> x7, other arithmetic: 1.19 us -> 14.4 us  [the longest x1 2.82 us: local(): gq[None].astype(F32)]
    pallas_call x1, Pallas kernels: 411 us -> 401 us  [run_sections(): pl.pallas_call(section_kernel, name='sections', out_shape=(out(MB, SEQ, W...]
    concatenate x1 -> x0, other arithmetic: 8.51 us -> none  [local(): jnp.concatenate([v_first, jnp.concatenate([gv, go], axis=1)], axis=0)]
    broadcast_in_dim x2 -> x0, local copies, waits for them, and re-layouts: 6.45 us -> none  [the longest x1 5.21 us: local(): total[None, HALF:, 2 * HEAD:]]
  transfers between devices with their start and end apart: 4 -> 0, of which waited for: 0 -> 0; matrix products, arithmetic and copies ran while one was open for 7% -> 0% of each run, Pallas kernels for 22% -> 0%
where the time goes in v2:
time: 524 us; the launch traced here: 523 us
  Pallas kernels  491 us (94%)
  other arithmetic  17.8 us (3%)
  blocking collectives  8.79 us (2%)
    pallas_call x1, Pallas kernels, run_sections(): pl.pallas_call(section_kernel, name='sections', out_shape=(out(MB, SEQ, W...  401 us
    pallas_call x1, Pallas kernels, reduce_grads(): pl.pallas_call(grads_kernel, name='grads', out_shape=(out(HALF, WIDTH), o...  89.5 us

profile of v2, /device:TPU:0, one launch (start us, length us, event | category | flops | bytes accessed | tf_op | source)
XLA Modules:
  0.0 523.1 jit_solution(833819777277950442)
XLA Ops:
  0.7 4.5 all-gather.1
  5.1 0.7 pad_maximum_fusion.2
  5.8 4.3 all_gather.9
  10.2 0.6 fusion.3
  10.8 0.2 convert_reduce_fusion
  11.0 0.1 mul.22
  11.1 0.8 fusion.mask_t
  11.9 0.8 fusion.1
  12.7 0.9 pad_maximum_fusion
  13.6 401.4 %sections.1 = (bf16[2,96,1536]{2,1,0:T(8,128)(2,1)}, bf16[2,96,1536]{2,1,0:T(8,128)(2,1)}, f32[8,1536]{1,0:T(8,128)}, bf16[2,512,1536]{2,1,0:T(8,128)(2,1)}, bf1...) custom-call(bf16[2,96,1536]{2,1,0:T(8,128)(2,1)} %x_in.1, ...), custom_call_target="tpu_custom_call" | custom-call | tf_op jit(solution)/shard_map/sections/pallas_call | solution.py:631
  415.0 89.5 %grads.1 = (bf16[768,1536]{1,0:T(8,128)(2,1)}, bf16[768,256]{1,0:T(8,128)(2,1)}, bf16[768,256]{1,0:T(8,128)(2,1)}, bf16[768,1536]{1,0:T(8,128)(2,1)}, bf16[768,7...) custom-call(bf16[1024,1536]{1,0:T(8,128)(2,1)} %bitcast.46, ...), custom_call_target="tpu_custom_call" | custom-call | tf_op jit(solution)/shard_map/grads/pallas_call | solution.py:1051
  504.5 0.0 copy-start.1
  504.6 1.5 fusion.2
  506.0 1.9 bitcast_convert_fusion.6
  508.0 1.9 bitcast_convert_fusion.5
  509.9 0.0 copy-done.1
  509.9 0.0 copy-start.4
  509.9 2.8 bitcast_convert_fusion.1
  512.7 0.0 copy-done.4
  512.7 0.0 copy-start.3
  512.7 1.6 bitcast_convert_fusion.4
  514.3 0.1 copy-done.3
  514.4 0.0 copy-start.2
  514.4 1.6 bitcast_convert_fusion.3
  516.0 0.1 copy-done.2
  516.1 0.0 copy-start
  516.1 1.7 bitcast_convert_fusion.2
  517.8 0.8 copy-done
  518.6 0.0 copy-start.6
  518.6 0.0 copy-start.5
  518.6 2.8 bitcast_convert_fusion
  521.4 0.0 copy-done.6
  521.4 0.8 copy.31
  522.2 0.0 copy-done.5
  522.3 0.8 copy.32
  (4 shorter events, 0.0 us)
Async XLA Ops:
  504.5 5.4 %copy-start.1 = (bf16[768,1536]{1,0:T(8,128)(2,1)S(1)}, bf16[768,1536]{1,0:T(8,128)(2,1)}, u32[]{:S(2)}) copy-start(bf16[768,1536]{1,0:T(8,128)(2,1)} %get-tuple-element.43) | copy-start | bytes 7077892
  509.9 2.8 copy-start.4
  512.7 1.7 copy-start.3
  514.4 1.7 copy-start.2
  516.1 2.5 copy-start
  518.6 2.8 copy-start.6
  518.6 3.6 copy-start.5

commit v3 on v2

--- a/solution.py
+++ b/solution.py
@@ -2,6 +2,7 @@
 
 import jax
 import jax.numpy as jnp
+import numpy as np
 from jax import lax
 from jax.experimental import pallas as pl
 from jax.experimental.pallas import tpu as pltpu
@@ -22,6 +23,7 @@
 WIDTH = 1536
 HALF = 768
 EXPERTS = 32
+PLANE = 16
 SLOTS = 16
 ROWS = EXPERTS * SLOTS
 HIDDEN = 768
@@ -58,6 +60,71 @@
 
 def rotate(head, cos, sin):
     return head * cos + pltpu.roll(head, HEAD // 2, 1) * sin
+
+
+(ATTEND, NORM, TWIN, HIDE, GIVE, FAR, JOIN, GRAD, GRAD_TWIN, BACK, FAR_BACK, MID, ATTEND_BACK, CLOSE, LOAD, REST) = range(16)
+
+FIRST_PLAN = (
+    (ATTEND, 0),
+    (ATTEND, 1),
+    (NORM, 0),
+    (TWIN, 0),
+    (NORM, 1),
+    (TWIN, 1),
+    (HIDE, 0),
+    (GIVE, 0),
+    (HIDE, 1),
+    (GIVE, 1),
+    (FAR, 0),
+    (JOIN, 0),
+    (FAR, 1),
+    (JOIN, 1),
+    (GRAD, 0),
+    (GRAD_TWIN, 0),
+    (GRAD, 1),
+    (GRAD_TWIN, 1),
+    (BACK, 0),
+    (BACK, 1),
+    (FAR_BACK, 0),
+    (MID, 0),
+    (FAR_BACK, 1),
+    (MID, 1),
+    (ATTEND_BACK, 0),
+    (ATTEND_BACK, 1),
+    (CLOSE, 0),
+    (CLOSE, 1),
+)
+SECOND_PLAN = (
+    (GRAD, 0),
+    (GRAD, 1),
+    (LOAD, 0),
+    (ATTEND, 0),
+    (ATTEND, 1),
+    (NORM, 0),
+    (TWIN, 0),
+    (NORM, 1),
+    (TWIN, 1),
+    (GRAD_TWIN, 0),
+    (GRAD_TWIN, 1),
+    (HIDE, 0),
+    (BACK, 0),
+    (HIDE, 1),
+    (BACK, 1),
+    (FAR_BACK, 0),
+    (MID, 0),
+    (FAR_BACK, 1),
+    (MID, 1),
+    (ATTEND_BACK, 0),
+    (ATTEND_BACK, 1),
+    (CLOSE, 0),
+    (CLOSE, 1),
+    (GIVE, 0),
+    (GIVE, 1),
+    (FAR, 0),
+    (JOIN, 0),
+    (FAR, 1),
+    (JOIN, 1),
+)
 
 
 def section_kernel(
@@ -70,13 +137,9 @@
     wg_in,
     wu_in,
     wd_in,
-    gain_one,
-    gain_two,
-    ids_t,
-    logits_t,
-    cos_t,
-    sin_t,
-    mask_t,
+    side_in,
+    meta_in,
+    freq_in,
     acts_out,
     ingrad_out,
     gains_out,
@@ -105,6 +168,8 @@
     sel,
     cg_hi,
     cg_lo,
+    n2pair,
+    gpair,
     dsend,
     bsend,
     n2recv,
@@ -114,8 +179,9 @@
     gs,
     us,
     hid,
+    far_send,
+    far_recv,
     acts_s,
-    g_buf,
     dh_s,
     da_pair,
     dqkv_all,
@@ -123,6 +189,12 @@
     dn1_recv,
     ingrad_s,
     gains_acc,
+    side,
+    meta,
+    gains,
+    cos_t,
+    sin_t,
+    mask_t,
     lw_sem,
     ws_sem,
     wr_sem,
@@ -130,6 +202,8 @@
     ar_sem,
     ps_sem,
     pr_sem,
+    ts_sem,
+    tr_sem,
     xs_sem,
     xr_sem,
     gs_sem,
@@ -140,24 +214,37 @@
     sec = lax.axis_index("section")
     f = lax.axis_index("fsdp")
     e = lax.axis_index("expert")
+    y, x, z = e // 8, lax.rem(e // 4, 2), lax.rem(e, 4)
+    q = y * 4 + z
+    away = 1 - x
     other = 1 - f
     own_rows = aligned(f * SEQ, SEQ, 16)
     other_rows = aligned(other * SEQ, SEQ, 16)
     own_half = aligned(f * HALF, HALF, 128)
     other_half = aligned(other * HALF, HALF, 128)
-    my_slots = aligned(e * SLOTS, SLOTS, 16)
     partner = {"fsdp": other}
+    twin_place = y * 8 + away * 4 + z
+    twin = {"expert": twin_place}
     first, second = sec == 0, sec == 1
 
+    def in_plane(d):
+        at = lax.rem(q + d, PLANE)
+        return at, {"expert": (at // 4) * 8 + x * 4 + lax.rem(at, 4)}
+
     barrier = pltpu.get_barrier_semaphore()
 
-    @pl.loop(1, EXPERTS)
+    @pl.loop(1, PLANE)
     def _(d):
-        pl.semaphore_signal(
-            barrier, inc=1, device_id={"expert": lax.rem(e + d, EXPERTS)}, device_id_type=MESH
-        )
-
-    for place in ({"fsdp": other}, {"section": 1 - sec}, {"section": 1 - sec, "fsdp": other}):
+        pl.semaphore_signal(barrier, inc=1, device_id=in_plane(d)[1], device_id_type=MESH)
+
+    others = (
+        twin,
+        partner,
+        {"section": 1 - sec},
+        {"section": 1 - sec, "fsdp": other},
+        {"section": 1 - sec, "expert": twin_place},
+    )
+    for place in others:
         pl.semaphore_signal(barrier, inc=1, device_id=place, device_id_type=MESH)
 
     local = [
@@ -173,169 +260,192 @@
     for copy in local:
         copy.start()
     x_local = pltpu.make_async_copy(x_in, xpair.at[:, own_rows], lw_sem.at[7])
-    ct_local = pltpu.make_async_copy(ct_in, g_buf, lw_sem.at[8])
+    ct_local = pltpu.make_async_copy(ct_in, gpair.at[:, x], lw_sem.at[8])
     pl.when(first)(x_local.start)
     pl.when(second)(ct_local.start)
 
-    def remote(src, dst, i):
+    def remote(src, dst, send, recv, place):
         return pltpu.make_async_remote_copy(
             src_ref=src,
             dst_ref=dst,
-            send_sem=ws_sem.at[i],
-            recv_sem=wr_sem.at[i],
-            device_id=partner,
+            send_sem=send,
+            recv_sem=recv,
+            device_id=place,
             device_id_type=MESH,
         )
 
+    def wait_for(ref, sem):
+        pltpu.make_async_copy(ref, ref, sem).wait()
+
+    def weight(src, dst, i):
+        return remote(src, dst, ws_sem.at[i], wr_sem.at[i], partner)
+
     w_attn = [
-        remote(wq_in.at[:, other_half], wqkv.at[own_half, pl.ds(0, HALF)], 0),
-        remote(
+        weight(wq_in.at[:, other_half], wqkv.at[own_half, pl.ds(0, HALF)], 0),
+        weight(
             wk_in.at[:, aligned(other * HEAD, HEAD, 128)],
             wqkv.at[own_half, pl.ds(HALF, HEAD)],
             1,
         ),
-        remote(
+        weight(
             wv_in.at[:, aligned(other * HEAD, HEAD, 128)],
             wqkv.at[own_half, pl.ds(HALF + HEAD, HEAD)],
             2,
         ),
     ]
     w_moe = [
-        remote(wg_in, wg.at[own_half], 3),
-        remote(wu_in, wu.at[own_half], 4),
-        remote(wd_in, wd.at[aligned(f * (HIDDEN // 2), HIDDEN // 2, 16)], 5),
+        weight(wg_in, wg.at[own_half], 3),
+        weight(wu_in, wu.at[own_half], 4),
+        weight(wd_in, wd.at[aligned(f * (HIDDEN // 2), HIDDEN // 2, 16)], 5),
     ]
-    x_remote = remote(x_in, xpair.at[:, own_rows], 6)
-
-    pl.semaphore_wait(barrier, EXPERTS - 1 + 3)
+
+    def x_copy(m):
+        return weight(x_in.at[m], xpair.at[m, own_rows], 6 + m)
+
+    def ct_copy(m):
+        return remote(ct_in.at[m], gpair.at[m, x], ws_sem.at[10 + m], gr_sem.at[x, m], twin)
+
+    side[f] = side_in[...]
+    meta[x] = meta_in[...]
+    side_copy = weight(side.at[f], side.at[f], 8)
+    meta_copy = remote(meta.at[x], meta.at[x], ws_sem.at[9], wr_sem.at[9], twin)
+    gains_acc[...] = jnp.zeros_like(gains_acc)
+
+    pl.semaphore_wait(barrier, PLANE - 1 + len(others))
+    side_copy.start()
+    meta_copy.start()
 
     @pl.when(first)
     def _():
-        x_remote.start()
-        for copy in w_attn + w_moe:
+        x_copy(0).start()
+        for copy in w_attn:
             copy.start()
-
-    gains_acc[...] = jnp.zeros_like(gains_acc)
-
-    @pl.loop(0, MB)
-    def _(m):
-        ids = ids_t[m]
-        logits = logits_t[m]
+        x_copy(1).start()
+
+    meta_copy.wait_recv()
+    earlier = lax.broadcasted_iota(jnp.int32, (SEQ, SEQ), 0) < lax.broadcasted_iota(
+        jnp.int32, (SEQ, SEQ), 1
+    )
+    earlier = jnp.where(earlier, 1.0, 0.0).astype(BF)
+
+    @pl.loop(0, 2 * MB)
+    def _(i):
+        m, source = lax.rem(i, MB), i // MB
+        rows = meta[source, m]
+        ids, logits = rows[:4], rows[4:]
         raised = jnp.exp(logits - jnp.max(logits, axis=0, keepdims=True))
         gates = raised / jnp.sum(raised, axis=0, keepdims=True)
-        expert = lax.broadcasted_iota(jnp.int32, (EXPERTS, SEQ), 0)
-        named = jnp.zeros((EXPERTS, SEQ), F32)
-        weight = jnp.zeros((EXPERTS, SEQ), F32)
+        place = lax.broadcasted_iota(jnp.int32, (PLANE, SEQ), 0)
+        expert = ((place // 4) * 8 + x * 4 + lax.rem(place, 4)).astype(F32)
+        named = jnp.zeros((PLANE, SEQ), F32)
+        weights = jnp.zeros((PLANE, SEQ), F32)
         for k in range(4):
             hit = expert == ids[k : k + 1, :]
             named = jnp.where(hit, 1.0, named)
-            weight = jnp.where(hit, gates[k : k + 1, :], weight)
-        earlier = lax.broadcasted_iota(jnp.int32, (SEQ, SEQ), 0) < lax.broadcasted_iota(
-            jnp.int32, (SEQ, SEQ), 1
+            weights = jnp.where(hit, gates[k : k + 1, :], weights)
+        slot = dot(named.astype(BF), earlier)
+        slot = jnp.where(named > 0.0, slot, -1.0)
+        shape = (PLANE, SLOTS, SEQ)
+        count = lax.broadcasted_iota(jnp.int32, shape, 1).astype(F32)
+        chosen = jnp.where(jnp.broadcast_to(slot[:, None, :], shape) == count, 1.0, 0.0)
+        scaled = chosen * jnp.broadcast_to(weights[:, None, :], shape)
+        scaled = scaled.reshape(PLANE * SLOTS, SEQ)
+        high = scaled.astype(BF)
+        sel[m, source] = chosen.reshape(PLANE * SLOTS, SEQ).astype(BF)
+        cg_hi[m, source] = high
+        cg_lo[m, source] = (scaled - high.astype(F32)).astype(BF)
+
+    side_copy.wait_recv()
+    gains[:, pl.ds(0, HALF)] = side[0, 0:2]
+    gains[:, pl.ds(HALF, HALF)] = side[1, 0:2]
+    row = lax.broadcasted_iota(jnp.int32, (SEQ, SEQ), 0)
+    col = lax.broadcasted_iota(jnp.int32, (SEQ, SEQ), 1)
+    lane = lax.broadcasted_iota(jnp.int32, (SEQ, HEAD), 1)
+    turn = jnp.where(lane < HEAD // 2, -1.0, 1.0)
+    for m in range(MB):
+        for s in range(2):
+            across = jnp.broadcast_to(side[s, 2 + m : 3 + m, :SEQ], (SEQ, SEQ))
+            down = dot_nt(jnp.where(row == col, 1.0, 0.0).astype(BF), across.astype(BF))
+            same = jnp.where(down == across, 1.0, 0.0)
+            mask_t[m, s] = jnp.where(col <= row, same, 0.0)
+            places = jnp.sum(jnp.where(col < row, same, 0.0), axis=1, keepdims=True)
+            angles = places * freq_in[...]
+            cos_t[m, pl.ds(s * SEQ, SEQ)] = jnp.cos(angles)
+            sin_t[m, pl.ds(s * SEQ, SEQ)] = jnp.sin(angles) * turn
+
+    def exchange_half(kind, m, src, dst, source):
+        @pl.loop(1, PLANE)
+        def _(d):
+            at, place = in_plane(d)
+            remote(
+                src.at[m, at, source],
+                dst.at[m, q, source],
+                as_sem.at[kind, m],
+                ar_sem.at[kind, m],
+                place,
+            ).start()
+
+        dst[m, q, source] = src[m, q, source]
+
+    def exchange(kind, m, src, dst):
+        @pl.loop(1, PLANE)
+        def _(d):
+            at, place = in_plane(d)
+            remote(
+                src.at[m, at], dst.at[m, q], as_sem.at[kind, m], ar_sem.at[kind, m], place
+            ).start()
+
+        dst[m, q] = src[m, q]
+
+    def received(kind, m, dst):
+        wait_for(dst.at[m, pl.ds(0, PLANE - 1)], ar_sem.at[kind, m])
+
+    def sent(kind, m, src):
+        wait_for(src.at[m, pl.ds(0, PLANE - 1)], as_sem.at[kind, m])
+
+    def to_partner(kind, m, src, dst):
+        return remote(src, dst, ps_sem.at[kind, m], pr_sem.at[kind, m], partner)
+
+    def to_twin(kind, m, src, dst):
+        return remote(src, dst, ts_sem.at[kind, m], tr_sem.at[kind, m], twin)
+
+    def n2_copy(m):
+        return to_twin(0, m, n2pair.at[m, x], n2pair.at[m, x])
+
+    def far_copy(kind, m):
+        return to_twin(kind, m, far_send.at[kind - 1, m], far_recv.at[kind - 1, m])
+
+    def acts_copy(m, cross):
+        place = {"section": 1, "fsdp": other} if cross else {"section": 1}
+        return remote(
+            acts_s.at[m], xpair.at[m, own_rows], xs_sem.at[cross, m], xr_sem.at[f, m], place
         )
-        slot = dot(named.astype(BF), jnp.where(earlier, 1.0, 0.0).astype(BF))
-        slot = jnp.where(named > 0.0, slot, -1.0)
-        place = lax.broadcasted_iota(jnp.int32, (EXPERTS, SLOTS, SEQ), 1).astype(F32)
-        chosen = jnp.where(
-            jnp.broadcast_to(slot[:, None, :], (EXPERTS, SLOTS, SEQ)) == place, 1.0, 0.0
-        )
-        scaled = chosen * jnp.broadcast_to(weight[:, None, :], (EXPERTS, SLOTS, SEQ))
-        scaled = scaled.reshape(ROWS, SEQ)
-        high = scaled.astype(BF)
-        sel[m] = chosen.reshape(ROWS, SEQ).astype(BF)
-        cg_hi[m] = high
-        cg_lo[m] = (scaled - high.astype(F32)).astype(BF)
-
-    def exchange(kind, m, src, dst):
-        @pl.loop(1, EXPERTS)
-        def _(d):
-            p = lax.rem(e + d, EXPERTS)
-            pltpu.make_async_remote_copy(
-                src_ref=src.at[m, aligned(p * SLOTS, SLOTS, 16)],
-                dst_ref=dst.at[m, my_slots],
-                send_sem=as_sem.at[kind, m],
-                recv_sem=ar_sem.at[kind, m],
-                device_id={"expert": p},
-                device_id_type=MESH,
-            ).start()
-
-        dst[m, my_slots] = src[m, my_slots]
-
-    def received(kind, m, dst):
-        whole = dst.at[m, pl.ds(0, ROWS - SLOTS)]
-        pltpu.make_async_copy(whole, whole, ar_sem.at[kind, m]).wait()
-
-    def sent(kind, m, src):
-        whole = src.at[m, pl.ds(0, ROWS - SLOTS)]
-        pltpu.make_async_copy(whole, whole, as_sem.at[kind, m]).wait()
-
-    def to_partner(kind, m, src, dst):
-        return pltpu.make_async_remote_copy(
-            src_ref=src,
-            dst_ref=dst,
-            send_sem=ps_sem.at[kind, m],
-            recv_sem=pr_sem.at[kind, m],
-            device_id=partner,
-            device_id_type=MESH,
-        )
-
-    def acts_copy(m, cross):
-        return pltpu.make_async_remote_copy(
-            src_ref=acts_s.at[m],
-            dst_ref=xpair.at[m, own_rows],
-            send_sem=xs_sem.at[cross, m],
-            recv_sem=xr_sem.at[f, m],
-            device_id={"section": 1, "fsdp": other} if cross else {"section": 1},
-            device_id_type=MESH,
-        )
-
-    def acts_arrived(m):
-        for at, rows in ((f, own_rows), (other, other_rows)):
-            place = xpair.at[m, rows]
-            pltpu.make_async_copy(place, place, xr_sem.at[at, m]).wait()
-
-    def grad_copy(m):
-        return pltpu.make_async_remote_copy(
-            src_ref=ingrad_s.at[m],
-            dst_ref=g_buf.at[m],
-            send_sem=gs_sem.at[m],
-            recv_sem=gr_sem.at[m],
-            device_id={"section": 0},
-            device_id_type=MESH,
+
+    def grad_copy(m, cross):
+        place = {"section": 0, "expert": twin_place} if cross else {"section": 0}
+        return remote(
+            ingrad_s.at[m], gpair.at[m, x], gs_sem.at[cross, m], gr_sem.at[x, m], place
         )
 
     def out_copy(i, src, dst, m):
         return pltpu.make_async_copy(src, dst, out_sem.at[i, m])
 
-    def send_dy(m):
-        gate = jnp.sum(cg_hi[m].astype(F32) + cg_lo[m].astype(F32), axis=1, keepdims=True)
-
+    def flat(ref, m):
+        return ref[m].reshape(ROWS, WIDTH)
+
+    def spread(m, source, rows, dst, scale=None):
         @pl.loop(0, WIDTH // 512)
         def _(j):
             cols = aligned(j * 512, 512, 128)
-            bsend[m, :, cols] = (dot(sel[m], g_buf[m, :, cols]) * gate).astype(BF)
-
-        exchange(2, m, bsend, dyrecv)
-
-    @pl.when(second)
-    def _():
-        ct_local.wait()
+            block = dot(sel[m, source], rows[m, source, :, cols])
+            if scale is not None:
+                block = block * scale
+            dst[m, :, source, :, cols] = block.astype(BF).reshape(PLANE, SLOTS, 512)
+
+    def load_step(m):
         pl.semaphore_wait(go_sem, 1)
         for copy in w_attn:
             copy.start()
-        pl.loop(0, MB)(send_dy)
-        for copy in w_moe:
-            copy.start()
-
-    @pl.when(first)
-    def _():
-        x_local.wait()
-        x_remote.wait_recv()
-
-    for copy in local[:4]:
-        copy.wait()
-    for copy in w_attn:
-        copy.wait_recv()
 
     def heads_of(ref, m, rows):
         return jnp.concatenate(
@@ -349,9 +459,35 @@
         raised = jnp.exp(scores - jnp.max(scores, axis=-1, keepdims=True))
         return raised / jnp.sum(raised, axis=-1, keepdims=True)
 
-    def attend(m):
+    def attend_step(m):
+        @pl.when(m == 0)
+        def _():
+            for copy in local[:4]:
+                copy.wait()
+            for copy in w_attn:
+                copy.wait_recv()
+            for copy in w_attn:
+                copy.wait_send()
+            for copy in w_moe:
+                copy.start()
+            pl.when(first)(x_local.wait)
+
+            @pl.when(second)
+            def _():
+                ct_copy(0).start()
+                ct_copy(1).start()
+
+        @pl.when(first)
+        def _():
+            x_copy(m).wait_recv()
+
+        @pl.when(second)
+        def _():
+            for at, rows in ((f, own_rows), (other, other_rows)):
+                wait_for(xpair.at[m, rows], xr_sem.at[at, m])
+
         rows = xpair[m].astype(F32)
-        n1s[m] = (rows * inverse_rms(rows) * gain_one[...]).astype(BF)
+        n1s[m] = (rows * inverse_rms(rows) * gains[0:1]).astype(BF)
         cos, sin = cos_t[m], sin_t[m]
         for j in range(4):
             block = dot(n1s[m], wqkv[:, pl.ds(j * 256, 256)])
@@ -383,93 +519,125 @@
 
         to_partner(0, m, part_send.at[m], part_recv.at[m]).start()
 
-    def dispatch(m):
+    def norm_step(m):
         to_partner(0, m, part_send.at[m], part_recv.at[m]).wait_recv()
         rows = xpair[m, own_rows].astype(F32) + (hid_one[m] + part_recv[m].astype(F32))
         hid_one[m] = rows
-        n2 = (rows * inverse_rms(rows) * gain_two[...]).astype(BF)
-        dsend[m] = dot(sel[m], n2).astype(BF)
-        exchange(0, m, dsend, n2recv)
-
-    def forward(m):
-        pl.when(second)(lambda: acts_arrived(m))
-        attend(m)
-        dispatch(m)
-
-    pl.loop(0, MB)(forward)
-
-    for copy in local[4:]:
-        copy.wait()
-    for copy in w_moe:
-        copy.wait_recv()
-
-    @pl.when(first)
-    def _():
-        for copy in w_attn + w_moe:
-            copy.wait_send()
-        pl.semaphore_signal(go_sem, inc=1, device_id={"section": 1}, device_id_type=MESH)
-
-    def experts(m):
+        n2pair[m, x] = (rows * inverse_rms(rows) * gains[1:2]).astype(BF)
+        n2_copy(m).start()
+        spread(m, x, n2pair, dsend)
+        exchange_half(0, m, dsend, n2recv, x)
+
+    def twin_step(m):
+        n2_copy(m).wait_recv()
+        spread(m, away, n2pair, dsend)
+        exchange_half(0, m, dsend, n2recv, away)
+
+    def hide_step(m):
+        @pl.when(m == 0)
+        def _():
+            for copy in local[4:6]:
+                copy.wait()
+            for copy in w_moe[:2]:
+                copy.wait_recv()
+
         received(0, m, n2recv)
         out_copy(0, n2recv.at[m], n2rows_out.at[m], m).start()
 
         @pl.loop(0, HIDDEN // 256)
         def _(j):
             cols = aligned(j * 256, 256, 128)
-            gate = dot(n2recv[m], wg[:, cols])
-            up = dot(n2recv[m], wu[:, cols])
+            rows = flat(n2recv, m)
+            gate = dot(rows, wg[:, cols])
+            up = dot(rows, wu[:, cols])
             bend = jnp.tanh(GELU_C * (gate + GELU_A * gate * gate * gate))
             gs[m, :, cols] = gate.astype(BF)
             us[m, :, cols] = up.astype(BF)
             hid[m, :, cols] = (0.5 * gate * (1.0 + bend) * up).astype(BF)
 
         out_copy(1, hid.at[m], hid_out.at[m], m).start()
-        pl.when(second)(lambda: sent(2, m, bsend))
+
+        @pl.when(m == 0)
+        def _():
+            local[6].wait()
+            w_moe[2].wait_recv()
+            for copy in w_moe:
+                copy.wait_send()
+
+            @pl.when(first)
+            def _():
+                pl.semaphore_signal(go_sem, inc=1, device_id={"section": 1}, device_id_type=MESH)
+
+    def give_step(m):
+        pl.when(second)(lambda: sent(3, m, bsend))
 
         @pl.loop(0, WIDTH // 512)
         def _(j):
             cols = aligned(j * 512, 512, 128)
-            bsend[m, :, cols] = dot(hid[m], wd[:, cols]).astype(BF)
+            block = dot(hid[m], wd[:, cols]).astype(BF)
+            bsend[m, :, :, :, cols] = block.reshape(PLANE, 2, SLOTS, 512)
 
         exchange(1, m, bsend, yrecv)
 
-    pl.loop(0, MB)(experts)
-
-    def combine(m):
+    def weighed(m, source, cols):
+        block = yrecv[m, :, source, :, cols].reshape(PLANE * SLOTS, 512)
+        return dot_tn(cg_hi[m, source], block) + dot_tn(cg_lo[m, source], block)
+
+    def far_step(m):
         received(1, m, yrecv)
 
         @pl.loop(0, WIDTH // 512)
         def _(j):
             cols = aligned(j * 512, 512, 128)
-            block = yrecv[m, :, cols]
-            mixed = dot_tn(cg_hi[m], block) + dot_tn(cg_lo[m], block)
-            acts_s[m, :, cols] = (hid_one[m, :, cols] + mixed).astype(BF)
-
-        out_copy(2, acts_s.at[m], acts_out.at[m], m).start()
-
-    @pl.when(first)
-    def _():
-        @pl.loop(0, MB)
-        def _(m):
-            combine(m)
+            far_send[0, m, :, cols] = weighed(m, away, cols).astype(BF)
+
+        far_copy(1, m).start()
+
+        @pl.loop(0, WIDTH // 512)
+        def _(j):
+            cols = aligned(j * 512, 512, 128)
+            part_own[m, :, cols] = hid_one[m, :, cols] + weighed(m, x, cols)
+
+    def join_step(m):
+        far_copy(1, m).wait_recv()
+        acts_s[m] = (part_own[m] + far_recv[0, m].astype(F32)).astype(BF)
+
+        @pl.when(first)
+        def _():
             for cross in (0, 1):
                 acts_copy(m, cross).start()
 
-        @pl.loop(0, MB)
-        def _(m):
+        out_copy(2, acts_s.at[m], acts_out.at[m], m).start()
+
+    def dy_half(m, source):
+        gate = cg_hi[m, source].astype(F32) + cg_lo[m, source].astype(F32)
+        spread(m, source, gpair, bsend, jnp.sum(gate, axis=1, keepdims=True))
+        exchange_half(2, m, bsend, dyrecv, source)
+
+    def grad_step(m):
+        @pl.when(first)
+        def _():
             sent(1, m, bsend)
-            place = g_buf.at[m]
-            pltpu.make_async_copy(place, place, gr_sem.at[m]).wait()
-            send_dy(m)
-
-    def experts_back(m):
+            wait_for(gpair.at[m, x], gr_sem.at[x, m])
+
+        @pl.when(jnp.logical_and(second, m == 0))
+        def _():
+            ct_local.wait()
+
+        dy_half(m, x)
+
+    def grad_twin_step(m):
+        wait_for(gpair.at[m, away], gr_sem.at[away, m])
+        dy_half(m, away)
+
+    def back_step(m):
         received(2, m, dyrecv)
         out_copy(3, dyrecv.at[m], dyrows_out.at[m], m).start()
 
         @pl.loop(0, HIDDEN // 256)
         def _(j):
             cols = aligned(j * 256, 256, 128)
-            dhid = dot_nt(dyrecv[m], wd[cols, :])
+            dhid = dot_nt(flat(dyrecv, m), wd[cols, :])
             gate = gs[m, :, cols].astype(F32)
             up = us[m, :, cols].astype(F32)
             square = gate * gate
@@ -483,37 +651,58 @@
 
         out_copy(4, gs.at[m], dgate_out.at[m], m).start()
         out_copy(5, us.at[m], dup_out.at[m], m).start()
-        pl.when(first)(lambda: sent(2, m, bsend))
-        pl.when(second)(lambda: sent(1, m, bsend))
+        sent(2, m, bsend)
 
         @pl.loop(0, WIDTH // 512)
         def _(j):
             cols = aligned(j * 512, 512, 128)
             block = dot_nt(gs[m], wg[cols, :]) + dot_nt(us[m], wu[cols, :])
-            bsend[m, :, cols] = block.astype(BF)
+            bsend[m, :, :, :, cols] = block.astype(BF).reshape(PLANE, 2, SLOTS, 512)
 
         exchange(3, m, bsend, dn2recv)
 
-    pl.loop(0, MB)(experts_back)
-
-    def attend_back(m):
+    def gathered(m, source, cols):
+        return dot_tn(
+            sel[m, source], dn2recv[m, :, source, :, cols].reshape(PLANE * SLOTS, 512)
+        )
+
+    def far_back_step(m):
         received(3, m, dn2recv)
-        rows = hid_one[m]
-        inverse = inverse_rms(rows)
 
         @pl.loop(0, WIDTH // 512)
         def _(j):
             cols = aligned(j * 512, 512, 128)
-            dh_s[m, :, cols] = dot_tn(sel[m], dn2recv[m, :, cols])
-
-        grad = dh_s[m]
+            far_send[1, m, :, cols] = gathered(m, away, cols).astype(BF)
+
+        far_copy(2, m).start()
+
+        @pl.loop(0, WIDTH // 512)
+        def _(j):
+            cols = aligned(j * 512, 512, 128)
+            dh_s[m, :, cols] = gathered(m, x, cols)
+
+    def mid_step(m):
+        far_copy(2, m).wait_recv()
+        rows = hid_one[m]
+        inverse = inverse_rms(rows)
+        grad = dh_s[m] + far_recv[1, m].astype(F32)
         gains_acc[1:2] += jnp.sum(grad * rows * inverse, axis=0, keepdims=True)
-        total = g_buf[m].astype(F32) + rms_back(rows, inverse, gain_two[...], grad)
+        total = gpair[m, x].astype(F32) + rms_back(rows, inverse, gains[1:2], grad)
         dh_s[m] = total
         da_pair[m, own_rows] = total.astype(BF)
-        da_copy = to_partner(1, m, da_pair.at[m, own_rows], da_pair.at[m, own_rows])
-        da_copy.start()
-        da_copy.wait_recv()
+        da_copy(m).start()
+
+    def da_copy(m):
+        return to_partner(1, m, da_pair.at[m, own_rows], da_pair.at[m, own_rows])
+
+    def dqkv_copy(m):
+        return to_partner(3, m, dqkv_all.at[m, f], dqkv_all.at[m, f])
+
+    def dn1_copy(m):
+        return to_partner(2, m, dn1_send.at[m], dn1_recv.at[m])
+
+    def attend_back_step(m):
+        da_copy(m).wait_recv()
         out_copy(6, da_pair.at[m], da_out.at[m], m).start()
 
         @pl.loop(0, 2)
@@ -541,65 +730,96 @@
             dqkv_all[m, f, at, pl.ds(HALF, HEAD)] = dkeys.astype(BF)
             dqkv_all[m, f, at, pl.ds(HALF + HEAD, HEAD)] = dvalues.astype(BF)
 
-        dqkv_copy = to_partner(3, m, dqkv_all.at[m, f], dqkv_all.at[m, f])
-        dqkv_copy.start()
-
         @pl.loop(0, WIDTH // 512)
         def _(j):
             cols = aligned(j * 512, 512, 128)
             block = dot_nt(dqkv_all[m, f], wqkv[cols, :])
             top, low = block[:SEQ], block[SEQ:]
             mine = f == 0
-            part_own[:, cols] = jnp.where(mine, top, low)
+            part_own[m, :, cols] = jnp.where(mine, top, low)
             dn1_send[m, :, cols] = jnp.where(mine, low, top).astype(BF)
 
-        dn1_copy = to_partner(2, m, dn1_send.at[m], dn1_recv.at[m])
-        dn1_copy.start()
-        dn1_copy.wait_recv()
-        grad = part_own[...] + dn1_recv[m].astype(F32)
+        dn1_copy(m).start()
+        dqkv_copy(m).start()
+
+    def close_step(m):
+        dn1_copy(m).wait_recv()
+        grad = part_own[m] + dn1_recv[m].astype(F32)
         rows = xpair[m, own_rows].astype(F32)
         inverse = inverse_rms(rows)
         gains_acc[0:1] += jnp.sum(grad * rows * inverse, axis=0, keepdims=True)
-        ingrad_s[m] = (dh_s[m] + rms_back(rows, inverse, gain_one[...], grad)).astype(BF)
+        ingrad_s[m] = (dh_s[m] + rms_back(rows, inverse, gains[0:1], grad)).astype(BF)
+
+        @pl.when(second)
+        def _():
+            for cross in (0, 1):
+                grad_copy(m, cross).start()
+
         out_copy(7, ingrad_s.at[m], ingrad_out.at[m], m).start()
-        pl.when(second)(grad_copy(m).start)
-
-    pl.loop(0, MB)(attend_back)
-
-    pl.when(second)(lambda: pl.loop(0, MB)(combine))
+
+    steps = {
+        ATTEND: attend_step,
+        NORM: norm_step,
+        TWIN: twin_step,
+        HIDE: hide_step,
+        GIVE: give_step,
+        FAR: far_step,
+        JOIN: join_step,
+        GRAD: grad_step,
+        GRAD_TWIN: grad_twin_step,
+        BACK: back_step,
+        FAR_BACK: far_back_step,
+        MID: mid_step,
+        ATTEND_BACK: attend_back_step,
+        CLOSE: close_step,
+        LOAD: load_step,
+    }
+    length = max(len(FIRST_PLAN), len(SECOND_PLAN))
+    plans = [plan + ((REST, 0),) * (length - len(plan)) for plan in (FIRST_PLAN, SECOND_PLAN)]
+
+    @pl.loop(0, length)
+    def _(i):
+        code = jnp.int32(REST * MB)
+        for at, ((step_a, m_a), (step_b, m_b)) in enumerate(zip(*plans)):
+            here = jnp.where(first, step_a * MB + m_a, step_b * MB + m_b)
+            code = jnp.where(i == at, here, code)
+        m = lax.rem(code, MB)
+        for step, work in steps.items():
+            pl.when(code // MB == step)(functools.partial(work, m))
+
+    gains_out[...] = gains_acc[...]
 
     @pl.loop(0, MB)
     def _(m):
-        to_partner(3, m, dqkv_all.at[m, f], dqkv_all.at[m, f]).wait_recv()
+        dqkv_copy(m).wait_recv()
         out_copy(8, n1s.at[m, :, own_half], n1_out.at[m], m).start()
         out_copy(9, dqkv_all.at[m], dqkv_out.at[m], m).start()
         out_copy(10, att.at[m], att_out.at[m], m).start()
         sent(0, m, dsend)
-        sent(3, m, bsend)
+        pl.when(first)(lambda: sent(3, m, bsend))
+        pl.when(second)(lambda: sent(1, m, bsend))
         to_partner(0, m, part_send.at[m], part_recv.at[m]).wait_send()
-        to_partner(1, m, da_pair.at[m, own_rows], da_pair.at[m, own_rows]).wait_send()
-        to_partner(2, m, dn1_send.at[m], dn1_recv.at[m]).wait_send()
-        to_partner(3, m, dqkv_all.at[m, f], dqkv_all.at[m, f]).wait_send()
-
-    gains_out[...] = gains_acc[...]
-
-    @pl.when(first)
-    def _():
-        x_remote.wait_send()
-
-        @pl.loop(0, MB)
-        def _(m):
+        da_copy(m).wait_send()
+        dn1_copy(m).wait_send()
+        dqkv_copy(m).wait_send()
+        n2_copy(m).wait_send()
+        far_copy(1, m).wait_send()
+        far_copy(2, m).wait_send()
+
+        @pl.when(first)
+        def _():
+            x_copy(m).wait_send()
             for cross in (0, 1):
                 acts_copy(m, cross).wait_send()
 
-    @pl.when(second)
-    def _():
-        for copy in w_attn + w_moe:
-            copy.wait_send()
-
-        @pl.loop(0, MB)
-        def _(m):
-            grad_copy(m).wait_send()
+        @pl.when(second)
+        def _():
+            ct_copy(m).wait_send()
+            for cross in (0, 1):
+                grad_copy(m, cross).wait_send()
+
+    side_copy.wait_send()
+    meta_copy.wait_send()
 
     @pl.loop(0, MB)
     def _(m):
@@ -628,6 +848,7 @@
     vmem = pl.BlockSpec(memory_space=pltpu.VMEM)
     anywhere = pl.BlockSpec(memory_space=pl.ANY)
     dma = pltpu.SemaphoreType.DMA
+    blocks = (MB, PLANE, 2, SLOTS, WIDTH)
     return pl.pallas_call(
         section_kernel,
         name="sections",
@@ -635,8 +856,8 @@
             out(MB, SEQ, WIDTH),
             out(MB, SEQ, WIDTH),
             out(8, WIDTH, dtype=F32),
-            out(MB, ROWS, WIDTH),
-            out(MB, ROWS, WIDTH),
+            out(*blocks),
+            out(*blocks),
             out(MB, ROWS, HIDDEN),
             out(MB, ROWS, HIDDEN),
             out(MB, ROWS, HIDDEN),
@@ -645,7 +866,7 @@
             out(MB, 2 * SEQ, HALF),
             out(MB, 2 * SEQ, WIDTH),
         ),
-        in_specs=[anywhere] * 9 + [vmem] * 7,
+        in_specs=[anywhere] * 9 + [vmem] * 3,
         out_specs=[anywhere] * 2 + [vmem] + [anywhere] * 9,
         scratch_shapes=[
             pltpu.VMEM((WIDTH, QKV), BF),
@@ -658,22 +879,25 @@
             pltpu.VMEM((MB, 2 * SEQ, QKV), BF),
             pltpu.VMEM((MB, 2 * SEQ, HALF), BF),
             pltpu.VMEM((MB, SEQ, WIDTH), F32),
-            pltpu.VMEM((SEQ, WIDTH), F32),
+            pltpu.VMEM((MB, SEQ, WIDTH), F32),
             pltpu.VMEM((MB, SEQ, WIDTH), BF),
             pltpu.VMEM((MB, SEQ, WIDTH), BF),
-            pltpu.VMEM((MB, ROWS, SEQ), BF),
-            pltpu.VMEM((MB, ROWS, SEQ), BF),
-            pltpu.VMEM((MB, ROWS, SEQ), BF),
-            pltpu.VMEM((MB, ROWS, WIDTH), BF),
-            pltpu.VMEM((MB, ROWS, WIDTH), BF),
-            pltpu.VMEM((MB, ROWS, WIDTH), BF),
-            pltpu.VMEM((MB, ROWS, WIDTH), BF),
-            pltpu.VMEM((MB, ROWS, WIDTH), BF),
-            pltpu.VMEM((MB, ROWS, WIDTH), BF),
+            pltpu.VMEM((MB, 2, PLANE * SLOTS, SEQ), BF),
+            pltpu.VMEM((MB, 2, PLANE * SLOTS, SEQ), BF),
+            pltpu.VMEM((MB, 2, PLANE * SLOTS, SEQ), BF),
+            pltpu.VMEM((MB, 2, SEQ, WIDTH), BF),
+            pltpu.VMEM((MB, 2, SEQ, WIDTH), BF),
+            pltpu.VMEM(blocks, BF),
+            pltpu.VMEM(blocks, BF),
+            pltpu.VMEM(blocks, BF),
+            pltpu.VMEM(blocks, BF),
+            pltpu.VMEM(blocks, BF),
+            pltpu.VMEM(blocks, BF),
             pltpu.VMEM((MB, ROWS, HIDDEN), BF),
             pltpu.VMEM((MB, ROWS, HIDDEN), BF),
             pltpu.VMEM((MB, ROWS, HIDDEN), BF),
-            pltpu.VMEM((MB, SEQ, WIDTH), BF),
+            pltpu.VMEM((2, MB, SEQ, WIDTH), BF),
+            pltpu.VMEM((2, MB, SEQ, WIDTH), BF),
             pltpu.VMEM((MB, SEQ, WIDTH), BF),
             pltpu.VMEM((MB, SEQ, WIDTH), F32),
             pltpu.VMEM((MB, 2 * SEQ, WIDTH), BF),
@@ -682,17 +906,25 @@
             pltpu.VMEM((MB, SEQ, WIDTH), BF),
             pltpu.VMEM((MB, SEQ, WIDTH), BF),
             pltpu.VMEM((8, WIDTH), F32),
+            pltpu.VMEM((2, 8, HALF), F32),
+            pltpu.VMEM((2, MB, 8, SEQ), F32),
+            pltpu.VMEM((2, WIDTH), F32),
+            pltpu.VMEM((MB, 2 * SEQ, HEAD), F32),
+            pltpu.VMEM((MB, 2 * SEQ, HEAD), F32),
+            pltpu.VMEM((MB, 2, SEQ, SEQ), F32),
             dma((9,)),
-            dma((7,)),
-            dma((7,)),
+            dma((12,)),
+            dma((10,)),
             dma((4, MB)),
             dma((4, MB)),
             dma((4, MB)),
             dma((4, MB)),
+            dma((3, MB)),
+            dma((3, MB)),
             dma((2, MB)),
             dma((2, MB)),
-            dma((MB,)),
-            dma((MB,)),
+            dma((2, MB)),
+            dma((2, MB)),
             dma((11, MB)),
             pltpu.SemaphoreType.REGULAR,
         ],
@@ -1114,19 +1346,19 @@
     w_up,
     w_down,
 ):
-    pair_segments = jnp.swapaxes(lax.all_gather(segments, "fsdp"), 0, 1)
-    gains = lax.all_gather(jnp.stack([gain_attn[0], gain_moe[0]]), "fsdp", axis=1, tiled=True)
-    gains = gains.astype(F32)
-    same = pair_segments[..., :, None] == pair_segments[..., None, :]
-    row = lax.broadcasted_iota(jnp.int32, (SEQ, SEQ), 0)
-    col = lax.broadcasted_iota(jnp.int32, (SEQ, SEQ), 1)
-    places = jnp.sum((same & (col < row)).astype(F32), axis=-1)
-    frequency = ROPE_BASE ** (-(jnp.arange(HEAD // 2, dtype=F32) * 2.0 / HEAD))
-    angles = places[..., None] * frequency
-    cosine, sine = jnp.cos(angles), jnp.sin(angles)
-    cos_t = jnp.concatenate([cosine, cosine], axis=-1).reshape(MB, 2 * SEQ, HEAD)
-    sin_t = jnp.concatenate([-sine, sine], axis=-1).reshape(MB, 2 * SEQ, HEAD)
-    mask_t = (same & (col <= row)).astype(F32)
+    side = jnp.concatenate(
+        [
+            gain_attn.astype(F32),
+            gain_moe.astype(F32),
+            jnp.pad(segments.astype(F32), ((0, 0), (0, HALF - SEQ))),
+            jnp.zeros((4, HALF), F32),
+        ],
+        axis=0,
+    )
+    meta = jnp.concatenate([expert_ids[0].astype(F32), gate_logits[0]], axis=-1)
+    meta = jnp.swapaxes(meta, 1, 2)
+    steps = np.arange(HEAD) % (HEAD // 2)
+    frequency = (ROPE_BASE ** (-steps * 2.0 / HEAD)).astype(np.float32)[None]
     (
         acts,
         in_grads,
@@ -1150,13 +1382,9 @@
         w_gate[0, 0],
         w_up[0, 0],
         w_down[0, 0],
-        gains[0:1],
-        gains[1:2],
-        jnp.swapaxes(expert_ids[0], 1, 2),
-        jnp.swapaxes(gate_logits[0], 1, 2),
-        cos_t,
-        sin_t,
-        mask_t,
+        side,
+        meta,
+        jnp.asarray(frequency),
     )
     gq, gk, gv, go, grad_gate, grad_up, grad_down, gains = reduce_grads(
         n2rows.reshape(MB * ROWS, WIDTH),

time: 524 us -> 481 us (0.918)
  Pallas kernels: 491 us -> 458 us
  blocking collectives: 8.79 us -> 0 us
    pallas_call x1, Pallas kernels: 401 us -> 370 us  [run_sections(): pl.pallas_call(section_kernel, name='sections', out_shape=(out(MB, SEQ, W...]
    all_gather x2 -> x0, blocking collectives: 8.79 us -> none  [the longest x1 4.46 us: local(): pair_segments = jnp.swapaxes(lax.all_gather(segments, 'fsdp'), 0, 1)]
where the time goes in v3:
time: 481 us; the launch traced here: 480 us
  Pallas kernels  458 us (95%)
  other arithmetic  16.5 us (3%)
    pallas_call x1, Pallas kernels, run_sections(): pl.pallas_call(section_kernel, name='sections', out_shape=(out(MB, SEQ, W...  370 us
    pallas_call x1, Pallas kernels, reduce_grads(): pl.pallas_call(grads_kernel, name='grads', out_shape=(out(HALF, WIDTH), o...  88.5 us

profile of v3, /device:TPU:0, one launch (start us, length us, event | category | flops | bytes accessed | tf_op | source)
XLA Modules:
  0.0 479.5 jit_solution(12585631426474730302)
XLA Ops:
  0.7 0.1 pad.10.clone
  0.7 0.7 convert_element_type.61
  1.4 0.7 convert_element_type.59
  2.1 0.7 convert_element_type.60
  2.8 0.7 convert_bitcast_fusion
  3.5 1.3 maximum_bitcast_fusion.meta_in
  4.8 0.7 fusion.side_in
  5.4 369.9 %sections.1 = (bf16[2,96,1536]{2,1,0:T(8,128)(2,1)}, bf16[2,96,1536]{2,1,0:T(8,128)(2,1)}, f32[8,1536]{1,0:T(8,128)}, bf16[2,16,2,16,1536]{4,3,2,1,0:T(8,128)(2,...) custom-call(bf16[2,96,1536]{2,1,0:T(8,128)(2,1)} %x_in.1, ...), custom_call_target="tpu_custom_call" | custom-call | tf_op jit(solution)/shard_map/sections/pallas_call | solution.py:852
  375.3 88.5 %grads.1 = (bf16[768,1536]{1,0:T(8,128)(2,1)}, bf16[768,256]{1,0:T(8,128)(2,1)}, bf16[768,256]{1,0:T(8,128)(2,1)}, bf16[768,1536]{1,0:T(8,128)(2,1)}, bf16[768,7...) custom-call(bf16[1024,1536]{1,0:T(8,128)(2,1)} %bitcast.43, ...), custom_call_target="tpu_custom_call" | custom-call | tf_op jit(solution)/shard_map/grads/pallas_call | solution.py:1283
  463.8 0.0 copy-start.4
  463.8 1.4 fusion.2
  465.2 0.0 copy-start.1
  465.2 2.5 bitcast_convert_fusion.5
  467.8 0.0 copy-start
  467.8 0.0 copy-done.4
  467.8 1.7 bitcast_convert_fusion.2
  469.5 0.0 copy-done.1
  469.5 0.8 copy-done
  470.3 0.0 copy-start.2
  470.3 0.0 copy-start.3
  470.3 5.1 %bitcast_convert_fusion = (f32[1,768,1536]{2,1,0:T(8,128)}, f32[1,768,1536]{2,1,0:T(8,128)}) fusion(bf16[768,1536]{1,0:T(8,128)(2,1)S(1)} %copy-done.1, bf16[768,1536]{1,0:T(8,128)(2,1)S(1)} %copy-done), kind=kLoop, calls=%fused_computation | loop fusion | flops 2359296 | bytes 14155776 | tf_op jit(solution)/shard_map/convert_element_type | solution.py:1407
  475.4 0.0 copy-done.2
  475.4 0.0 copy-done.3
  475.4 0.0 copy-start.6
  475.4 0.0 copy-start.5
  475.4 2.5 bitcast_convert_fusion.3
  477.9 0.0 copy-done.6
  477.9 0.8 copy.28
  478.7 0.0 copy-done.5
  478.7 0.8 copy.29
  (1 shorter events, 0.0 us)
Async XLA Ops:
  463.8 4.0 copy-start.4
  465.2 4.2 copy-start.1
  467.8 2.5 copy-start
  470.3 5.1 %copy-start.2 = (bf16[768,768]{1,0:T(8,128)(2,1)S(1)}, bf16[768,768]{1,0:T(8,128)(2,1)}, u32[]{:S(2)}) copy-start(bf16[768,768]{1,0:T(8,128)(2,1)} %get-tuple-element.48) | copy-start | bytes 3538948
  470.3 5.1 %copy-start.3 = (bf16[768,768]{1,0:T(8,128)(2,1)S(1)}, bf16[768,768]{1,0:T(8,128)(2,1)}, u32[]{:S(2)}) copy-start(bf16[768,768]{1,0:T(8,128)(2,1)} %get-tuple-element.49) | copy-start | bytes 3538948
  475.4 2.6 copy-start.6
  475.4 3.4 copy-start.5

commit v4 on v3

--- a/solution.py
+++ b/solution.py
@@ -62,18 +62,18 @@
     return head * cos + pltpu.roll(head, HEAD // 2, 1) * sin
 
 
-(ATTEND, NORM, TWIN, HIDE, GIVE, FAR, JOIN, GRAD, GRAD_TWIN, BACK, FAR_BACK, MID, ATTEND_BACK, CLOSE, LOAD, REST) = range(16)
+(ATTEND, NORM, TWIN, HIDE, GIVE, FAR, JOIN, GRAD, GRAD_TWIN, BACK, FAR_BACK, MID, ATTEND_BACK, CLOSE, LOAD, GRADS_IN, GRADS_OUT, REST) = range(18)
 
 FIRST_PLAN = (
     (ATTEND, 0),
     (ATTEND, 1),
     (NORM, 0),
+    (NORM, 1),
     (TWIN, 0),
-    (NORM, 1),
     (TWIN, 1),
     (HIDE, 0),
+    (HIDE, 1),
     (GIVE, 0),
-    (HIDE, 1),
     (GIVE, 1),
     (FAR, 0),
     (JOIN, 0),
@@ -85,13 +85,17 @@
     (GRAD_TWIN, 1),
     (BACK, 0),
     (BACK, 1),
+    (GRADS_IN, 0),
     (FAR_BACK, 0),
+    (GRADS_IN, 1),
     (MID, 0),
+    (GRADS_OUT, 0),
     (FAR_BACK, 1),
+    (ATTEND_BACK, 0),
     (MID, 1),
-    (ATTEND_BACK, 0),
+    (GRADS_OUT, 1),
+    (CLOSE, 0),
     (ATTEND_BACK, 1),
-    (CLOSE, 0),
     (CLOSE, 1),
 )
 SECOND_PLAN = (
@@ -101,8 +105,8 @@
     (ATTEND, 0),
     (ATTEND, 1),
     (NORM, 0),
+    (NORM, 1),
     (TWIN, 0),
-    (NORM, 1),
     (TWIN, 1),
     (GRAD_TWIN, 0),
     (GRAD_TWIN, 1),
@@ -110,19 +114,23 @@
     (BACK, 0),
     (HIDE, 1),
     (BACK, 1),
+    (GIVE, 0),
+    (GIVE, 1),
     (FAR_BACK, 0),
+    (GRADS_IN, 0),
     (MID, 0),
     (FAR_BACK, 1),
+    (ATTEND_BACK, 0),
     (MID, 1),
-    (ATTEND_BACK, 0),
+    (GRADS_IN, 1),
+    (CLOSE, 0),
     (ATTEND_BACK, 1),
-    (CLOSE, 0),
+    (GRADS_OUT, 0),
     (CLOSE, 1),
-    (GIVE, 0),
-    (GIVE, 1),
+    (GRADS_OUT, 1),
     (FAR, 0),
+    (FAR, 1),
     (JOIN, 0),
-    (FAR, 1),
     (JOIN, 1),
 )
 
@@ -137,17 +145,21 @@
     wg_in,
     wu_in,
     wd_in,
-    side_in,
-    meta_in,
+    gain_one_in,
+    gain_two_in,
+    segments_in,
+    ids_in,
+    logits_in,
     freq_in,
     acts_out,
     ingrad_out,
     gains_out,
-    n2rows_out,
-    dyrows_out,
-    hid_out,
-    dgate_out,
-    dup_out,
+    own_gate_out,
+    own_up_out,
+    own_down_out,
+    their_gate_out,
+    their_up_out,
+    their_down_out,
     n1_out,
     dqkv_out,
     att_out,
@@ -299,14 +311,41 @@
         weight(wd_in, wd.at[aligned(f * (HIDDEN // 2), HIDDEN // 2, 16)], 5),
     ]
 
+    w_pieces = [
+        weight(src.at[aligned(i * size, size, 16)], dst.at[aligned(f * 4 * size + i * size, size, 16)], n)
+        for n, src, dst, size in (
+            (3, wg_in, wg, HALF // 4),
+            (4, wu_in, wu, HALF // 4),
+            (5, wd_in, wd, HIDDEN // 8),
+        )
+        for i in range(4)
+    ]
+
+    def send_pieces(start, stop):
+        for copy in w_pieces[start:stop]:
+            copy.start()
+
     def x_copy(m):
         return weight(x_in.at[m], xpair.at[m, own_rows], 6 + m)
 
     def ct_copy(m):
         return remote(ct_in.at[m], gpair.at[m, x], ws_sem.at[10 + m], gr_sem.at[x, m], twin)
 
-    side[f] = side_in[...]
-    meta[x] = meta_in[...]
+    side[f, 0:1] = gain_one_in[...].astype(F32)
+    side[f, 1:2] = gain_two_in[...].astype(F32)
+    side[f, 2:4, :SEQ] = segments_in[...].astype(F32)
+    row = lax.broadcasted_iota(jnp.int32, (SEQ, SEQ), 0)
+    col = lax.broadcasted_iota(jnp.int32, (SEQ, SEQ), 1)
+    unit = jnp.where(row == col, 1.0, 0.0).astype(BF)
+    for m in range(MB):
+        left = logits_in[m]
+        turned = jnp.zeros((4, SEQ), F32)
+        for _ in range(3):
+            high = left.astype(BF)
+            left = left - high.astype(F32)
+            turned = turned + dot_tn(high, unit)
+        meta[x, m, 0:4] = dot_tn(ids_in[m].astype(F32).astype(BF), unit)
+        meta[x, m, 4:8] = turned
     side_copy = weight(side.at[f], side.at[f], 8)
     meta_copy = remote(meta.at[x], meta.at[x], ws_sem.at[9], wr_sem.at[9], twin)
     gains_acc[...] = jnp.zeros_like(gains_acc)
@@ -323,10 +362,7 @@
         x_copy(1).start()
 
     meta_copy.wait_recv()
-    earlier = lax.broadcasted_iota(jnp.int32, (SEQ, SEQ), 0) < lax.broadcasted_iota(
-        jnp.int32, (SEQ, SEQ), 1
-    )
-    earlier = jnp.where(earlier, 1.0, 0.0).astype(BF)
+    earlier = jnp.where(row < col, 1.0, 0.0).astype(BF)
 
     @pl.loop(0, 2 * MB)
     def _(i):
@@ -358,14 +394,12 @@
     side_copy.wait_recv()
     gains[:, pl.ds(0, HALF)] = side[0, 0:2]
     gains[:, pl.ds(HALF, HALF)] = side[1, 0:2]
-    row = lax.broadcasted_iota(jnp.int32, (SEQ, SEQ), 0)
-    col = lax.broadcasted_iota(jnp.int32, (SEQ, SEQ), 1)
     lane = lax.broadcasted_iota(jnp.int32, (SEQ, HEAD), 1)
     turn = jnp.where(lane < HEAD // 2, -1.0, 1.0)
     for m in range(MB):
         for s in range(2):
             across = jnp.broadcast_to(side[s, 2 + m : 3 + m, :SEQ], (SEQ, SEQ))
-            down = dot_nt(jnp.where(row == col, 1.0, 0.0).astype(BF), across.astype(BF))
+            down = dot_nt(unit, across.astype(BF))
             same = jnp.where(down == across, 1.0, 0.0)
             mask_t[m, s] = jnp.where(col <= row, same, 0.0)
             places = jnp.sum(jnp.where(col < row, same, 0.0), axis=1, keepdims=True)
@@ -468,14 +502,15 @@
                 copy.wait_recv()
             for copy in w_attn:
                 copy.wait_send()
-            for copy in w_moe:
-                copy.start()
             pl.when(first)(x_local.wait)
+
+            send_pieces(0, 1)
 
             @pl.when(second)
             def _():
                 ct_copy(0).start()
                 ct_copy(1).start()
+                send_pieces(1, 4)
 
         @pl.when(first)
         def _():
@@ -518,6 +553,8 @@
             part_send[m, :, cols] = jnp.where(mine, low, top).astype(BF)
 
         to_partner(0, m, part_send.at[m], part_recv.at[m]).start()
+        pl.when(jnp.logical_and(first, m == 0))(lambda: send_pieces(1, 2))
+        pl.when(jnp.logical_and(first, m == 1))(lambda: send_pieces(2, 4))
 
     def norm_step(m):
         to_partner(0, m, part_send.at[m], part_recv.at[m]).wait_recv()
@@ -525,6 +562,8 @@
         hid_one[m] = rows
         n2pair[m, x] = (rows * inverse_rms(rows) * gains[1:2]).astype(BF)
         n2_copy(m).start()
+        pl.when(m == 0)(lambda: send_pieces(4, 5))
+        pl.when(m == 1)(lambda: send_pieces(5, 12))
         spread(m, x, n2pair, dsend)
         exchange_half(0, m, dsend, n2recv, x)
 
@@ -542,7 +581,6 @@
                 copy.wait_recv()
 
         received(0, m, n2recv)
-        out_copy(0, n2recv.at[m], n2rows_out.at[m], m).start()
 
         @pl.loop(0, HIDDEN // 256)
         def _(j):
@@ -555,29 +593,28 @@
             us[m, :, cols] = up.astype(BF)
             hid[m, :, cols] = (0.5 * gate * (1.0 + bend) * up).astype(BF)
 
-        out_copy(1, hid.at[m], hid_out.at[m], m).start()
-
-        @pl.when(m == 0)
+
+    def need_down():
+        local[6].wait()
+        w_moe[2].wait_recv()
+        for copy in w_moe:
+            copy.wait_send()
+
+    def give_step(m):
+        @pl.when(jnp.logical_and(first, m == 0))
         def _():
-            local[6].wait()
-            w_moe[2].wait_recv()
-            for copy in w_moe:
-                copy.wait_send()
-
-            @pl.when(first)
-            def _():
-                pl.semaphore_signal(go_sem, inc=1, device_id={"section": 1}, device_id_type=MESH)
-
-    def give_step(m):
-        pl.when(second)(lambda: sent(3, m, bsend))
+            need_down()
+            pl.semaphore_signal(go_sem, inc=1, device_id={"section": 1}, device_id_type=MESH)
+
+        sent(0, m, dsend)
 
         @pl.loop(0, WIDTH // 512)
         def _(j):
             cols = aligned(j * 512, 512, 128)
             block = dot(hid[m], wd[:, cols]).astype(BF)
-            bsend[m, :, :, :, cols] = block.reshape(PLANE, 2, SLOTS, 512)
-
-        exchange(1, m, bsend, yrecv)
+            dsend[m, :, :, :, cols] = block.reshape(PLANE, 2, SLOTS, 512)
+
+        exchange(1, m, dsend, yrecv)
 
     def weighed(m, source, cols):
         block = yrecv[m, :, source, :, cols].reshape(PLANE * SLOTS, 512)
@@ -607,7 +644,7 @@
             for cross in (0, 1):
                 acts_copy(m, cross).start()
 
-        out_copy(2, acts_s.at[m], acts_out.at[m], m).start()
+        out_copy(3, acts_s.at[m], acts_out.at[m], m).start()
 
     def dy_half(m, source):
         gate = cg_hi[m, source].astype(F32) + cg_lo[m, source].astype(F32)
@@ -617,7 +654,6 @@
     def grad_step(m):
         @pl.when(first)
         def _():
-            sent(1, m, bsend)
             wait_for(gpair.at[m, x], gr_sem.at[x, m])
 
         @pl.when(jnp.logical_and(second, m == 0))
@@ -631,8 +667,8 @@
         dy_half(m, away)
 
     def back_step(m):
+        pl.when(jnp.logical_and(second, m == 0))(need_down)
         received(2, m, dyrecv)
-        out_copy(3, dyrecv.at[m], dyrows_out.at[m], m).start()
 
         @pl.loop(0, HIDDEN // 256)
         def _(j):
@@ -649,8 +685,6 @@
             gs[m, :, cols] = (dhid * up * slope).astype(BF)
             us[m, :, cols] = (dhid * (gate * half)).astype(BF)
 
-        out_copy(4, gs.at[m], dgate_out.at[m], m).start()
-        out_copy(5, us.at[m], dup_out.at[m], m).start()
         sent(2, m, bsend)
 
         @pl.loop(0, WIDTH // 512)
@@ -740,7 +774,11 @@
             dn1_send[m, :, cols] = jnp.where(mine, low, top).astype(BF)
 
         dn1_copy(m).start()
-        dqkv_copy(m).start()
+
+        @pl.when(m == 1)
+        def _():
+            dqkv_copy(0).start()
+            dqkv_copy(1).start()
 
     def close_step(m):
         dn1_copy(m).wait_recv()
@@ -757,7 +795,51 @@
 
         out_copy(7, ingrad_s.at[m], ingrad_out.at[m], m).start()
 
+    half_rows = HALF
+    quarter_rows = HIDDEN // 2
+
+    def expert_out(i, m):
+        src, own, their = (
+            (wg, own_gate_out, their_gate_out),
+            (wu, own_up_out, their_up_out),
+            (wd, own_down_out, their_down_out),
+        )[i]
+        size = src.shape[0] // 2
+        part = src.at[aligned(m * size, size, 16)]
+        own = pltpu.make_async_copy(part, own, out_sem.at[i, m])
+        their = pltpu.make_async_copy(part, their, out_sem.at[i, m])
+        return own, their
+
+    def start_out(i, m):
+        own, their = expert_out(i, m)
+        pl.when(m == f)(own.start)
+        pl.when(m != f)(their.start)
+
+    def grads_in_step(m):
+        @pl.loop(0, 3)
+        def _(j):
+            cols = aligned(m * half_rows + j * 256, 256, 128)
+            rows = n2recv[:, :, :, :, cols].reshape(MB * ROWS, 256)
+            wg[cols, :] = dot_tn(rows, gs[...].reshape(MB * ROWS, HIDDEN)).astype(BF)
+            wu[cols, :] = dot_tn(rows, us[...].reshape(MB * ROWS, HIDDEN)).astype(BF)
+
+        start_out(0, m)
+        start_out(1, m)
+
+    def grads_out_step(m):
+        cols = aligned(m * quarter_rows, quarter_rows, 128)
+
+        @pl.loop(0, 3)
+        def _(j):
+            at = aligned(j * 512, 512, 128)
+            rows = dyrecv[:, :, :, :, at].reshape(MB * ROWS, 512)
+            wd[cols, at] = dot_tn(hid[:, :, cols].reshape(MB * ROWS, quarter_rows), rows).astype(BF)
+
+        start_out(2, m)
+
     steps = {
+        GRADS_IN: grads_in_step,
+        GRADS_OUT: grads_out_step,
         ATTEND: attend_step,
         NORM: norm_step,
         TWIN: twin_step,
@@ -795,9 +877,8 @@
         out_copy(8, n1s.at[m, :, own_half], n1_out.at[m], m).start()
         out_copy(9, dqkv_all.at[m], dqkv_out.at[m], m).start()
         out_copy(10, att.at[m], att_out.at[m], m).start()
-        sent(0, m, dsend)
-        pl.when(first)(lambda: sent(3, m, bsend))
-        pl.when(second)(lambda: sent(1, m, bsend))
+        sent(1, m, dsend)
+        sent(3, m, bsend)
         to_partner(0, m, part_send.at[m], part_recv.at[m]).wait_send()
         da_copy(m).wait_send()
         dn1_copy(m).wait_send()
@@ -824,21 +905,17 @@
     @pl.loop(0, MB)
     def _(m):
         pairs = (
-            (n2recv, n2rows_out),
-            (hid, hid_out),
-            (acts_s, acts_out),
-            (dyrecv, dyrows_out),
-            (gs, dgate_out),
-            (us, dup_out),
-            (da_pair, da_out),
-            (ingrad_s, ingrad_out),
-            (None, n1_out),
-            (dqkv_all, dqkv_out),
-            (att, att_out),
+            (3, acts_s.at[m], acts_out.at[m]),
+            (6, da_pair.at[m], da_out.at[m]),
+            (7, ingrad_s.at[m], ingrad_out.at[m]),
+            (8, n1s.at[m, :, own_half], n1_out.at[m]),
+            (9, dqkv_all.at[m], dqkv_out.at[m]),
+            (10, att.at[m], att_out.at[m]),
         )
-        for i, (src, dst) in enumerate(pairs):
-            src = n1s.at[m, :, own_half] if src is None else src.at[m]
-            out_copy(i, src, dst.at[m], m).wait()
+        for i, src, dst in pairs:
+            out_copy(i, src, dst, m).wait()
+        for i in range(3):
+            expert_out(i, m)[0].wait()
 
 
 def run_sections(*operands):
@@ -856,18 +933,19 @@
             out(MB, SEQ, WIDTH),
             out(MB, SEQ, WIDTH),
             out(8, WIDTH, dtype=F32),
-            out(*blocks),
-            out(*blocks),
-            out(MB, ROWS, HIDDEN),
-            out(MB, ROWS, HIDDEN),
-            out(MB, ROWS, HIDDEN),
+            out(HALF, HIDDEN),
+            out(HALF, HIDDEN),
+            out(HIDDEN // 2, WIDTH),
+            out(HALF, HIDDEN),
+            out(HALF, HIDDEN),
+            out(HIDDEN // 2, WIDTH),
             out(MB, 2 * SEQ, HALF),
             out(MB, 2, 2 * SEQ, QKV),
             out(MB, 2 * SEQ, HALF),
             out(MB, 2 * SEQ, WIDTH),
         ),
-        in_specs=[anywhere] * 9 + [vmem] * 3,
-        out_specs=[anywhere] * 2 + [vmem] + [anywhere] * 9,
+        in_specs=[anywhere] * 9 + [vmem] * 6,
+        out_specs=[anywhere] * 2 + [vmem] + [anywhere] * 10,
         scratch_shapes=[
             pltpu.VMEM((WIDTH, QKV), BF),
             pltpu.VMEM((HALF, WIDTH), BF),
@@ -936,16 +1014,13 @@
 
 BAND = 192
 SLICE = 48
-WIDE = 1792
-NARROW = 896
+LANES = (("z", 1024), ("y", 1024), ("z", 768), ("y", 768))
 
 
 def grads_kernel(
-    n2_in,
-    dy_in,
-    hid_in,
-    dgate_in,
-    dup_in,
+    their_gate,
+    their_up,
+    their_down,
     n1_in,
     dqkv_in,
     att_in,
@@ -955,61 +1030,35 @@
     k_out,
     v_out,
     o_out,
-    gate_out,
-    up_out,
-    down_out,
+    part_gate,
+    part_up,
+    part_down,
     gains_out,
-    n2,
-    dy,
-    hid,
-    dgate,
-    dup,
     n1,
     dqkv,
     att,
     da,
-    v_a,
-    v_b,
-    r1_a,
-    r1_b,
-    s1_a,
-    s1_b,
-    r2_a,
-    r2_b,
-    s2_a,
-    s2_b,
-    r3_a,
-    r3_b,
-    g_a,
-    g_b,
-    their_gate,
-    their_up,
-    their_down,
-    part_gate,
-    part_up,
-    part_down,
-    own_gate,
-    own_up,
-    own_down,
-    small,
-    small_recv,
-    load_sem,
-    send_sem,
-    recv_sem,
-    pair_send,
-    pair_recv,
-    small_send,
-    small_recv_sem,
-    out_sem,
+    *rest,
 ):
+    lane_refs, rest = [rest[i * 7 : i * 7 + 7] for i in range(len(LANES))], rest[7 * len(LANES) :]
+    (
+        small,
+        small_recv,
+        load_sem,
+        send_sem,
+        recv_sem,
+        pair_send,
+        pair_recv,
+        small_send,
+        small_recv_sem,
+        out_sem,
+    ) = rest
     f = lax.axis_index("fsdp")
     e = lax.axis_index("expert")
     y, x, z = e // 8, lax.rem(e // 4, 2), lax.rem(e, 4)
     other = 1 - f
     own_half = aligned(f * HALF, HALF, 128)
     other_half = aligned(other * HALF, HALF, 128)
-    own_quarter = aligned(f * (HIDDEN // 2), HIDDEN // 2, 128)
-    other_quarter = aligned(other * (HIDDEN // 2), HIDDEN // 2, 128)
 
     def along_y(d):
         return {"expert": lax.rem(y + d, 4) * 8 + x * 4 + z}
@@ -1031,11 +1080,6 @@
         (da_in, da),
         (n1_in, n1),
         (dqkv_in, dqkv),
-        (n2_in, n2),
-        (dgate_in, dgate),
-        (dup_in, dup),
-        (hid_in, hid),
-        (dy_in, dy),
     ]
     loads = [pltpu.make_async_copy(a, b, load_sem.at[i]) for i, (a, b) in enumerate(loads)]
     for copy in loads:
@@ -1054,44 +1098,96 @@
     def wait_for(ref, sem):
         pltpu.make_async_copy(ref, ref, sem).wait()
 
+    class Lane:
+        def __init__(self, i):
+            self.i = i
+            self.v, self.r1, self.s1, self.r2, self.s2, self.r3, self.g = lane_refs[i]
+            axes = ((along_y, y), (along_z, z))
+            (self.axis, self.at), (self.next, self.to) = axes if LANES[i][0] == "y" else axes[::-1]
+            half = LANES[i][1] // 2
+            self.mine = aligned(x * half, half, 128)
+            self.theirs = aligned((1 - x) * half, half, 128)
+            self.place = aligned(self.at * BAND + self.to * SLICE, SLICE, 16)
+
+        def send(self, stage, src, dst, place):
+            remote(
+                src, dst, send_sem.at[self.i, stage], recv_sem.at[self.i, stage], place
+            ).start()
+
+        def arrived(self, stage, ref):
+            wait_for(ref, recv_sem.at[self.i, stage])
+
+        def spread(self):
+            for d in (1, 2, 3):
+                rows = aligned(lax.rem(self.at + d, 4) * BAND, BAND, 16)
+                self.send(0, self.v.at[rows], self.r1.at[self.at], self.axis(d))
+
+        def join_one(self):
+            self.arrived(0, self.r1.at[pl.ds(0, 3)])
+            total = self.v[aligned(self.at * BAND, BAND, 16)].astype(F32)
+            for d in (1, 2, 3):
+                total = total + self.r1[lax.rem(self.at + d, 4)].astype(F32)
+            self.s1[...] = total.astype(BF)
+            for d in (1, 2, 3):
+                rows = aligned(lax.rem(self.to + d, 4) * SLICE, SLICE, 16)
+                self.send(1, self.s1.at[rows], self.r2.at[self.to], self.next(d))
+
+        def join_two(self):
+            self.arrived(1, self.r2.at[pl.ds(0, 3)])
+            total = self.s1[aligned(self.to * SLICE, SLICE, 16)].astype(F32)
+            for d in (1, 2, 3):
+                total = total + self.r2[lax.rem(self.to + d, 4)].astype(F32)
+            self.s2[...] = total.astype(BF)
+            self.send(2, self.s2.at[:, self.theirs], self.r3, twin)
+
+        def join_three(self):
+            self.arrived(2, self.r3)
+            total = self.s2[:, self.mine].astype(F32) + self.r3[...].astype(F32)
+            self.g[self.place, self.mine] = total.astype(BF)
+            part = self.g.at[self.place, self.mine]
+            self.send(3, part, part, twin)
+
+        def gather_two(self):
+            self.arrived(3, self.g.at[self.place, self.theirs])
+            part = self.g.at[self.place]
+            for d in (1, 2, 3):
+                self.send(4, part, part, self.next(d))
+
+        def gather_one(self):
+            self.arrived(4, self.g.at[pl.ds(0, 3 * SLICE)])
+            part = self.g.at[aligned(self.at * BAND, BAND, 16)]
+            for d in (1, 2, 3):
+                self.send(5, part, part, self.axis(d))
+
+        def finish(self):
+            self.arrived(5, self.g.at[pl.ds(0, 3 * BAND)])
+
+        def drain(self):
+            wait_for(self.v.at[pl.ds(0, 3 * BAND)], send_sem.at[self.i, 0])
+            wait_for(self.s1.at[pl.ds(0, 3 * SLICE)], send_sem.at[self.i, 1])
+            wait_for(self.s2.at[:, self.theirs], send_sem.at[self.i, 2])
+            wait_for(self.g.at[self.place, self.mine], send_sem.at[self.i, 3])
+            wait_for(self.g.at[pl.ds(0, 3 * SLICE)], send_sem.at[self.i, 4])
+            wait_for(self.g.at[pl.ds(0, 3 * BAND)], send_sem.at[self.i, 5])
+
+    out_one, query_one, out_two, query_two = lanes = [Lane(i) for i in range(len(LANES))]
+
+    def over_micro(group, cols):
+        block = jnp.concatenate([dqkv[m, group, :, cols] for m in range(MB)], axis=0)
+        return dot_tn(n1[...], block).astype(BF)
+
     for copy in loads[:2]:
         copy.wait()
-
-    @pl.loop(0, WIDTH // 512)
-    def _(j):
-        cols = aligned(j * 512, 512, 128)
-        v_b[:, cols] = dot_tn(att[...], da[:, cols]).astype(BF)
-
+    for j in range(2):
+        cols = pl.ds(j * 512, 512)
+        out_one.v[:, cols] = dot_tn(att[...], da[:, cols]).astype(BF)
+    pl.semaphore_wait(barrier, len(neighbours))
+    out_one.spread()
     for copy in loads[2:4]:
         copy.wait()
-
-    def over_micro(cols):
-        block = jnp.concatenate([dqkv[m, :, :, cols] for m in range(MB)], axis=1)
-        return [dot_tn(n1[...], block[g]).astype(BF) for g in range(2)]
-
-    for g, block in enumerate(over_micro(pl.ds(HALF + HEAD, HEAD))):
-        v_b[:, pl.ds(WIDTH + g * HEAD, HEAD)] = block
-    pl.semaphore_wait(barrier, len(neighbours))
-
-    lanes = (
-        (0, v_a, r1_a, s1_a, r2_a, s2_a, r3_a, g_a, along_y, y, along_z, z),
-        (1, v_b, r1_b, s1_b, r2_b, s2_b, r3_b, g_b, along_z, z, along_y, y),
-    )
-
-    def spread_one(lane):
-        i, v, r1, _, _, _, _, _, axis, at, _, _ = lane
-        for d in (1, 2, 3):
-            rows = aligned(lax.rem(at + d, 4) * BAND, BAND, 16)
-            remote(v.at[rows], r1.at[at], send_sem.at[i, 0], recv_sem.at[i, 0], axis(d)).start()
-
-    spread_one(lanes[1])
-    for j in range(3):
-        for g, block in enumerate(over_micro(pl.ds(j * 256, 256))):
-            v_a[:, pl.ds(g * HALF + j * 256, 256)] = block
-    for g, block in enumerate(over_micro(pl.ds(HALF, HEAD))):
-        v_a[:, pl.ds(WIDTH + g * HEAD, HEAD)] = block
-    spread_one(lanes[0])
-
+    query_one.v[:, pl.ds(0, HALF)] = over_micro(0, pl.ds(0, HALF))
+    query_one.v[:, pl.ds(HALF, 256)] = over_micro(1, pl.ds(0, 256))
+    query_one.spread()
     small[...] = gains_in[...]
     small_pair = remote(
         small.at[:, other_half],
@@ -1101,24 +1197,31 @@
         partner,
     )
     small_pair.start()
-
-    for copy in loads[4:6]:
-        copy.wait()
-    their_gate[...] = dot_tn(n2[:, other_half], dgate[...]).astype(BF)
-    pair = [remote(their_gate, part_gate, pair_send.at[0], pair_recv.at[0], partner)]
-    pair[0].start()
-    loads[6].wait()
-    their_up[...] = dot_tn(n2[:, other_half], dup[...]).astype(BF)
-    pair.append(remote(their_up, part_up, pair_send.at[1], pair_recv.at[1], partner))
-    pair[1].start()
-    for copy in loads[7:]:
-        copy.wait()
-    their_down[...] = dot_tn(hid[:, other_quarter], dy[...]).astype(BF)
-    pair.append(remote(their_down, part_down, pair_send.at[2], pair_recv.at[2], partner))
-    pair[2].start()
-    own_gate[...] = dot_tn(n2[:, own_half], dgate[...])
-    own_up[...] = dot_tn(n2[:, own_half], dup[...])
-    own_down[...] = dot_tn(hid[:, own_quarter], dy[...])
+    out_two.v[:, pl.ds(0, 512)] = dot_tn(att[...], da[:, pl.ds(1024, 512)]).astype(BF)
+    query_two.v[:, pl.ds(0, 512)] = over_micro(1, pl.ds(256, 512))
+    for g in range(2):
+        query_two.v[:, pl.ds(512 + g * HEAD, HEAD)] = over_micro(g, pl.ds(HALF, HEAD))
+        out_two.v[:, pl.ds(512 + g * HEAD, HEAD)] = over_micro(g, pl.ds(HALF + HEAD, HEAD))
+
+    pair = [
+        remote(src, dst, pair_send.at[i], pair_recv.at[i], partner)
+        for i, (src, dst) in enumerate(
+            ((their_gate, part_gate), (their_up, part_up), (their_down, part_down))
+        )
+    ]
+    pieces = [
+        remote(src.at[rows], dst.at[rows], pair_send.at[n], pair_recv.at[n], partner)
+        for n, src, dst, size in (
+            (0, their_gate, part_gate, HALF // 4),
+            (1, their_up, part_up, HALF // 4),
+            (2, their_down, part_down, HIDDEN // 8),
+        )
+        for rows in [pl.ds(i * size, size) for i in range(4)]
+    ]
+
+    def send_pieces(start, stop):
+        for copy in pieces[start:stop]:
+            copy.start()
 
     def spread_small(i, axis):
         for d in (1, 2, 3):
@@ -1148,36 +1251,15 @@
     small[:, pl.ds(0, HALF)] = small[:, own_half] + small_recv[0]
     spread_small(0, along_y)
 
-    def join_one(lane):
-        i, v, r1, s1, r2, _, _, _, _, at, axis, to = lane
-        wait_for(r1.at[pl.ds(0, 3)], recv_sem.at[i, 0])
-        total = v[aligned(at * BAND, BAND, 16)].astype(F32)
-        for d in (1, 2, 3):
-            total = total + r1[lax.rem(at + d, 4)].astype(F32)
-        s1[...] = total.astype(BF)
-        for d in (1, 2, 3):
-            rows = aligned(lax.rem(to + d, 4) * SLICE, SLICE, 16)
-            remote(s1.at[rows], r2.at[to], send_sem.at[i, 1], recv_sem.at[i, 1], axis(d)).start()
-
-    join_one(lanes[1])
-    join_one(lanes[0])
+    out_two.spread()
+    query_two.spread()
+    send_pieces(0, 4)
     join_small(0, along_y)
     spread_small(1, along_z)
-
-    mine = aligned(x * NARROW, NARROW, 128)
-    theirs = aligned((1 - x) * NARROW, NARROW, 128)
-
-    def join_two(lane):
-        i, _, _, s1, r2, s2, r3, _, _, _, _, to = lane
-        wait_for(r2.at[pl.ds(0, 3)], recv_sem.at[i, 1])
-        total = s1[aligned(to * SLICE, SLICE, 16)].astype(F32)
-        for d in (1, 2, 3):
-            total = total + r2[lax.rem(to + d, 4)].astype(F32)
-        s2[...] = total.astype(BF)
-        remote(s2.at[:, theirs], r3, send_sem.at[i, 2], recv_sem.at[i, 2], twin).start()
-
-    join_two(lanes[1])
-    join_two(lanes[0])
+    for lane in lanes:
+        lane.join_one()
+    for lane in lanes:
+        lane.join_two()
     join_small(1, along_z)
     small_twin = remote(
         small.at[:, pl.ds(0, HALF)],
@@ -1187,74 +1269,39 @@
         twin,
     )
     small_twin.start()
-
-    def place_of(lane):
-        _, _, _, _, _, _, _, _, _, at, _, to = lane
-        return aligned(at * BAND + to * SLICE, SLICE, 16)
-
-    def join_three(lane):
-        i, _, _, _, _, s2, r3, g, _, _, _, _ = lane
-        wait_for(r3, recv_sem.at[i, 2])
-        total = s2[:, mine].astype(F32) + r3[...].astype(F32)
-        g[place_of(lane), mine] = total.astype(BF)
-        part = g.at[place_of(lane), mine]
-        remote(part, part, send_sem.at[i, 3], recv_sem.at[i, 3], twin).start()
-
-    def gather_two(lane):
-        i, _, _, _, _, _, _, g, _, _, axis, _ = lane
-        wait_for(g.at[place_of(lane), theirs], recv_sem.at[i, 3])
-        part = g.at[place_of(lane)]
-        for d in (1, 2, 3):
-            remote(part, part, send_sem.at[i, 4], recv_sem.at[i, 4], axis(d)).start()
-
-    def gather_one(lane):
-        i, _, _, _, _, _, _, g, axis, at, _, _ = lane
-        wait_for(g.at[pl.ds(0, 3 * SLICE)], recv_sem.at[i, 4])
-        part = g.at[aligned(at * BAND, BAND, 16)]
-        for d in (1, 2, 3):
-            remote(part, part, send_sem.at[i, 5], recv_sem.at[i, 5], axis(d)).start()
-
-    for step in (join_three, gather_two, gather_one):
-        step(lanes[1])
-        step(lanes[0])
-
+    send_pieces(4, 5)
+    for lane in lanes:
+        lane.join_three()
+    send_pieces(5, 12)
+    for lane in lanes:
+        lane.gather_two()
+    for lane in lanes:
+        lane.gather_one()
     small_twin.wait()
     gains_out[...] = small[:, pl.ds(0, HALF)] + small_recv[7]
 
-    def out_copy(i, src, dst):
-        copy = pltpu.make_async_copy(src, dst, out_sem.at[i])
+    outs = []
+
+    def out_copy(src, dst):
+        copy = pltpu.make_async_copy(src, dst, out_sem.at[len(outs)])
         copy.start()
-        return copy
-
-    outs = []
-    for i, (arrived, part, own, dst) in enumerate(
-        (
-            (pair[0], part_gate, own_gate, gate_out),
-            (pair[1], part_up, own_up, up_out),
-            (pair[2], part_down, own_down, down_out),
-        )
-    ):
-        arrived.wait_recv()
-        part[...] = (own[...] + part[...].astype(F32)).astype(BF)
-        outs.append(out_copy(i, part, dst))
-
-    wait_for(g_b.at[pl.ds(0, 3 * BAND)], recv_sem.at[1, 5])
-    outs.append(out_copy(3, g_b.at[:, pl.ds(0, WIDTH)], o_out))
-    outs.append(out_copy(4, g_b.at[:, pl.ds(WIDTH, 256)], v_out))
-    wait_for(g_a.at[pl.ds(0, 3 * BAND)], recv_sem.at[0, 5])
-    outs.append(out_copy(5, g_a.at[:, pl.ds(0, WIDTH)], q_out))
-    outs.append(out_copy(6, g_a.at[:, pl.ds(WIDTH, 256)], k_out))
+        outs.append(copy)
+
+    out_one.finish()
+    out_copy(out_one.g, o_out.at[:, pl.ds(0, 1024)])
+    query_one.finish()
+    out_copy(query_one.g, q_out.at[:, pl.ds(0, 1024)])
+    out_two.finish()
+    out_copy(out_two.g.at[:, pl.ds(0, 512)], o_out.at[:, pl.ds(1024, 512)])
+    out_copy(out_two.g.at[:, pl.ds(512, 256)], v_out)
+    query_two.finish()
+    out_copy(query_two.g.at[:, pl.ds(0, 512)], q_out.at[:, pl.ds(1024, 512)])
+    out_copy(query_two.g.at[:, pl.ds(512, 256)], k_out)
 
     for lane in lanes:
-        i, v, _, s1, _, s2, _, g = lane[:8]
-        wait_for(v.at[pl.ds(0, 3 * BAND)], send_sem.at[i, 0])
-        wait_for(s1.at[pl.ds(0, 3 * SLICE)], send_sem.at[i, 1])
-        wait_for(s2.at[:, theirs], send_sem.at[i, 2])
-        wait_for(g.at[place_of(lane), mine], send_sem.at[i, 3])
-        wait_for(g.at[pl.ds(0, 3 * SLICE)], send_sem.at[i, 4])
-        wait_for(g.at[pl.ds(0, 3 * BAND)], send_sem.at[i, 5])
+        lane.drain()
     for copy in pair:
-        copy.wait_send()
+        copy.wait()
     for copy in outs:
         copy.wait()
 
@@ -1266,20 +1313,17 @@
     vmem = pl.BlockSpec(memory_space=pltpu.VMEM)
     anywhere = pl.BlockSpec(memory_space=pl.ANY)
     dma = pltpu.SemaphoreType.DMA
-    lane = [
-        pltpu.VMEM((HALF, WIDE), BF),
-        pltpu.VMEM((4, BAND, WIDE), BF),
-        pltpu.VMEM((BAND, WIDE), BF),
-        pltpu.VMEM((4, SLICE, WIDE), BF),
-        pltpu.VMEM((SLICE, WIDE), BF),
-        pltpu.VMEM((SLICE, NARROW), BF),
-        pltpu.VMEM((HALF, WIDE), BF),
-    ]
-    expert = [
-        pltpu.VMEM((HALF, HIDDEN), BF),
-        pltpu.VMEM((HALF, HIDDEN), BF),
-        pltpu.VMEM((HIDDEN // 2, WIDTH), BF),
-    ]
+    lanes = []
+    for _, width in LANES:
+        lanes += [
+            pltpu.VMEM((HALF, width), BF),
+            pltpu.VMEM((4, BAND, width), BF),
+            pltpu.VMEM((BAND, width), BF),
+            pltpu.VMEM((4, SLICE, width), BF),
+            pltpu.VMEM((SLICE, width), BF),
+            pltpu.VMEM((SLICE, width // 2), BF),
+            pltpu.VMEM((HALF, width), BF),
+        ]
     return pl.pallas_call(
         grads_kernel,
         name="grads",
@@ -1293,41 +1337,71 @@
             out(HIDDEN // 2, WIDTH),
             jax.ShapeDtypeStruct((8, HALF), F32),
         ),
-        in_specs=[anywhere] * 9 + [vmem],
+        in_specs=[anywhere] * 7 + [vmem],
         out_specs=[anywhere] * 7 + [vmem],
         scratch_shapes=[
-            pltpu.VMEM((MB * ROWS, WIDTH), BF),
-            pltpu.VMEM((MB * ROWS, WIDTH), BF),
-            pltpu.VMEM((MB * ROWS, HIDDEN), BF),
-            pltpu.VMEM((MB * ROWS, HIDDEN), BF),
-            pltpu.VMEM((MB * ROWS, HIDDEN), BF),
             pltpu.VMEM((MB * 2 * SEQ, HALF), BF),
             pltpu.VMEM((MB, 2, 2 * SEQ, QKV), BF),
             pltpu.VMEM((MB * 2 * SEQ, HALF), BF),
             pltpu.VMEM((MB * 2 * SEQ, WIDTH), BF),
         ]
-        + [part for shape in lane for part in (shape, shape)]
-        + expert
-        + expert
+        + lanes
         + [
-            pltpu.VMEM((HALF, HIDDEN), F32),
-            pltpu.VMEM((HALF, HIDDEN), F32),
-            pltpu.VMEM((HIDDEN // 2, WIDTH), F32),
             pltpu.VMEM((8, WIDTH), F32),
             pltpu.VMEM((8, 8, HALF), F32),
-            dma((9,)),
-            dma((2, 6)),
-            dma((2, 6)),
+            dma((4,)),
+            dma((len(LANES), 6)),
+            dma((len(LANES), 6)),
             dma((3,)),
             dma((3,)),
             dma((8,)),
             dma((8,)),
-            dma((7,)),
+            dma((9,)),
         ],
         compiler_params=pltpu.CompilerParams(
             collective_id=1, has_side_effects=True, vmem_limit_bytes=62 * 2**20
         ),
     )(*operands)
+
+
+def finish_kernel(*refs):
+    (q, k, v, o, own_g, own_u, own_d, part_g, part_u, part_d, acts, grads, gains), outs = (
+        refs[:13],
+        refs[13:],
+    )
+    for src, dst in zip((q, k, v, o), outs):
+        dst[...] = src[...].astype(F32)
+    for own, part, dst in zip((own_g, own_u, own_d), (part_g, part_u, part_d), outs[4:]):
+        dst[...] = own[...].astype(F32) + part[...].astype(F32)
+    outs[7][...] = acts[...]
+    outs[8][...] = grads[...]
+    outs[9][...] = gains[0:1]
+    outs[10][...] = gains[1:2]
+
+
+def finish(*blocks):
+    steps = 6
+
+    def spec(rows, cols):
+        return pl.BlockSpec((rows // steps, cols), lambda i: (i, 0))
+
+    def whole(rows, cols):
+        return pl.BlockSpec((rows, cols), lambda i: (0, 0))
+
+    gains = blocks[-1]
+    split = blocks[:-1]
+    results = split[:7] + split[10:]
+    dtypes = [F32] * 7 + [BF] * 2
+    return pl.pallas_call(
+        finish_kernel,
+        name="finish",
+        grid=(steps,),
+        out_shape=[jax.ShapeDtypeStruct(b.shape, t) for b, t in zip(results, dtypes)]
+        + [jax.ShapeDtypeStruct((1, HALF), F32)] * 2,
+        in_specs=[spec(*b.shape) for b in split] + [whole(*gains.shape)],
+        out_specs=[spec(*b.shape) for b in results] + [whole(1, HALF)] * 2,
+        compiler_params=pltpu.CompilerParams(vmem_limit_bytes=62 * 2**20),
+    )(*blocks)
 
 
 def local(
@@ -1346,28 +1420,18 @@
     w_up,
     w_down,
 ):
-    side = jnp.concatenate(
-        [
-            gain_attn.astype(F32),
-            gain_moe.astype(F32),
-            jnp.pad(segments.astype(F32), ((0, 0), (0, HALF - SEQ))),
-            jnp.zeros((4, HALF), F32),
-        ],
-        axis=0,
-    )
-    meta = jnp.concatenate([expert_ids[0].astype(F32), gate_logits[0]], axis=-1)
-    meta = jnp.swapaxes(meta, 1, 2)
     steps = np.arange(HEAD) % (HEAD // 2)
     frequency = (ROPE_BASE ** (-steps * 2.0 / HEAD)).astype(np.float32)[None]
     (
         acts,
         in_grads,
         gain_parts,
-        n2rows,
-        dyrows,
-        hid,
-        dgate,
-        dup,
+        own_gate,
+        own_up,
+        own_down,
+        their_gate,
+        their_up,
+        their_down,
         n1,
         dqkv,
         att,
@@ -1382,34 +1446,50 @@
         w_gate[0, 0],
         w_up[0, 0],
         w_down[0, 0],
-        side,
-        meta,
+        gain_attn,
+        gain_moe,
+        segments,
+        expert_ids[0],
+        gate_logits[0],
         jnp.asarray(frequency),
     )
-    gq, gk, gv, go, grad_gate, grad_up, grad_down, gains = reduce_grads(
-        n2rows.reshape(MB * ROWS, WIDTH),
-        dyrows.reshape(MB * ROWS, WIDTH),
-        hid.reshape(MB * ROWS, HIDDEN),
-        dgate.reshape(MB * ROWS, HIDDEN),
-        dup.reshape(MB * ROWS, HIDDEN),
+    gq, gk, gv, go, part_gate, part_up, part_down, gains = reduce_grads(
+        their_gate,
+        their_up,
+        their_down,
         n1.reshape(MB * 2 * SEQ, HALF),
         dqkv,
         att.reshape(MB * 2 * SEQ, HALF),
         da.reshape(MB * 2 * SEQ, WIDTH),
         gain_parts,
     )
+    gq, gk, gv, go, grad_gate, grad_up, grad_down, acts, in_grads, gain_one, gain_two = finish(
+        gq,
+        gk,
+        gv,
+        go,
+        own_gate,
+        own_up,
+        own_down,
+        part_gate,
+        part_up,
+        part_down,
+        acts.reshape(MB * SEQ, WIDTH),
+        in_grads.reshape(MB * SEQ, WIDTH),
+        gains,
+    )
     return (
-        acts[None],
-        in_grads[None],
-        gq[None].astype(F32),
-        gk[None].astype(F32),
-        gv[None].astype(F32),
-        go[None].astype(F32),
-        gains[0:1],
-        gains[1:2],
-        grad_gate[None, None].astype(F32),
-        grad_up[None, None].astype(F32),
-        grad_down[None, None].astype(F32),
+        acts.reshape(1, MB, SEQ, WIDTH),
+        in_grads.reshape(1, MB, SEQ, WIDTH),
+        gq[None],
+        gk[None],
+        gv[None],
+        go[None],
+        gain_one,
+        gain_two,
+        grad_gate[None, None],
+        grad_up[None, None],
+        grad_down[None, None],
     )
 
 

time: 481 us -> 422 us (0.88)
  Pallas kernels: 458 us -> 418 us
  other arithmetic: 16.5 us -> 0 us
    pallas_call x1, Pallas kernels: 370 us -> 333 us  [run_sections(): pl.pallas_call(section_kernel, name='sections', out_shape=(out(MB, SEQ, W...]
    pallas_call x1, Pallas kernels: 88.5 us -> 72 us  [reduce_grads(): pl.pallas_call(grads_kernel, name='grads', out_shape=(out(HALF, WIDTH), o...]
    convert_element_type x8 -> x0, other arithmetic: 14.6 us -> none  [the longest x1 5.06 us: local(): go[None].astype(F32)]
    pallas_call x0 -> x1, Pallas kernels: none -> 12.1 us  [finish(): pl.pallas_call(finish_kernel, name='finish', grid=(steps,), out_shape=[ja...]
where the time goes in v4:
time: 422 us; the launch traced here: 421 us
  Pallas kernels  418 us (99%)
    pallas_call x1, Pallas kernels, run_sections(): pl.pallas_call(section_kernel, name='sections', out_shape=(out(MB, SEQ, W...  333 us
    pallas_call x1, Pallas kernels, reduce_grads(): pl.pallas_call(grads_kernel, name='grads', out_shape=(out(HALF, WIDTH), o...  72 us
    pallas_call x1, Pallas kernels, finish(): pl.pallas_call(finish_kernel, name='finish', grid=(steps,), out_shape=[ja...  12.1 us

profile of v4, /device:TPU:0, one launch (start us, length us, event | category | flops | bytes accessed | tf_op | source)
XLA Modules:
  0.0 421.4 jit_solution(9660734989664103481)
XLA Ops:
  0.6 1.4 copy.26
  2.1 1.4 copy.27
  3.5 333.5 %sections.1 = (bf16[2,96,1536]{2,1,0:T(8,128)(2,1)}, bf16[2,96,1536]{2,1,0:T(8,128)(2,1)}, f32[8,1536]{1,0:T(8,128)}, bf16[768,768]{1,0:T(8,128)(2,1)}, bf16[768...) custom-call(bf16[2,96,1536]{2,1,0:T(8,128)(2,1)} %x_in.1, ...), custom_call_target="tpu_custom_call" | custom-call | tf_op jit(solution)/shard_map/sections/pallas_call | solution.py:929
  337.0 72.0 %grads.1 = (bf16[768,1536]{1,0:T(8,128)(2,1)}, bf16[768,256]{1,0:T(8,128)(2,1)}, bf16[768,256]{1,0:T(8,128)(2,1)}, bf16[768,1536]{1,0:T(8,128)(2,1)}, bf16[768,7...) custom-call(bf16[768,768]{1,0:T(8,128)(2,1)} %get-tuple-element.43.their_gate, ...), custom_call_target="tpu_custom_call" | custom-call | tf_op jit(solution)/shard_map/grads/pallas_call | solution.py:1327
  409.1 12.1 %finish.1 = (f32[768,1536]{1,0:T(8,128)}, f32[768,256]{1,0:T(8,128)}, f32[768,256]{1,0:T(8,128)}, f32[768,1536]{1,0:T(8,128)}, f32[768,768]{1,0:T(8,128)}, /*ind...) custom-call(bf16[768,1536]{1,0:T(8,128)(2,1)} %get-tuple-element.51., ...), custom_call_target="tpu_custom_call" | custom-call | tf_op jit(solution)/shard_map/finish/pallas_call | solution.py:1395

commit v5 on v4

--- a/solution.py
+++ b/solution.py
@@ -62,76 +62,110 @@
     return head * cos + pltpu.roll(head, HEAD // 2, 1) * sin
 
 
-(ATTEND, NORM, TWIN, HIDE, GIVE, FAR, JOIN, GRAD, GRAD_TWIN, BACK, FAR_BACK, MID, ATTEND_BACK, CLOSE, LOAD, GRADS_IN, GRADS_OUT, REST) = range(18)
+(
+    ENTER,
+    PROJECT,
+    ATTEND,
+    NORM,
+    TWIN,
+    HIDE,
+    GIVE,
+    FAR,
+    JOIN,
+    GRAD,
+    GRAD_TWIN,
+    BACK,
+    FAR_BACK,
+    MID,
+    ATTEND_BACK,
+    PROJECT_BACK,
+    CLOSE,
+    LOAD,
+    GRADS_IN,
+    GRADS_OUT,
+    REST,
+) = range(21)
 
 FIRST_PLAN = (
-    (ATTEND, 0),
-    (ATTEND, 1),
-    (NORM, 0),
-    (NORM, 1),
-    (TWIN, 0),
-    (TWIN, 1),
-    (HIDE, 0),
-    (HIDE, 1),
-    (GIVE, 0),
-    (GIVE, 1),
-    (FAR, 0),
-    (JOIN, 0),
-    (FAR, 1),
-    (JOIN, 1),
-    (GRAD, 0),
-    (GRAD_TWIN, 0),
-    (GRAD, 1),
-    (GRAD_TWIN, 1),
-    (BACK, 0),
-    (BACK, 1),
-    (GRADS_IN, 0),
-    (FAR_BACK, 0),
-    (GRADS_IN, 1),
-    (MID, 0),
-    (GRADS_OUT, 0),
-    (FAR_BACK, 1),
-    (ATTEND_BACK, 0),
-    (MID, 1),
-    (GRADS_OUT, 1),
-    (CLOSE, 0),
-    (ATTEND_BACK, 1),
-    (CLOSE, 1),
+    (ENTER, 0, 0),
+    (ENTER, 1, 1),
+    (PROJECT, 0, 1),
+    (PROJECT, 1, 1),
+    (ATTEND, 0, 1),
+    (ATTEND, 1, 1),
+    (NORM, 0, 1),
+    (NORM, 1, 6),
+    (TWIN, 0, 0),
+    (TWIN, 1, 0),
+    (HIDE, 0, 0),
+    (HIDE, 1, 0),
+    (GIVE, 0, 0),
+    (GIVE, 1, 0),
+    (FAR, 0, 0),
+    (JOIN, 0, 0),
+    (FAR, 1, 0),
+    (JOIN, 1, 0),
+    (GRAD, 0, 0),
+    (GRAD_TWIN, 0, 0),
+    (GRAD, 1, 0),
+    (GRAD_TWIN, 1, 0),
+    (BACK, 0, 0),
+    (BACK, 1, 0),
+    (GRADS_IN, 0, 0),
+    (FAR_BACK, 0, 0),
+    (GRADS_IN, 1, 0),
+    (MID, 0, 0),
+    (GRADS_OUT, 0, 0),
+    (FAR_BACK, 1, 0),
+    (ATTEND_BACK, 0, 0),
+    (MID, 1, 0),
+    (PROJECT_BACK, 0, 0),
+    (GRADS_OUT, 1, 0),
+    (ATTEND_BACK, 1, 0),
+    (CLOSE, 0, 0),
+    (PROJECT_BACK, 1, 0),
+    (CLOSE, 1, 0),
 )
 SECOND_PLAN = (
-    (GRAD, 0),
-    (GRAD, 1),
-    (LOAD, 0),
-    (ATTEND, 0),
-    (ATTEND, 1),
-    (NORM, 0),
-    (NORM, 1),
-    (TWIN, 0),
-    (TWIN, 1),
-    (GRAD_TWIN, 0),
-    (GRAD_TWIN, 1),
-    (HIDE, 0),
-    (BACK, 0),
-    (HIDE, 1),
-    (BACK, 1),
-    (GIVE, 0),
-    (GIVE, 1),
-    (FAR_BACK, 0),
-    (GRADS_IN, 0),
-    (MID, 0),
-    (FAR_BACK, 1),
-    (ATTEND_BACK, 0),
-    (MID, 1),
-    (GRADS_IN, 1),
-    (CLOSE, 0),
-    (ATTEND_BACK, 1),
-    (GRADS_OUT, 0),
-    (CLOSE, 1),
-    (GRADS_OUT, 1),
-    (FAR, 0),
-    (FAR, 1),
-    (JOIN, 0),
-    (JOIN, 1),
+    (GRAD, 0, 0),
+    (GRAD, 1, 0),
+    (LOAD, 0, 5),
+    (ENTER, 0, 0),
+    (PROJECT, 0, 1),
+    (ENTER, 1, 1),
+    (ATTEND, 0, 1),
+    (PROJECT, 1, 1),
+    (NORM, 0, 1),
+    (ATTEND, 1, 1),
+    (TWIN, 0, 0),
+    (NORM, 1, 1),
+    (TWIN, 1, 0),
+    (GRAD_TWIN, 0, 0),
+    (GRAD_TWIN, 1, 0),
+    (HIDE, 0, 0),
+    (HIDE, 1, 0),
+    (BACK, 0, 0),
+    (BACK, 1, 0),
+    (GIVE, 0, 0),
+    (GIVE, 1, 0),
+    (FAR_BACK, 0, 0),
+    (GRADS_IN, 0, 0),
+    (MID, 0, 0),
+    (FAR_BACK, 1, 0),
+    (ATTEND_BACK, 0, 0),
+    (MID, 1, 0),
+    (PROJECT_BACK, 0, 0),
+    (GRADS_IN, 1, 0),
+    (ATTEND_BACK, 1, 0),
+    (CLOSE, 0, 0),
+    (GRADS_OUT, 0, 0),
+    (PROJECT_BACK, 1, 0),
+    (GRADS_OUT, 1, 0),
+    (CLOSE, 1, 0),
+    (FAR, 0, 0),
+    (FAR, 1, 0),
+    (JOIN, 0, 0),
+    (JOIN, 1, 0),
 )
 
 
@@ -169,8 +203,12 @@
     wg,
     wu,
     wd,
-    xpair,
-    n1s,
+    x_own,
+    n1p,
+    n1_send,
+    pq_own,
+    pq_send,
+    pq_recv,
     qkvs,
     att,
     hid_one,
@@ -231,7 +269,6 @@
     away = 1 - x
     other = 1 - f
     own_rows = aligned(f * SEQ, SEQ, 16)
-    other_rows = aligned(other * SEQ, SEQ, 16)
     own_half = aligned(f * HALF, HALF, 128)
     other_half = aligned(other * HALF, HALF, 128)
     partner = {"fsdp": other}
@@ -253,16 +290,19 @@
         twin,
         partner,
         {"section": 1 - sec},
-        {"section": 1 - sec, "fsdp": other},
         {"section": 1 - sec, "expert": twin_place},
     )
     for place in others:
         pl.semaphore_signal(barrier, inc=1, device_id=place, device_id_type=MESH)
 
-    local = [
-        (wq_in.at[:, own_half], wqkv.at[own_half, pl.ds(0, HALF)]),
-        (wk_in.at[:, aligned(f * HEAD, HEAD, 128)], wqkv.at[own_half, pl.ds(HALF, HEAD)]),
-        (wv_in.at[:, aligned(f * HEAD, HEAD, 128)], wqkv.at[own_half, pl.ds(HALF + HEAD, HEAD)]),
+    local = []
+    for g in range(2):
+        local += [
+            (wq_in.at[:, pl.ds(g * HALF, HALF)], wqkv.at[:, pl.ds(g * QKV, HALF)]),
+            (wk_in.at[:, pl.ds(g * HEAD, HEAD)], wqkv.at[:, pl.ds(g * QKV + HALF, HEAD)]),
+            (wv_in.at[:, pl.ds(g * HEAD, HEAD)], wqkv.at[:, pl.ds(g * QKV + HALF + HEAD, HEAD)]),
+        ]
+    local += [
         (wo_in, wo),
         (wg_in, wg.at[own_half]),
         (wu_in, wu.at[own_half]),
@@ -271,8 +311,8 @@
     local = [pltpu.make_async_copy(a, b, lw_sem.at[i]) for i, (a, b) in enumerate(local)]
     for copy in local:
         copy.start()
-    x_local = pltpu.make_async_copy(x_in, xpair.at[:, own_rows], lw_sem.at[7])
-    ct_local = pltpu.make_async_copy(ct_in, gpair.at[:, x], lw_sem.at[8])
+    x_local = pltpu.make_async_copy(x_in, x_own, lw_sem.at[10])
+    ct_local = pltpu.make_async_copy(ct_in, gpair.at[:, x], lw_sem.at[11])
     pl.when(first)(x_local.start)
     pl.when(second)(ct_local.start)
 
@@ -292,19 +332,6 @@
     def weight(src, dst, i):
         return remote(src, dst, ws_sem.at[i], wr_sem.at[i], partner)
 
-    w_attn = [
-        weight(wq_in.at[:, other_half], wqkv.at[own_half, pl.ds(0, HALF)], 0),
-        weight(
-            wk_in.at[:, aligned(other * HEAD, HEAD, 128)],
-            wqkv.at[own_half, pl.ds(HALF, HEAD)],
-            1,
-        ),
-        weight(
-            wv_in.at[:, aligned(other * HEAD, HEAD, 128)],
-            wqkv.at[own_half, pl.ds(HALF + HEAD, HEAD)],
-            2,
-        ),
-    ]
     w_moe = [
         weight(wg_in, wg.at[own_half], 3),
         weight(wu_in, wu.at[own_half], 4),
@@ -321,31 +348,18 @@
         for i in range(4)
     ]
 
-    def send_pieces(start, stop):
-        for copy in w_pieces[start:stop]:
-            copy.start()
-
-    def x_copy(m):
-        return weight(x_in.at[m], xpair.at[m, own_rows], 6 + m)
-
     def ct_copy(m):
         return remote(ct_in.at[m], gpair.at[m, x], ws_sem.at[10 + m], gr_sem.at[x, m], twin)
 
     side[f, 0:1] = gain_one_in[...].astype(F32)
     side[f, 1:2] = gain_two_in[...].astype(F32)
     side[f, 2:4, :SEQ] = segments_in[...].astype(F32)
+    for m in range(MB):
+        meta[x, m, 0:4] = ids_in[m].astype(F32)
+        meta[x, m, 4:8] = logits_in[m]
     row = lax.broadcasted_iota(jnp.int32, (SEQ, SEQ), 0)
     col = lax.broadcasted_iota(jnp.int32, (SEQ, SEQ), 1)
     unit = jnp.where(row == col, 1.0, 0.0).astype(BF)
-    for m in range(MB):
-        left = logits_in[m]
-        turned = jnp.zeros((4, SEQ), F32)
-        for _ in range(3):
-            high = left.astype(BF)
-            left = left - high.astype(F32)
-            turned = turned + dot_tn(high, unit)
-        meta[x, m, 0:4] = dot_tn(ids_in[m].astype(F32).astype(BF), unit)
-        meta[x, m, 4:8] = turned
     side_copy = weight(side.at[f], side.at[f], 8)
     meta_copy = remote(meta.at[x], meta.at[x], ws_sem.at[9], wr_sem.at[9], twin)
     gains_acc[...] = jnp.zeros_like(gains_acc)
@@ -353,13 +367,6 @@
     pl.semaphore_wait(barrier, PLANE - 1 + len(others))
     side_copy.start()
     meta_copy.start()
-
-    @pl.when(first)
-    def _():
-        x_copy(0).start()
-        for copy in w_attn:
-            copy.start()
-        x_copy(1).start()
 
     meta_copy.wait_recv()
     earlier = jnp.where(row < col, 1.0, 0.0).astype(BF)
@@ -449,11 +456,14 @@
     def far_copy(kind, m):
         return to_twin(kind, m, far_send.at[kind - 1, m], far_recv.at[kind - 1, m])
 
-    def acts_copy(m, cross):
-        place = {"section": 1, "fsdp": other} if cross else {"section": 1}
-        return remote(
-            acts_s.at[m], xpair.at[m, own_rows], xs_sem.at[cross, m], xr_sem.at[f, m], place
-        )
+    def acts_copy(m):
+        return remote(acts_s.at[m], x_own.at[m], xs_sem.at[m], xr_sem.at[m], {"section": 1})
+
+    def n1_copy(m):
+        return to_partner(4, m, n1_send.at[m], n1p.at[m, own_rows])
+
+    def pq_copy(m):
+        return to_partner(5, m, pq_send.at[m], pq_recv.at[m])
 
     def grad_copy(m, cross):
         place = {"section": 0, "expert": twin_place} if cross else {"section": 0}
@@ -478,8 +488,8 @@
 
     def load_step(m):
         pl.semaphore_wait(go_sem, 1)
-        for copy in w_attn:
-            copy.start()
+        ct_copy(0).start()
+        ct_copy(1).start()
 
     def heads_of(ref, m, rows):
         return jnp.concatenate(
@@ -493,44 +503,49 @@
         raised = jnp.exp(scores - jnp.max(scores, axis=-1, keepdims=True))
         return raised / jnp.sum(raised, axis=-1, keepdims=True)
 
-    def attend_step(m):
+    def enter_step(m):
+        pl.when(jnp.logical_and(first, m == 0))(x_local.wait)
+        pl.when(second)(lambda: wait_for(x_own.at[m], xr_sem.at[m]))
+        rows = x_own[m].astype(F32)
+        scale = inverse_rms(rows)
+        n1p[m, own_rows] = (x_own[m, :, own_half].astype(F32) * scale * gains[0:1, own_half]).astype(BF)
+        n1_send[m] = (
+            x_own[m, :, other_half].astype(F32) * scale * gains[0:1, other_half]
+        ).astype(BF)
+        n1_copy(m).start()
+
+    def project_step(m):
         @pl.when(m == 0)
         def _():
-            for copy in local[:4]:
+            for copy in local[:6]:
                 copy.wait()
-            for copy in w_attn:
-                copy.wait_recv()
-            for copy in w_attn:
-                copy.wait_send()
-            pl.when(first)(x_local.wait)
-
-            send_pieces(0, 1)
-
-            @pl.when(second)
-            def _():
-                ct_copy(0).start()
-                ct_copy(1).start()
-                send_pieces(1, 4)
-
-        @pl.when(first)
-        def _():
-            x_copy(m).wait_recv()
-
-        @pl.when(second)
-        def _():
-            for at, rows in ((f, own_rows), (other, other_rows)):
-                wait_for(xpair.at[m, rows], xr_sem.at[at, m])
-
-        rows = xpair[m].astype(F32)
-        n1s[m] = (rows * inverse_rms(rows) * gains[0:1]).astype(BF)
+
+        n1_copy(m).wait_recv()
+
+        @pl.loop(0, QKV // 512)
+        def _(j):
+            cols = aligned(j * 512, 512, 128)
+            from_w = aligned(other * QKV + j * 512, 512, 128)
+            pq_send[m, :, cols] = dot(n1p[m], wqkv[:, from_w]).astype(BF)
+
+        pq_copy(m).start()
+
+        @pl.loop(0, QKV // 512)
+        def _(j):
+            cols = aligned(j * 512, 512, 128)
+            from_w = aligned(f * QKV + j * 512, 512, 128)
+            pq_own[m, :, cols] = dot(n1p[m], wqkv[:, from_w])
+
+    def attend_step(m):
+        pl.when(m == 0)(local[6].wait)
+        pq_copy(m).wait_recv()
         cos, sin = cos_t[m], sin_t[m]
-        for j in range(4):
-            block = dot(n1s[m], wqkv[:, pl.ds(j * 256, 256)])
-            qkvs[m, :, pl.ds(j * 256, HEAD)] = rotate(block[:, :HEAD], cos, sin).astype(BF)
-            late = block[:, HEAD:]
-            if j < 3:
-                late = rotate(late, cos, sin)
-            qkvs[m, :, pl.ds(j * 256 + HEAD, HEAD)] = late.astype(BF)
+        for j in range(2 * HEADS - 4):
+            cols = pl.ds(j * HEAD, HEAD)
+            head = pq_own[m, :, cols] + pq_recv[m, :, cols].astype(F32)
+            if j <= HEADS:
+                head = rotate(head, cos, sin)
+            qkvs[m, :, cols] = head.astype(BF)
 
         @pl.loop(0, 2)
         def _(s):
@@ -553,17 +568,13 @@
             part_send[m, :, cols] = jnp.where(mine, low, top).astype(BF)
 
         to_partner(0, m, part_send.at[m], part_recv.at[m]).start()
-        pl.when(jnp.logical_and(first, m == 0))(lambda: send_pieces(1, 2))
-        pl.when(jnp.logical_and(first, m == 1))(lambda: send_pieces(2, 4))
 
     def norm_step(m):
         to_partner(0, m, part_send.at[m], part_recv.at[m]).wait_recv()
-        rows = xpair[m, own_rows].astype(F32) + (hid_one[m] + part_recv[m].astype(F32))
+        rows = x_own[m].astype(F32) + (hid_one[m] + part_recv[m].astype(F32))
         hid_one[m] = rows
         n2pair[m, x] = (rows * inverse_rms(rows) * gains[1:2]).astype(BF)
         n2_copy(m).start()
-        pl.when(m == 0)(lambda: send_pieces(4, 5))
-        pl.when(m == 1)(lambda: send_pieces(5, 12))
         spread(m, x, n2pair, dsend)
         exchange_half(0, m, dsend, n2recv, x)
 
@@ -575,7 +586,7 @@
     def hide_step(m):
         @pl.when(m == 0)
         def _():
-            for copy in local[4:6]:
+            for copy in local[7:9]:
                 copy.wait()
             for copy in w_moe[:2]:
                 copy.wait_recv()
@@ -595,7 +606,7 @@
 
 
     def need_down():
-        local[6].wait()
+        local[9].wait()
         w_moe[2].wait_recv()
         for copy in w_moe:
             copy.wait_send()
@@ -641,8 +652,7 @@
 
         @pl.when(first)
         def _():
-            for cross in (0, 1):
-                acts_copy(m, cross).start()
+            acts_copy(m).start()
 
         out_copy(3, acts_s.at[m], acts_out.at[m], m).start()
 
@@ -763,27 +773,29 @@
                 dqkv_all[m, f, at, pl.ds(h * HEAD, HEAD)] = part.astype(BF)
             dqkv_all[m, f, at, pl.ds(HALF, HEAD)] = dkeys.astype(BF)
             dqkv_all[m, f, at, pl.ds(HALF + HEAD, HEAD)] = dvalues.astype(BF)
-
-        @pl.loop(0, WIDTH // 512)
+            part = dqkv_all.at[m, f, at]
+            to_partner(3, m, part, part).start()
+
+    def project_back_step(m):
+        dqkv_copy(m).wait_recv()
+
+        @pl.loop(0, HALF // 256)
         def _(j):
-            cols = aligned(j * 512, 512, 128)
-            block = dot_nt(dqkv_all[m, f], wqkv[cols, :])
+            cols = aligned(j * 256, 256, 128)
+            block = dot_nt(dqkv_all[m, 0], wqkv[cols, pl.ds(0, QKV)])
+            block = block + dot_nt(dqkv_all[m, 1], wqkv[cols, pl.ds(QKV, QKV)])
             top, low = block[:SEQ], block[SEQ:]
             mine = f == 0
-            part_own[m, :, cols] = jnp.where(mine, top, low)
+            part_own[m, :, aligned(f * HALF + j * 256, 256, 128)] = jnp.where(mine, top, low)
             dn1_send[m, :, cols] = jnp.where(mine, low, top).astype(BF)
 
         dn1_copy(m).start()
-
-        @pl.when(m == 1)
-        def _():
-            dqkv_copy(0).start()
-            dqkv_copy(1).start()
 
     def close_step(m):
         dn1_copy(m).wait_recv()
-        grad = part_own[m] + dn1_recv[m].astype(F32)
-        rows = xpair[m, own_rows].astype(F32)
+        part_own[m, :, other_half] = dn1_recv[m].astype(F32)
+        grad = part_own[m]
+        rows = x_own[m].astype(F32)
         inverse = inverse_rms(rows)
         gains_acc[0:1] += jnp.sum(grad * rows * inverse, axis=0, keepdims=True)
         ingrad_s[m] = (dh_s[m] + rms_back(rows, inverse, gains[0:1], grad)).astype(BF)
@@ -840,6 +852,9 @@
     steps = {
         GRADS_IN: grads_in_step,
         GRADS_OUT: grads_out_step,
+        ENTER: enter_step,
+        PROJECT: project_step,
+        PROJECT_BACK: project_back_step,
         ATTEND: attend_step,
         NORM: norm_step,
         TWIN: twin_step,
@@ -857,24 +872,35 @@
         LOAD: load_step,
     }
     length = max(len(FIRST_PLAN), len(SECOND_PLAN))
-    plans = [plan + ((REST, 0),) * (length - len(plan)) for plan in (FIRST_PLAN, SECOND_PLAN)]
+    plans = [plan + ((REST, 0, 0),) * (length - len(plan)) for plan in (FIRST_PLAN, SECOND_PLAN)]
 
     @pl.loop(0, length)
     def _(i):
         code = jnp.int32(REST * MB)
-        for at, ((step_a, m_a), (step_b, m_b)) in enumerate(zip(*plans)):
+        for at, ((step_a, m_a, _), (step_b, m_b, _)) in enumerate(zip(*plans)):
             here = jnp.where(first, step_a * MB + m_a, step_b * MB + m_b)
             code = jnp.where(i == at, here, code)
         m = lax.rem(code, MB)
         for step, work in steps.items():
             pl.when(code // MB == step)(functools.partial(work, m))
+        for mine, plan in zip((first, second), plans):
+            start = 0
+            for at, (_, _, count) in enumerate(plan):
+                if count:
+                    part = w_pieces[start : start + count]
+
+                    @pl.when(jnp.logical_and(mine, i == at))
+                    def _():
+                        for copy in part:
+                            copy.start()
+
+                start += count
 
     gains_out[...] = gains_acc[...]
 
     @pl.loop(0, MB)
     def _(m):
-        dqkv_copy(m).wait_recv()
-        out_copy(8, n1s.at[m, :, own_half], n1_out.at[m], m).start()
+        out_copy(8, n1p.at[m], n1_out.at[m], m).start()
         out_copy(9, dqkv_all.at[m], dqkv_out.at[m], m).start()
         out_copy(10, att.at[m], att_out.at[m], m).start()
         sent(1, m, dsend)
@@ -883,15 +909,15 @@
         da_copy(m).wait_send()
         dn1_copy(m).wait_send()
         dqkv_copy(m).wait_send()
+        n1_copy(m).wait_send()
+        pq_copy(m).wait_send()
         n2_copy(m).wait_send()
         far_copy(1, m).wait_send()
         far_copy(2, m).wait_send()
 
         @pl.when(first)
         def _():
-            x_copy(m).wait_send()
-            for cross in (0, 1):
-                acts_copy(m, cross).wait_send()
+            acts_copy(m).wait_send()
 
         @pl.when(second)
         def _():
@@ -908,7 +934,7 @@
             (3, acts_s.at[m], acts_out.at[m]),
             (6, da_pair.at[m], da_out.at[m]),
             (7, ingrad_s.at[m], ingrad_out.at[m]),
-            (8, n1s.at[m, :, own_half], n1_out.at[m]),
+            (8, n1p.at[m], n1_out.at[m]),
             (9, dqkv_all.at[m], dqkv_out.at[m]),
             (10, att.at[m], att_out.at[m]),
         )
@@ -947,13 +973,17 @@
         in_specs=[anywhere] * 9 + [vmem] * 6,
         out_specs=[anywhere] * 2 + [vmem] + [anywhere] * 10,
         scratch_shapes=[
-            pltpu.VMEM((WIDTH, QKV), BF),
+            pltpu.VMEM((HALF, 2 * QKV), BF),
             pltpu.VMEM((HALF, WIDTH), BF),
             pltpu.VMEM((WIDTH, HIDDEN), BF),
             pltpu.VMEM((WIDTH, HIDDEN), BF),
             pltpu.VMEM((HIDDEN, WIDTH), BF),
-            pltpu.VMEM((MB, 2 * SEQ, WIDTH), BF),
-            pltpu.VMEM((MB, 2 * SEQ, WIDTH), BF),
+            pltpu.VMEM((MB, SEQ, WIDTH), BF),
+            pltpu.VMEM((MB, 2 * SEQ, HALF), BF),
+            pltpu.VMEM((MB, SEQ, HALF), BF),
+            pltpu.VMEM((MB, 2 * SEQ, QKV), F32),
+            pltpu.VMEM((MB, 2 * SEQ, QKV), BF),
+            pltpu.VMEM((MB, 2 * SEQ, QKV), BF),
             pltpu.VMEM((MB, 2 * SEQ, QKV), BF),
             pltpu.VMEM((MB, 2 * SEQ, HALF), BF),
             pltpu.VMEM((MB, SEQ, WIDTH), F32),
@@ -980,8 +1010,8 @@
             pltpu.VMEM((MB, SEQ, WIDTH), F32),
             pltpu.VMEM((MB, 2 * SEQ, WIDTH), BF),
             pltpu.VMEM((MB, 2, 2 * SEQ, QKV), BF),
-            pltpu.VMEM((MB, SEQ, WIDTH), BF),
-            pltpu.VMEM((MB, SEQ, WIDTH), BF),
+            pltpu.VMEM((MB, SEQ, HALF), BF),
+            pltpu.VMEM((MB, SEQ, HALF), BF),
             pltpu.VMEM((MB, SEQ, WIDTH), BF),
             pltpu.VMEM((8, WIDTH), F32),
             pltpu.VMEM((2, 8, HALF), F32),
@@ -990,17 +1020,17 @@
             pltpu.VMEM((MB, 2 * SEQ, HEAD), F32),
             pltpu.VMEM((MB, 2 * SEQ, HEAD), F32),
             pltpu.VMEM((MB, 2, SEQ, SEQ), F32),
-            dma((9,)),
+            dma((12,)),
             dma((12,)),
             dma((10,)),
             dma((4, MB)),
             dma((4, MB)),
-            dma((4, MB)),
-            dma((4, MB)),
+            dma((6, MB)),
+            dma((6, MB)),
             dma((3, MB)),
             dma((3, MB)),
-            dma((2, MB)),
-            dma((2, MB)),
+            dma((MB,)),
+            dma((MB,)),
             dma((2, MB)),
             dma((2, MB)),
             dma((11, MB)),
@@ -1449,8 +1479,8 @@
         gain_attn,
         gain_moe,
         segments,
-        expert_ids[0],
-        gate_logits[0],
+        jnp.swapaxes(expert_ids[0], 1, 2),
+        jnp.swapaxes(gate_logits[0], 1, 2),
         jnp.asarray(frequency),
     )
     gq, gk, gv, go, part_gate, part_up, part_down, gains = reduce_grads(

time: 422 us -> 405 us (0.960)
  Pallas kernels: 418 us -> 404 us
    pallas_call x1, Pallas kernels: 333 us -> 316 us  [run_sections(): pl.pallas_call(section_kernel, name='sections', out_shape=(out(MB, SEQ, W...]
where the time goes in v5:
time: 405 us; the launch traced here: 404 us
  Pallas kernels  404 us (100%)
    pallas_call x1, Pallas kernels, run_sections(): pl.pallas_call(section_kernel, name='sections', out_shape=(out(MB, SEQ, W...  316 us
    pallas_call x1, Pallas kernels, reduce_grads(): pl.pallas_call(grads_kernel, name='grads', out_shape=(out(HALF, WIDTH), o...  75.4 us
    pallas_call x1, Pallas kernels, finish(): pl.pallas_call(finish_kernel, name='finish', grid=(steps,), out_shape=[ja...  12.1 us

profile of v5, /device:TPU:0, one launch (start us, length us, event | category | flops | bytes accessed | tf_op | source)
XLA Modules:
  0.0 404.5 jit_solution(5901641497137407360)
XLA Ops:
  0.6 316.1 %sections.1 = (bf16[2,96,1536]{2,1,0:T(8,128)(2,1)}, bf16[2,96,1536]{2,1,0:T(8,128)(2,1)}, f32[8,1536]{1,0:T(8,128)}, bf16[768,768]{1,0:T(8,128)(2,1)}, bf16[768...) custom-call(bf16[2,96,1536]{2,1,0:T(8,128)(2,1)} %x_in.1, ...), custom_call_target="tpu_custom_call" | custom-call | tf_op jit(solution)/shard_map/sections/pallas_call | solution.py:955
  316.8 75.4 %grads.1 = (bf16[768,1536]{1,0:T(8,128)(2,1)}, bf16[768,256]{1,0:T(8,128)(2,1)}, bf16[768,256]{1,0:T(8,128)(2,1)}, bf16[768,1536]{1,0:T(8,128)(2,1)}, bf16[768,7...) custom-call(bf16[768,768]{1,0:T(8,128)(2,1)} %get-tuple-element.43.their_gate, ...), custom_call_target="tpu_custom_call" | custom-call | tf_op jit(solution)/shard_map/grads/pallas_call | solution.py:1357
  392.2 12.1 %finish.1 = (f32[768,1536]{1,0:T(8,128)}, f32[768,256]{1,0:T(8,128)}, f32[768,256]{1,0:T(8,128)}, f32[768,1536]{1,0:T(8,128)}, f32[768,768]{1,0:T(8,128)}, /*ind...) custom-call(bf16[768,1536]{1,0:T(8,128)(2,1)} %get-tuple-element.51., ...), custom_call_target="tpu_custom_call" | custom-call | tf_op jit(solution)/shard_map/finish/pallas_call | solution.py:1425

commit v6 on v5

--- a/solution.py
+++ b/solution.py
@@ -81,10 +81,14 @@
     PROJECT_BACK,
     CLOSE,
     LOAD,
-    GRADS_IN,
-    GRADS_OUT,
+    IN_A,
+    IN_B,
+    IN_C,
+    OUT_A,
+    OUT_B,
+    OUT_C,
     REST,
-) = range(21)
+) = range(25)
 
 FIRST_PLAN = (
     (ENTER, 0, 0),
@@ -111,19 +115,27 @@
     (GRAD_TWIN, 1, 0),
     (BACK, 0, 0),
     (BACK, 1, 0),
-    (GRADS_IN, 0, 0),
+    (IN_A, 0, 0),
+    (IN_B, 0, 0),
+    (IN_C, 0, 0),
     (FAR_BACK, 0, 0),
-    (GRADS_IN, 1, 0),
+    (IN_A, 1, 0),
+    (IN_B, 1, 0),
     (MID, 0, 0),
-    (GRADS_OUT, 0, 0),
+    (IN_C, 1, 0),
+    (OUT_A, 0, 0),
+    (OUT_B, 0, 0),
     (FAR_BACK, 1, 0),
     (ATTEND_BACK, 0, 0),
     (MID, 1, 0),
+    (OUT_C, 0, 0),
     (PROJECT_BACK, 0, 0),
-    (GRADS_OUT, 1, 0),
+    (OUT_A, 1, 0),
     (ATTEND_BACK, 1, 0),
     (CLOSE, 0, 0),
+    (OUT_B, 1, 0),
     (PROJECT_BACK, 1, 0),
+    (OUT_C, 1, 0),
     (CLOSE, 1, 0),
 )
 SECOND_PLAN = (
@@ -149,19 +161,27 @@
     (GIVE, 0, 0),
     (GIVE, 1, 0),
     (FAR_BACK, 0, 0),
-    (GRADS_IN, 0, 0),
     (MID, 0, 0),
     (FAR_BACK, 1, 0),
     (ATTEND_BACK, 0, 0),
     (MID, 1, 0),
     (PROJECT_BACK, 0, 0),
-    (GRADS_IN, 1, 0),
     (ATTEND_BACK, 1, 0),
     (CLOSE, 0, 0),
-    (GRADS_OUT, 0, 0),
     (PROJECT_BACK, 1, 0),
-    (GRADS_OUT, 1, 0),
     (CLOSE, 1, 0),
+    (IN_A, 0, 0),
+    (IN_B, 0, 0),
+    (IN_C, 0, 0),
+    (IN_A, 1, 0),
+    (IN_B, 1, 0),
+    (IN_C, 1, 0),
+    (OUT_A, 0, 0),
+    (OUT_B, 0, 0),
+    (OUT_C, 0, 0),
+    (OUT_A, 1, 0),
+    (OUT_B, 1, 0),
+    (OUT_C, 1, 0),
     (FAR, 0, 0),
     (FAR, 1, 0),
     (JOIN, 0, 0),
@@ -548,7 +568,8 @@
             qkvs[m, :, cols] = head.astype(BF)
 
         @pl.loop(0, 2)
-        def _(s):
+        def _(i):
+            s = jnp.where(i == 0, other, f)
             at = aligned(s * SEQ, SEQ, 16)
             queries = heads_of(qkvs, m, at)
             keys = qkvs[m, at, pl.ds(HALF, HEAD)]
@@ -558,16 +579,20 @@
             for h in range(HEADS):
                 att[m, at, pl.ds(h * HEAD, HEAD)] = mixed[h * SEQ : (h + 1) * SEQ]
 
-        @pl.loop(0, WIDTH // 512)
-        def _(j):
-            cols = aligned(j * 512, 512, 128)
-            block = dot(att[m], wo[:, cols])
-            top, low = block[:SEQ], block[SEQ:]
-            mine = f == 0
-            hid_one[m, :, cols] = jnp.where(mine, top, low)
-            part_send[m, :, cols] = jnp.where(mine, low, top).astype(BF)
-
-        to_partner(0, m, part_send.at[m], part_recv.at[m]).start()
+            @pl.loop(0, WIDTH // 512)
+            def _(j):
+                cols = aligned(j * 512, 512, 128)
+                block = dot(att[m, at], wo[:, cols])
+
+                @pl.when(i == 0)
+                def _():
+                    part_send[m, :, cols] = block.astype(BF)
+
+                @pl.when(i == 1)
+                def _():
+                    hid_one[m, :, cols] = block
+
+            pl.when(i == 0)(to_partner(0, m, part_send.at[m], part_recv.at[m]).start)
 
     def norm_step(m):
         to_partner(0, m, part_send.at[m], part_recv.at[m]).wait_recv()
@@ -713,6 +738,11 @@
     def far_back_step(m):
         received(3, m, dn2recv)
 
+        @pl.when(jnp.logical_and(first, m == 1))
+        def _():
+            pl.semaphore_signal(go_sem, inc=1, device_id={"section": 1}, device_id_type=MESH)
+
+
         @pl.loop(0, WIDTH // 512)
         def _(j):
             cols = aligned(j * 512, 512, 128)
@@ -746,11 +776,15 @@
         return to_partner(2, m, dn1_send.at[m], dn1_recv.at[m])
 
     def attend_back_step(m):
-        da_copy(m).wait_recv()
-        out_copy(6, da_pair.at[m], da_out.at[m], m).start()
-
         @pl.loop(0, 2)
-        def _(s):
+        def _(i):
+            s = jnp.where(i == 0, f, other)
+
+            @pl.when(i == 1)
+            def _():
+                da_copy(m).wait_recv()
+                out_copy(6, da_pair.at[m], da_out.at[m], m).start()
+
             at = aligned(s * SEQ, SEQ, 16)
             dmix = dot_nt(da_pair[m, at], wo[...]).astype(BF)
             dmix = jnp.concatenate(
@@ -779,17 +813,25 @@
     def project_back_step(m):
         dqkv_copy(m).wait_recv()
 
-        @pl.loop(0, HALF // 256)
-        def _(j):
-            cols = aligned(j * 256, 256, 128)
-            block = dot_nt(dqkv_all[m, 0], wqkv[cols, pl.ds(0, QKV)])
-            block = block + dot_nt(dqkv_all[m, 1], wqkv[cols, pl.ds(QKV, QKV)])
-            top, low = block[:SEQ], block[SEQ:]
-            mine = f == 0
-            part_own[m, :, aligned(f * HALF + j * 256, 256, 128)] = jnp.where(mine, top, low)
-            dn1_send[m, :, cols] = jnp.where(mine, low, top).astype(BF)
-
-        dn1_copy(m).start()
+        @pl.loop(0, 2)
+        def _(i):
+            at = aligned(jnp.where(i == 0, other, f) * SEQ, SEQ, 16)
+
+            @pl.loop(0, HALF // 256)
+            def _(j):
+                cols = aligned(j * 256, 256, 128)
+                block = dot_nt(dqkv_all[m, 0, at], wqkv[cols, pl.ds(0, QKV)])
+                block = block + dot_nt(dqkv_all[m, 1, at], wqkv[cols, pl.ds(QKV, QKV)])
+
+                @pl.when(i == 0)
+                def _():
+                    dn1_send[m, :, cols] = block.astype(BF)
+
+                @pl.when(i == 1)
+                def _():
+                    part_own[m, :, aligned(f * HALF + j * 256, 256, 128)] = block
+
+            pl.when(i == 0)(dn1_copy(m).start)
 
     def close_step(m):
         dn1_copy(m).wait_recv()
@@ -827,31 +869,30 @@
         pl.when(m == f)(own.start)
         pl.when(m != f)(their.start)
 
-    def grads_in_step(m):
-        @pl.loop(0, 3)
-        def _(j):
-            cols = aligned(m * half_rows + j * 256, 256, 128)
-            rows = n2recv[:, :, :, :, cols].reshape(MB * ROWS, 256)
-            wg[cols, :] = dot_tn(rows, gs[...].reshape(MB * ROWS, HIDDEN)).astype(BF)
-            wu[cols, :] = dot_tn(rows, us[...].reshape(MB * ROWS, HIDDEN)).astype(BF)
-
-        start_out(0, m)
-        start_out(1, m)
-
-    def grads_out_step(m):
+    def grads_in_step(j, m):
+        cols = aligned(m * half_rows + j * 256, 256, 128)
+        rows = n2recv[:, :, :, :, cols].reshape(MB * ROWS, 256)
+        wg[cols, :] = dot_tn(rows, gs[...].reshape(MB * ROWS, HIDDEN)).astype(BF)
+        wu[cols, :] = dot_tn(rows, us[...].reshape(MB * ROWS, HIDDEN)).astype(BF)
+        if j == 2:
+            start_out(0, m)
+            start_out(1, m)
+
+    def grads_out_step(j, m):
         cols = aligned(m * quarter_rows, quarter_rows, 128)
-
-        @pl.loop(0, 3)
-        def _(j):
-            at = aligned(j * 512, 512, 128)
-            rows = dyrecv[:, :, :, :, at].reshape(MB * ROWS, 512)
-            wd[cols, at] = dot_tn(hid[:, :, cols].reshape(MB * ROWS, quarter_rows), rows).astype(BF)
-
-        start_out(2, m)
+        at = pl.ds(j * 512, 512)
+        rows = dyrecv[:, :, :, :, at].reshape(MB * ROWS, 512)
+        wd[cols, at] = dot_tn(hid[:, :, cols].reshape(MB * ROWS, quarter_rows), rows).astype(BF)
+        if j == 2:
+            start_out(2, m)
 
     steps = {
-        GRADS_IN: grads_in_step,
-        GRADS_OUT: grads_out_step,
+        IN_A: functools.partial(grads_in_step, 0),
+        IN_B: functools.partial(grads_in_step, 1),
+        IN_C: functools.partial(grads_in_step, 2),
+        OUT_A: functools.partial(grads_out_step, 0),
+        OUT_B: functools.partial(grads_out_step, 1),
+        OUT_C: functools.partial(grads_out_step, 2),
         ENTER: enter_step,
         PROJECT: project_step,
         PROJECT_BACK: project_back_step,
@@ -895,6 +936,8 @@
                             copy.start()
 
                 start += count
+
+    pl.when(second)(lambda: pl.semaphore_wait(go_sem, 1))
 
     gains_out[...] = gains_acc[...]
 
@@ -1070,7 +1113,7 @@
     da,
     *rest,
 ):
-    lane_refs, rest = [rest[i * 7 : i * 7 + 7] for i in range(len(LANES))], rest[7 * len(LANES) :]
+    lane_refs, rest = [rest[i * 9 : i * 9 + 9] for i in range(len(LANES))], rest[9 * len(LANES) :]
     (
         small,
         small_recv,
@@ -1131,13 +1174,23 @@
     class Lane:
         def __init__(self, i):
             self.i = i
-            self.v, self.r1, self.s1, self.r2, self.s2, self.r3, self.g = lane_refs[i]
+            self.v, self.far, self.merged, self.r1, self.s1, self.r2, self.s2, self.r3, self.g = (
+                lane_refs[i]
+            )
             axes = ((along_y, y), (along_z, z))
-            (self.axis, self.at), (self.next, self.to) = axes if LANES[i][0] == "y" else axes[::-1]
+            (axis, at), (self.next, self.to) = axes if LANES[i][0] == "y" else axes[::-1]
+            self.right, self.left = axis(1), axis(3)
+            self.at = at
             half = LANES[i][1] // 2
             self.mine = aligned(x * half, half, 128)
             self.theirs = aligned((1 - x) * half, half, 128)
-            self.place = aligned(self.at * BAND + self.to * SLICE, SLICE, 16)
+            self.place = aligned(at * BAND + self.to * SLICE, SLICE, 16)
+
+        def rows(self, distance, part=None):
+            start = lax.rem(self.at + distance, 4) * BAND
+            if part is None:
+                return aligned(start, BAND, 16)
+            return aligned(start + part * (BAND // 2), BAND // 2, 16)
 
         def send(self, stage, src, dst, place):
             remote(
@@ -1148,57 +1201,84 @@
             wait_for(ref, recv_sem.at[self.i, stage])
 
         def spread(self):
-            for d in (1, 2, 3):
-                rows = aligned(lax.rem(self.at + d, 4) * BAND, BAND, 16)
-                self.send(0, self.v.at[rows], self.r1.at[self.at], self.axis(d))
+            low = pl.ds(BAND // 2, BAND // 2)
+            top = pl.ds(0, BAND // 2)
+            self.send(0, self.v.at[self.rows(2, 0)], self.far.at[0], self.right)
+            self.send(1, self.v.at[self.rows(2, 1)], self.far.at[1], self.left)
+            self.send(2, self.v.at[self.rows(1, 1)], self.r1.at[0, low], self.right)
+            self.send(3, self.v.at[self.rows(3, 0)], self.r1.at[1, top], self.left)
+
+        def merge(self):
+            low = pl.ds(BAND // 2, BAND // 2)
+            top = pl.ds(0, BAND // 2)
+            self.arrived(0, self.far.at[0])
+            total = self.v[self.rows(1, 0)].astype(F32) + self.far[0].astype(F32)
+            self.merged[0] = total.astype(BF)
+            self.send(2, self.merged.at[0], self.r1.at[0, top], self.right)
+            self.arrived(1, self.far.at[1])
+            total = self.v[self.rows(3, 1)].astype(F32) + self.far[1].astype(F32)
+            self.merged[1] = total.astype(BF)
+            self.send(3, self.merged.at[1], self.r1.at[1, low], self.left)
 
         def join_one(self):
-            self.arrived(0, self.r1.at[pl.ds(0, 3)])
-            total = self.v[aligned(self.at * BAND, BAND, 16)].astype(F32)
-            for d in (1, 2, 3):
-                total = total + self.r1[lax.rem(self.at + d, 4)].astype(F32)
+            self.arrived(2, self.r1.at[0])
+            self.arrived(3, self.r1.at[1])
+            total = self.v[self.rows(0)].astype(F32)
+            total = total + self.r1[0].astype(F32) + self.r1[1].astype(F32)
             self.s1[...] = total.astype(BF)
             for d in (1, 2, 3):
                 rows = aligned(lax.rem(self.to + d, 4) * SLICE, SLICE, 16)
-                self.send(1, self.s1.at[rows], self.r2.at[self.to], self.next(d))
+                self.send(4, self.s1.at[rows], self.r2.at[self.to], self.next(d))
 
         def join_two(self):
-            self.arrived(1, self.r2.at[pl.ds(0, 3)])
+            self.arrived(4, self.r2.at[pl.ds(0, 3)])
             total = self.s1[aligned(self.to * SLICE, SLICE, 16)].astype(F32)
             for d in (1, 2, 3):
                 total = total + self.r2[lax.rem(self.to + d, 4)].astype(F32)
             self.s2[...] = total.astype(BF)
-            self.send(2, self.s2.at[:, self.theirs], self.r3, twin)
+            self.send(5, self.s2.at[:, self.theirs], self.r3, twin)
 
         def join_three(self):
-            self.arrived(2, self.r3)
+            self.arrived(5, self.r3)
             total = self.s2[:, self.mine].astype(F32) + self.r3[...].astype(F32)
             self.g[self.place, self.mine] = total.astype(BF)
             part = self.g.at[self.place, self.mine]
-            self.send(3, part, part, twin)
+            self.send(6, part, part, twin)
 
         def gather_two(self):
-            self.arrived(3, self.g.at[self.place, self.theirs])
+            self.arrived(6, self.g.at[self.place, self.theirs])
             part = self.g.at[self.place]
             for d in (1, 2, 3):
-                self.send(4, part, part, self.next(d))
+                self.send(7, part, part, self.next(d))
 
         def gather_one(self):
-            self.arrived(4, self.g.at[pl.ds(0, 3 * SLICE)])
-            part = self.g.at[aligned(self.at * BAND, BAND, 16)]
-            for d in (1, 2, 3):
-                self.send(5, part, part, self.axis(d))
+            self.arrived(7, self.g.at[pl.ds(0, 3 * SLICE)])
+            top, low = self.g.at[self.rows(0, 0)], self.g.at[self.rows(0, 1)]
+            self.send(8, top, top, self.right)
+            self.send(9, low, low, self.left)
+            self.send(10, low, low, self.right)
+            self.send(11, top, top, self.left)
+
+        def pass_on(self):
+            top, low = self.g.at[self.rows(3, 0)], self.g.at[self.rows(1, 1)]
+            self.arrived(8, top)
+            self.send(12, top, top, self.right)
+            self.arrived(9, low)
+            self.send(13, low, low, self.left)
 
         def finish(self):
-            self.arrived(5, self.g.at[pl.ds(0, 3 * BAND)])
+            part = self.g.at[pl.ds(0, BAND // 2)]
+            for stage in (10, 11, 12, 13):
+                self.arrived(stage, part)
 
         def drain(self):
-            wait_for(self.v.at[pl.ds(0, 3 * BAND)], send_sem.at[self.i, 0])
-            wait_for(self.s1.at[pl.ds(0, 3 * SLICE)], send_sem.at[self.i, 1])
-            wait_for(self.s2.at[:, self.theirs], send_sem.at[self.i, 2])
-            wait_for(self.g.at[self.place, self.mine], send_sem.at[self.i, 3])
-            wait_for(self.g.at[pl.ds(0, 3 * SLICE)], send_sem.at[self.i, 4])
-            wait_for(self.g.at[pl.ds(0, 3 * BAND)], send_sem.at[self.i, 5])
+            half = self.v.at[pl.ds(0, BAND // 2)]
+            band = self.v.at[pl.ds(0, BAND)]
+            slices = self.v.at[pl.ds(0, 3 * SLICE)]
+            sizes = [half, half, band, band, slices, self.s2.at[:, self.theirs]]
+            sizes += [self.g.at[self.place, self.mine], slices] + [half] * 6
+            for stage, ref in enumerate(sizes):
+                wait_for(ref, send_sem.at[self.i, stage])
 
     out_one, query_one, out_two, query_two = lanes = [Lane(i) for i in range(len(LANES))]
 
@@ -1287,6 +1367,8 @@
     join_small(0, along_y)
     spread_small(1, along_z)
     for lane in lanes:
+        lane.merge()
+    for lane in lanes:
         lane.join_one()
     for lane in lanes:
         lane.join_two()
@@ -1307,6 +1389,8 @@
         lane.gather_two()
     for lane in lanes:
         lane.gather_one()
+    for lane in lanes:
+        lane.pass_on()
     small_twin.wait()
     gains_out[...] = small[:, pl.ds(0, HALF)] + small_recv[7]
 
@@ -1347,7 +1431,9 @@
     for _, width in LANES:
         lanes += [
             pltpu.VMEM((HALF, width), BF),
-            pltpu.VMEM((4, BAND, width), BF),
+            pltpu.VMEM((2, BAND // 2, width), BF),
+            pltpu.VMEM((2, BAND // 2, width), BF),
+            pltpu.VMEM((2, BAND, width), BF),
             pltpu.VMEM((BAND, width), BF),
             pltpu.VMEM((4, SLICE, width), BF),
             pltpu.VMEM((SLICE, width), BF),
@@ -1380,8 +1466,8 @@
             pltpu.VMEM((8, WIDTH), F32),
             pltpu.VMEM((8, 8, HALF), F32),
             dma((4,)),
-            dma((len(LANES), 6)),
-            dma((len(LANES), 6)),
+            dma((len(LANES), 14)),
+            dma((len(LANES), 14)),
             dma((3,)),
             dma((3,)),
             dma((8,)),
@@ -1410,7 +1496,7 @@
 
 
 def finish(*blocks):
-    steps = 6
+    steps = 4
 
     def spec(rows, cols):
         return pl.BlockSpec((rows // steps, cols), lambda i: (i, 0))

time: 405 us -> 392 us (0.968)
  Pallas kernels: 404 us -> 391 us
    pallas_call x1, Pallas kernels: 316 us -> 308 us  [run_sections(): pl.pallas_call(section_kernel, name='sections', out_shape=(out(MB, SEQ, W...]
    pallas_call x1, Pallas kernels: 75.4 us -> 70.9 us  [reduce_grads(): pl.pallas_call(grads_kernel, name='grads', out_shape=(out(HALF, WIDTH), o...]
where the time goes in v6:
time: 392 us
  Pallas kernels  391 us (100%)
    pallas_call x1, Pallas kernels, run_sections(): pl.pallas_call(section_kernel, name='sections', out_shape=(out(MB, SEQ, W...  308 us
    pallas_call x1, Pallas kernels, reduce_grads(): pl.pallas_call(grads_kernel, name='grads', out_shape=(out(HALF, WIDTH), o...  70.9 us
    pallas_call x1, Pallas kernels, finish(): pl.pallas_call(finish_kernel, name='finish', grid=(steps,), out_shape=[ja...  12.2 us

profile of v6, /device:TPU:0, one launch (start us, length us, event | category | flops | bytes accessed | tf_op | source)
XLA Modules:
  0.0 391.8 jit_solution(15895180690182816852)
XLA Ops:
  0.6 307.9 %sections.1 = (bf16[2,96,1536]{2,1,0:T(8,128)(2,1)}, bf16[2,96,1536]{2,1,0:T(8,128)(2,1)}, f32[8,1536]{1,0:T(8,128)}, bf16[768,768]{1,0:T(8,128)(2,1)}, bf16[768...) custom-call(bf16[2,96,1536]{2,1,0:T(8,128)(2,1)} %x_in.1, ...), custom_call_target="tpu_custom_call" | custom-call | tf_op jit(solution)/shard_map/sections/pallas_call | solution.py:998
  308.6 70.9 %grads.1 = (bf16[768,1536]{1,0:T(8,128)(2,1)}, bf16[768,256]{1,0:T(8,128)(2,1)}, bf16[768,256]{1,0:T(8,128)(2,1)}, bf16[768,1536]{1,0:T(8,128)(2,1)}, bf16[768,7...) custom-call(bf16[768,768]{1,0:T(8,128)(2,1)} %get-tuple-element.43.their_gate, ...), custom_call_target="tpu_custom_call" | custom-call | tf_op jit(solution)/shard_map/grads/pallas_call | solution.py:1443
  379.4 12.2 %finish.1 = (f32[768,1536]{1,0:T(8,128)}, f32[768,256]{1,0:T(8,128)}, f32[768,256]{1,0:T(8,128)}, f32[768,1536]{1,0:T(8,128)}, f32[768,768]{1,0:T(8,128)}, /*ind...) custom-call(bf16[768,1536]{1,0:T(8,128)(2,1)} %get-tuple-element.51., ...), custom_call_target="tpu_custom_call" | custom-call | tf_op jit(solution)/shard_map/finish/pallas_call | solution.py:1511

commit v7 on v6

--- a/solution.py
+++ b/solution.py
@@ -74,7 +74,8 @@
     JOIN,
     GRAD,
     GRAD_TWIN,
-    BACK,
+    BACK_NEAR,
+    BACK_FAR,
     FAR_BACK,
     MID,
     ATTEND_BACK,
@@ -88,7 +89,7 @@
     OUT_B,
     OUT_C,
     REST,
-) = range(25)
+) = range(26)
 
 FIRST_PLAN = (
     (ENTER, 0, 0),
@@ -112,52 +113,56 @@
     (GRAD, 0, 0),
     (GRAD_TWIN, 0, 0),
     (GRAD, 1, 0),
+    (BACK_NEAR, 0, 0),
     (GRAD_TWIN, 1, 0),
-    (BACK, 0, 0),
-    (BACK, 1, 0),
+    (BACK_FAR, 0, 0),
+    (BACK_FAR, 1, 0),
+    (BACK_NEAR, 1, 0),
+    (FAR_BACK, 0, 0),
     (IN_A, 0, 0),
     (IN_B, 0, 0),
     (IN_C, 0, 0),
-    (FAR_BACK, 0, 0),
+    (MID, 0, 0),
     (IN_A, 1, 0),
     (IN_B, 1, 0),
-    (MID, 0, 0),
-    (IN_C, 1, 0),
-    (OUT_A, 0, 0),
-    (OUT_B, 0, 0),
     (FAR_BACK, 1, 0),
     (ATTEND_BACK, 0, 0),
     (MID, 1, 0),
-    (OUT_C, 0, 0),
+    (IN_C, 1, 0),
+    (OUT_A, 0, 0),
     (PROJECT_BACK, 0, 0),
-    (OUT_A, 1, 0),
+    (OUT_B, 0, 0),
     (ATTEND_BACK, 1, 0),
     (CLOSE, 0, 0),
+    (OUT_C, 0, 0),
+    (OUT_A, 1, 0),
+    (PROJECT_BACK, 1, 0),
     (OUT_B, 1, 0),
-    (PROJECT_BACK, 1, 0),
     (OUT_C, 1, 0),
     (CLOSE, 1, 0),
 )
 SECOND_PLAN = (
     (GRAD, 0, 0),
     (GRAD, 1, 0),
-    (LOAD, 0, 5),
+    (LOAD, 0, 3),
     (ENTER, 0, 0),
     (PROJECT, 0, 1),
-    (ENTER, 1, 1),
+    (ENTER, 1, 0),
     (ATTEND, 0, 1),
-    (PROJECT, 1, 1),
+    (PROJECT, 1, 0),
     (NORM, 0, 1),
     (ATTEND, 1, 1),
     (TWIN, 0, 0),
-    (NORM, 1, 1),
+    (NORM, 1, 5),
     (TWIN, 1, 0),
     (GRAD_TWIN, 0, 0),
     (GRAD_TWIN, 1, 0),
     (HIDE, 0, 0),
     (HIDE, 1, 0),
-    (BACK, 0, 0),
-    (BACK, 1, 0),
+    (BACK_FAR, 0, 0),
+    (BACK_NEAR, 0, 0),
+    (BACK_FAR, 1, 0),
+    (BACK_NEAR, 1, 0),
     (GIVE, 0, 0),
     (GIVE, 1, 0),
     (FAR_BACK, 0, 0),
@@ -441,28 +446,18 @@
             remote(
                 src.at[m, at, source],
                 dst.at[m, q, source],
-                as_sem.at[kind, m],
-                ar_sem.at[kind, m],
+                as_sem.at[kind, m, source],
+                ar_sem.at[kind, m, source],
                 place,
             ).start()
 
         dst[m, q, source] = src[m, q, source]
 
-    def exchange(kind, m, src, dst):
-        @pl.loop(1, PLANE)
-        def _(d):
-            at, place = in_plane(d)
-            remote(
-                src.at[m, at], dst.at[m, q], as_sem.at[kind, m], ar_sem.at[kind, m], place
-            ).start()
-
-        dst[m, q] = src[m, q]
-
-    def received(kind, m, dst):
-        wait_for(dst.at[m, pl.ds(0, PLANE - 1)], ar_sem.at[kind, m])
-
-    def sent(kind, m, src):
-        wait_for(src.at[m, pl.ds(0, PLANE - 1)], as_sem.at[kind, m])
+    def received(kind, m, dst, source):
+        wait_for(dst.at[m, pl.ds(0, PLANE - 1), source], ar_sem.at[kind, m, source])
+
+    def sent(kind, m, src, source):
+        wait_for(src.at[m, pl.ds(0, PLANE - 1), source], as_sem.at[kind, m, source])
 
     def to_partner(kind, m, src, dst):
         return remote(src, dst, ps_sem.at[kind, m], pr_sem.at[kind, m], partner)
@@ -616,7 +611,8 @@
             for copy in w_moe[:2]:
                 copy.wait_recv()
 
-        received(0, m, n2recv)
+        for source in range(2):
+            received(0, m, n2recv, source)
 
         @pl.loop(0, HIDDEN // 256)
         def _(j):
@@ -625,9 +621,11 @@
             gate = dot(rows, wg[:, cols])
             up = dot(rows, wu[:, cols])
             bend = jnp.tanh(GELU_C * (gate + GELU_A * gate * gate * gate))
-            gs[m, :, cols] = gate.astype(BF)
-            us[m, :, cols] = up.astype(BF)
-            hid[m, :, cols] = (0.5 * gate * (1.0 + bend) * up).astype(BF)
+            shape = (PLANE, 2, SLOTS, 256)
+            gs[m, :, :, :, cols] = gate.astype(BF).reshape(shape)
+            us[m, :, :, :, cols] = up.astype(BF).reshape(shape)
+            mixed = (0.5 * gate * (1.0 + bend) * up).astype(BF)
+            hid[m, :, :, :, cols] = mixed.reshape(shape)
 
 
     def need_down():
@@ -642,22 +640,26 @@
             need_down()
             pl.semaphore_signal(go_sem, inc=1, device_id={"section": 1}, device_id_type=MESH)
 
-        sent(0, m, dsend)
-
-        @pl.loop(0, WIDTH // 512)
-        def _(j):
-            cols = aligned(j * 512, 512, 128)
-            block = dot(hid[m], wd[:, cols]).astype(BF)
-            dsend[m, :, :, :, cols] = block.reshape(PLANE, 2, SLOTS, 512)
-
-        exchange(1, m, dsend, yrecv)
+        @pl.loop(0, 2)
+        def _(i):
+            source = jnp.where(i == 0, away, x)
+            sent(0, m, dsend, source)
+            rows = hid[m, :, source].reshape(PLANE * SLOTS, HIDDEN)
+
+            @pl.loop(0, WIDTH // 512)
+            def _(j):
+                cols = aligned(j * 512, 512, 128)
+                block = dot(rows, wd[:, cols]).astype(BF)
+                dsend[m, :, source, :, cols] = block.reshape(PLANE, SLOTS, 512)
+
+            exchange_half(1, m, dsend, yrecv, source)
 
     def weighed(m, source, cols):
         block = yrecv[m, :, source, :, cols].reshape(PLANE * SLOTS, 512)
         return dot_tn(cg_hi[m, source], block) + dot_tn(cg_lo[m, source], block)
 
     def far_step(m):
-        received(1, m, yrecv)
+        received(1, m, yrecv, away)
 
         @pl.loop(0, WIDTH // 512)
         def _(j):
@@ -665,6 +667,7 @@
             far_send[0, m, :, cols] = weighed(m, away, cols).astype(BF)
 
         far_copy(1, m).start()
+        received(1, m, yrecv, x)
 
         @pl.loop(0, WIDTH // 512)
         def _(j):
@@ -701,34 +704,37 @@
         wait_for(gpair.at[m, away], gr_sem.at[away, m])
         dy_half(m, away)
 
-    def back_step(m):
-        pl.when(jnp.logical_and(second, m == 0))(need_down)
-        received(2, m, dyrecv)
+    def back_step(source, m):
+        pl.when(jnp.logical_and(second, jnp.logical_and(m == 0, source == away)))(need_down)
+        received(2, m, dyrecv, source)
 
         @pl.loop(0, HIDDEN // 256)
         def _(j):
             cols = aligned(j * 256, 256, 128)
-            dhid = dot_nt(flat(dyrecv, m), wd[cols, :])
-            gate = gs[m, :, cols].astype(F32)
-            up = us[m, :, cols].astype(F32)
+            shape = (PLANE, SLOTS, 256)
+            dhid = dot_nt(dyrecv[m, :, source].reshape(PLANE * SLOTS, WIDTH), wd[cols, :])
+            gate = gs[m, :, source, :, cols].reshape(PLANE * SLOTS, 256).astype(F32)
+            up = us[m, :, source, :, cols].reshape(PLANE * SLOTS, 256).astype(F32)
             square = gate * gate
             bend = jnp.tanh(GELU_C * (gate + GELU_A * square * gate))
             half = 0.5 * (1.0 + bend)
             slope = half + 0.5 * gate * (1.0 - bend * bend) * (
                 GELU_C * (1.0 + 3.0 * GELU_A * square)
             )
-            gs[m, :, cols] = (dhid * up * slope).astype(BF)
-            us[m, :, cols] = (dhid * (gate * half)).astype(BF)
-
-        sent(2, m, bsend)
+            gs[m, :, source, :, cols] = (dhid * up * slope).astype(BF).reshape(shape)
+            us[m, :, source, :, cols] = (dhid * (gate * half)).astype(BF).reshape(shape)
+
+        sent(2, m, bsend, source)
 
         @pl.loop(0, WIDTH // 512)
         def _(j):
             cols = aligned(j * 512, 512, 128)
-            block = dot_nt(gs[m], wg[cols, :]) + dot_nt(us[m], wu[cols, :])
-            bsend[m, :, :, :, cols] = block.astype(BF).reshape(PLANE, 2, SLOTS, 512)
-
-        exchange(3, m, bsend, dn2recv)
+            dgate = gs[m, :, source].reshape(PLANE * SLOTS, HIDDEN)
+            dup = us[m, :, source].reshape(PLANE * SLOTS, HIDDEN)
+            block = dot_nt(dgate, wg[cols, :]) + dot_nt(dup, wu[cols, :])
+            bsend[m, :, source, :, cols] = block.astype(BF).reshape(PLANE, SLOTS, 512)
+
+        exchange_half(3, m, bsend, dn2recv, source)
 
     def gathered(m, source, cols):
         return dot_tn(
@@ -736,11 +742,7 @@
         )
 
     def far_back_step(m):
-        received(3, m, dn2recv)
-
-        @pl.when(jnp.logical_and(first, m == 1))
-        def _():
-            pl.semaphore_signal(go_sem, inc=1, device_id={"section": 1}, device_id_type=MESH)
+        received(3, m, dn2recv, away)
 
 
         @pl.loop(0, WIDTH // 512)
@@ -749,6 +751,11 @@
             far_send[1, m, :, cols] = gathered(m, away, cols).astype(BF)
 
         far_copy(2, m).start()
+        received(3, m, dn2recv, x)
+
+        @pl.when(jnp.logical_and(first, m == 1))
+        def _():
+            pl.semaphore_signal(go_sem, inc=1, device_id={"section": 1}, device_id_type=MESH)
 
         @pl.loop(0, WIDTH // 512)
         def _(j):
@@ -848,6 +855,9 @@
                 grad_copy(m, cross).start()
 
         out_copy(7, ingrad_s.at[m], ingrad_out.at[m], m).start()
+        out_copy(8, n1p.at[m], n1_out.at[m], m).start()
+        out_copy(9, dqkv_all.at[m], dqkv_out.at[m], m).start()
+        out_copy(10, att.at[m], att_out.at[m], m).start()
 
     half_rows = HALF
     quarter_rows = HIDDEN // 2
@@ -882,7 +892,7 @@
         cols = aligned(m * quarter_rows, quarter_rows, 128)
         at = pl.ds(j * 512, 512)
         rows = dyrecv[:, :, :, :, at].reshape(MB * ROWS, 512)
-        wd[cols, at] = dot_tn(hid[:, :, cols].reshape(MB * ROWS, quarter_rows), rows).astype(BF)
+        wd[cols, at] = dot_tn(hid[:, :, :, :, cols].reshape(MB * ROWS, quarter_rows), rows).astype(BF)
         if j == 2:
             start_out(2, m)
 
@@ -905,7 +915,8 @@
         JOIN: join_step,
         GRAD: grad_step,
         GRAD_TWIN: grad_twin_step,
-        BACK: back_step,
+        BACK_NEAR: functools.partial(back_step, x),
+        BACK_FAR: functools.partial(back_step, away),
         FAR_BACK: far_back_step,
         MID: mid_step,
         ATTEND_BACK: attend_back_step,
@@ -943,11 +954,9 @@
 
     @pl.loop(0, MB)
     def _(m):
-        out_copy(8, n1p.at[m], n1_out.at[m], m).start()
-        out_copy(9, dqkv_all.at[m], dqkv_out.at[m], m).start()
-        out_copy(10, att.at[m], att_out.at[m], m).start()
-        sent(1, m, dsend)
-        sent(3, m, bsend)
+        for source in range(2):
+            sent(1, m, dsend, source)
+            sent(3, m, bsend, source)
         to_partner(0, m, part_send.at[m], part_recv.at[m]).wait_send()
         da_copy(m).wait_send()
         dn1_copy(m).wait_send()
@@ -1044,9 +1053,9 @@
             pltpu.VMEM(blocks, BF),
             pltpu.VMEM(blocks, BF),
             pltpu.VMEM(blocks, BF),
-            pltpu.VMEM((MB, ROWS, HIDDEN), BF),
-            pltpu.VMEM((MB, ROWS, HIDDEN), BF),
-            pltpu.VMEM((MB, ROWS, HIDDEN), BF),
+            pltpu.VMEM(blocks[:-1] + (HIDDEN,), BF),
+            pltpu.VMEM(blocks[:-1] + (HIDDEN,), BF),
+            pltpu.VMEM(blocks[:-1] + (HIDDEN,), BF),
             pltpu.VMEM((2, MB, SEQ, WIDTH), BF),
             pltpu.VMEM((2, MB, SEQ, WIDTH), BF),
             pltpu.VMEM((MB, SEQ, WIDTH), BF),
@@ -1066,8 +1075,8 @@
             dma((12,)),
             dma((12,)),
             dma((10,)),
-            dma((4, MB)),
-            dma((4, MB)),
+            dma((4, MB, 2)),
+            dma((4, MB, 2)),
             dma((6, MB)),
             dma((6, MB)),
             dma((3, MB)),

time: 392 us -> 380 us (0.969)
  Pallas kernels: 391 us -> 378 us
    pallas_call x1, Pallas kernels: 308 us -> 295 us  [run_sections(): pl.pallas_call(section_kernel, name='sections', out_shape=(out(MB, SEQ, W...]
where the time goes in v7:
time: 380 us; the launch traced here: 379 us
  Pallas kernels  378 us (99%)
    pallas_call x1, Pallas kernels, run_sections(): pl.pallas_call(section_kernel, name='sections', out_shape=(out(MB, SEQ, W...  295 us
    pallas_call x1, Pallas kernels, reduce_grads(): pl.pallas_call(grads_kernel, name='grads', out_shape=(out(HALF, WIDTH), o...  70.7 us
    pallas_call x1, Pallas kernels, finish(): pl.pallas_call(finish_kernel, name='finish', grid=(steps,), out_shape=[ja...  12.2 us

profile of v7, /device:TPU:0, one launch (start us, length us, event | category | flops | bytes accessed | tf_op | source)
XLA Modules:
  0.0 378.9 jit_solution(6718503411670634244)
XLA Ops:
  0.6 295.2 %sections.1 = (bf16[2,96,1536]{2,1,0:T(8,128)(2,1)}, bf16[2,96,1536]{2,1,0:T(8,128)(2,1)}, f32[8,1536]{1,0:T(8,128)}, bf16[768,768]{1,0:T(8,128)(2,1)}, bf16[768...) custom-call(bf16[2,96,1536]{2,1,0:T(8,128)(2,1)} %x_in.1, ...), custom_call_target="tpu_custom_call" | custom-call | tf_op jit(solution)/shard_map/sections/pallas_call | solution.py:1007
  295.9 70.7 %grads.1 = (bf16[768,1536]{1,0:T(8,128)(2,1)}, bf16[768,256]{1,0:T(8,128)(2,1)}, bf16[768,256]{1,0:T(8,128)(2,1)}, bf16[768,1536]{1,0:T(8,128)(2,1)}, bf16[768,7...) custom-call(bf16[768,768]{1,0:T(8,128)(2,1)} %get-tuple-element.43.their_gate, ...), custom_call_target="tpu_custom_call" | custom-call | tf_op jit(solution)/shard_map/grads/pallas_call | solution.py:1452
  366.6 12.2 %finish.1 = (f32[768,1536]{1,0:T(8,128)}, f32[768,256]{1,0:T(8,128)}, f32[768,256]{1,0:T(8,128)}, f32[768,1536]{1,0:T(8,128)}, f32[768,768]{1,0:T(8,128)}, /*ind...) custom-call(bf16[768,1536]{1,0:T(8,128)(2,1)} %get-tuple-element.51., ...), custom_call_target="tpu_custom_call" | custom-call | tf_op jit(solution)/shard_map/finish/pallas_call | solution.py:1520

commit v8 on v7

--- a/solution.py
+++ b/solution.py
@@ -94,12 +94,12 @@
 FIRST_PLAN = (
     (ENTER, 0, 0),
     (ENTER, 1, 1),
-    (PROJECT, 0, 1),
+    (PROJECT, 0, 0),
     (PROJECT, 1, 1),
     (ATTEND, 0, 1),
-    (ATTEND, 1, 1),
+    (ATTEND, 1, 0),
     (NORM, 0, 1),
-    (NORM, 1, 6),
+    (NORM, 1, 8),
     (TWIN, 0, 0),
     (TWIN, 1, 0),
     (HIDE, 0, 0),

time: 380 us -> 379 us (level)
  no operation moved by 1% of the time
where the time goes in v8:
time: 379 us; the launch traced here: 378 us
  Pallas kernels  378 us (100%)
    pallas_call x1, Pallas kernels, run_sections(): pl.pallas_call(section_kernel, name='sections', out_shape=(out(MB, SEQ, W...  295 us
    pallas_call x1, Pallas kernels, reduce_grads(): pl.pallas_call(grads_kernel, name='grads', out_shape=(out(HALF, WIDTH), o...  70.9 us
    pallas_call x1, Pallas kernels, finish(): pl.pallas_call(finish_kernel, name='finish', grid=(steps,), out_shape=[ja...  12.2 us

profile of v8, /device:TPU:0, one launch (start us, length us, event | category | flops | bytes accessed | tf_op | source)
XLA Modules:
  0.0 378.4 jit_solution(1915040833198293908)
XLA Ops:
  0.6 294.5 %sections.1 = (bf16[2,96,1536]{2,1,0:T(8,128)(2,1)}, bf16[2,96,1536]{2,1,0:T(8,128)(2,1)}, f32[8,1536]{1,0:T(8,128)}, bf16[768,768]{1,0:T(8,128)(2,1)}, bf16[768...) custom-call(bf16[2,96,1536]{2,1,0:T(8,128)(2,1)} %x_in.1, ...), custom_call_target="tpu_custom_call" | custom-call | tf_op jit(solution)/shard_map/sections/pallas_call | solution.py:1007
  295.2 70.9 %grads.1 = (bf16[768,1536]{1,0:T(8,128)(2,1)}, bf16[768,256]{1,0:T(8,128)(2,1)}, bf16[768,256]{1,0:T(8,128)(2,1)}, bf16[768,1536]{1,0:T(8,128)(2,1)}, bf16[768,7...) custom-call(bf16[768,768]{1,0:T(8,128)(2,1)} %get-tuple-element.43.their_gate, ...), custom_call_target="tpu_custom_call" | custom-call | tf_op jit(solution)/shard_map/grads/pallas_call | solution.py:1452
  366.1 12.2 %finish.1 = (f32[768,1536]{1,0:T(8,128)}, f32[768,256]{1,0:T(8,128)}, f32[768,256]{1,0:T(8,128)}, f32[768,1536]{1,0:T(8,128)}, f32[768,768]{1,0:T(8,128)}, /*ind...) custom-call(bf16[768,1536]{1,0:T(8,128)(2,1)} %get-tuple-element.51., ...), custom_call_target="tpu_custom_call" | custom-call | tf_op jit(solution)/shard_map/finish/pallas_call | solution.py:1520

commit v9 on v8

--- a/solution.py
+++ b/solution.py
@@ -93,13 +93,13 @@
 
 FIRST_PLAN = (
     (ENTER, 0, 0),
-    (ENTER, 1, 1),
+    (ENTER, 1, 0),
     (PROJECT, 0, 0),
     (PROJECT, 1, 1),
     (ATTEND, 0, 1),
     (ATTEND, 1, 0),
     (NORM, 0, 1),
-    (NORM, 1, 8),
+    (NORM, 1, 7),
     (TWIN, 0, 0),
     (TWIN, 1, 0),
     (HIDE, 0, 0),
@@ -393,6 +393,11 @@
     side_copy.start()
     meta_copy.start()
 
+    @pl.when(first)
+    def _():
+        for copy in w_pieces[:2]:
+            copy.start()
+
     meta_copy.wait_recv()
     earlier = jnp.where(row < col, 1.0, 0.0).astype(BF)
 
@@ -935,8 +940,7 @@
         m = lax.rem(code, MB)
         for step, work in steps.items():
             pl.when(code // MB == step)(functools.partial(work, m))
-        for mine, plan in zip((first, second), plans):
-            start = 0
+        for mine, plan, start in ((first, plans[0], 2), (second, plans[1], 0)):
             for at, (_, _, count) in enumerate(plan):
                 if count:
                     part = w_pieces[start : start + count]

time: 379 us -> 375 us (0.989)
  Pallas kernels: 378 us -> 374 us
where the time goes in v9:
time: 375 us
  Pallas kernels  374 us (100%)
    pallas_call x1, Pallas kernels, run_sections(): pl.pallas_call(section_kernel, name='sections', out_shape=(out(MB, SEQ, W...  291 us
    pallas_call x1, Pallas kernels, reduce_grads(): pl.pallas_call(grads_kernel, name='grads', out_shape=(out(HALF, WIDTH), o...  70.4 us
    pallas_call x1, Pallas kernels, finish(): pl.pallas_call(finish_kernel, name='finish', grid=(steps,), out_shape=[ja...  12.2 us

profile of v9, /device:TPU:0, one launch (start us, length us, event | category | flops | bytes accessed | tf_op | source)
XLA Modules:
  0.0 374.7 jit_solution(11391461634664511152)
XLA Ops:
  0.6 291.3 %sections.1 = (bf16[2,96,1536]{2,1,0:T(8,128)(2,1)}, bf16[2,96,1536]{2,1,0:T(8,128)(2,1)}, f32[8,1536]{1,0:T(8,128)}, bf16[768,768]{1,0:T(8,128)(2,1)}, bf16[768...) custom-call(bf16[2,96,1536]{2,1,0:T(8,128)(2,1)} %x_in.1, ...), custom_call_target="tpu_custom_call" | custom-call | tf_op jit(solution)/shard_map/sections/pallas_call | solution.py:1011
  292.0 70.4 %grads.1 = (bf16[768,1536]{1,0:T(8,128)(2,1)}, bf16[768,256]{1,0:T(8,128)(2,1)}, bf16[768,256]{1,0:T(8,128)(2,1)}, bf16[768,1536]{1,0:T(8,128)(2,1)}, bf16[768,7...) custom-call(bf16[768,768]{1,0:T(8,128)(2,1)} %get-tuple-element.43.their_gate, ...), custom_call_target="tpu_custom_call" | custom-call | tf_op jit(solution)/shard_map/grads/pallas_call | solution.py:1456
  362.3 12.2 %finish.1 = (f32[768,1536]{1,0:T(8,128)}, f32[768,256]{1,0:T(8,128)}, f32[768,256]{1,0:T(8,128)}, f32[768,1536]{1,0:T(8,128)}, f32[768,768]{1,0:T(8,128)}, /*ind...) custom-call(bf16[768,1536]{1,0:T(8,128)(2,1)} %get-tuple-element.51., ...), custom_call_target="tpu_custom_call" | custom-call | tf_op jit(solution)/shard_map/finish/pallas_call | solution.py:1524
